TPU v7x, 32 devices: a whole 2x2x4 slice. The times are simulated.
32 devices in a mesh: groups: 2 (over y), ctx: 8 (over z, x), tp: 2 (over core).
Axes of the slice: x: 2, y: 2, z: 4, core: 2. Of those that a mesh axis runs over, the one named last changes fastest.
Arguments:
- queries: bfloat16 [2048, 4096], P(('groups', 'ctx'), 'tp'), parts along dimension 0, may hold values from -6 to 6
- keys: bfloat16 [2048, 4096], P(('groups', 'ctx'), 'tp'), parts along dimension 0, may hold values from -6 to 6
- values: bfloat16 [2048, 4096], P(('groups', 'ctx'), 'tp'), parts along dimension 0, may hold values from -30 to 30
- grad_y: bfloat16 [2048, 4096], P(('groups', 'ctx'), 'tp'), parts along dimension 0, may hold values from -6 to 6
- state_low: bfloat16 [16, 32, 128, 128], P(('groups', 'ctx'), 'tp'), parts along dimension 0, may hold values from -48 to 48
- gain: float32 [4096], P('tp'), may hold values from 0.5 to 2
Outputs:
- grad_query: bfloat16 [2048, 4096], P(('groups', 'ctx'), 'tp'), parts along dimension 0
- grad_key: bfloat16 [2048, 4096], P(('groups', 'ctx'), 'tp'), parts along dimension 0
- grad_value: bfloat16 [2048, 4096], P(('groups', 'ctx'), 'tp'), parts along dimension 0
There are 2 independent parts, one for each index of `groups`. A program takes and returns all parts, laid end to end along the dimension named above; an argument that names none is the same for every part. Nothing has to cross between parts.
All inputs are finite; a program needn't handle non-finite values.
Results may differ from a plain program's by a relative error of at most 0.0058.
Values sent between devices are 32-bit elements; how exact they have to be, the bound alone decides.
No kernel may reach another device: no remote copies, remote signals or barrier semaphores. Data moves between devices by JAX's collectives and lax.ppermute only.
A program may use at most 64 MiB of HBM per device.

v0:
```python
import jax
import jax.numpy as jnp
from jax import lax
from jax.sharding import PartitionSpec as P

HEADS = 32
HEAD = 128


def from_behind(value, axis, steps):
    count = lax.axis_size(axis)
    initial, last = (max(0, -steps), min(count, count - steps))
    return lax.ppermute(value, axis, [(source, source + steps) for source in range(initial, last)])


def per_device(queries, keys, values, grad_y, state_low, gain):
    row_count = queries.shape[0]
    local_heads = queries.shape[1] // HEAD
    block_shape = (row_count, local_heads, HEAD)
    query_rows = queries.reshape(block_shape)
    key_rows = keys.reshape(block_shape)
    value_rows = values.reshape(block_shape)
    grad_rows = grad_y.reshape(block_shape)
    gain_rows = gain.reshape(local_heads, HEAD)
    saved_state = state_low[0]
    lower_mask = lax.broadcasted_iota(jnp.int32, (row_count, row_count), 0) >= lax.broadcasted_iota(
        jnp.int32, (row_count, row_count), 1
    )
    features = HEADS * HEAD
    scores = jnp.einsum("tha,sha->hts", query_rows, key_rows, preferred_element_type=jnp.float32)
    probs = jnp.where(lower_mask, scores, 0.0).astype(jnp.bfloat16)
    attn_out = jnp.einsum("hts,shb->thb", probs, value_rows, preferred_element_type=jnp.float32)
    attn_out = attn_out + jnp.einsum(
        "tha,hab->thb", query_rows, saved_state, preferred_element_type=jnp.float32
    )
    weighted = gain_rows * grad_rows.astype(jnp.float32)
    square_sum = lax.psum(jnp.sum(attn_out * attn_out, axis=(1, 2)), "tp")
    inv_rms = lax.rsqrt(square_sum / features + 1e-06)
    normed = attn_out * inv_rms[:, None, None]
    cross_normed = lax.psum(jnp.sum(weighted * normed, axis=(1, 2)), "tp")
    grad_out = inv_rms[:, None, None] * (
        weighted - normed * (cross_normed / features)[:, None, None]
    )
    grad_out = grad_out.astype(jnp.bfloat16)
    own_grad = jnp.einsum("tha,thb->hab", query_rows, grad_out, preferred_element_type=jnp.float32)
    level_count = (lax.axis_size("ctx") - 1).bit_length()
    running = own_grad
    for level in range(level_count):
        running = running + from_behind(running, "ctx", -(1 << level))
    later_sum = running - own_grad
    grad_low = later_sum.astype(jnp.bfloat16)
    grad_scores = jnp.einsum(
        "thb,shb->hts", grad_out, value_rows, preferred_element_type=jnp.float32
    )
    grad_probs = jnp.where(lower_mask, grad_scores, 0.0).astype(jnp.bfloat16)
    grad_query = jnp.einsum(
        "hts,sha->tha", grad_probs, key_rows, preferred_element_type=jnp.float32
    )
    grad_query = grad_query + jnp.einsum(
        "thb,hab->tha", grad_out, saved_state, preferred_element_type=jnp.float32
    )
    grad_key = jnp.einsum(
        "hts,tha->sha", grad_probs, query_rows, preferred_element_type=jnp.float32
    )
    grad_key = grad_key + jnp.einsum(
        "shb,hab->sha", value_rows, grad_low, preferred_element_type=jnp.float32
    )
    grad_value = jnp.einsum("hts,thb->shb", probs, grad_out, preferred_element_type=jnp.float32)
    grad_value = grad_value + jnp.einsum(
        "sha,hab->shb", key_rows, grad_low, preferred_element_type=jnp.float32
    )
    flat = (row_count, local_heads * HEAD)
    return (
        grad_query.astype(jnp.bfloat16).reshape(flat),
        grad_key.astype(jnp.bfloat16).reshape(flat),
        grad_value.astype(jnp.bfloat16).reshape(flat),
    )


def solution(mesh):
    in_specs = (
        P(("groups", "ctx"), "tp"),
        P(("groups", "ctx"), "tp"),
        P(("groups", "ctx"), "tp"),
        P(("groups", "ctx"), "tp"),
        P(("groups", "ctx"), "tp", None, None),
        P("tp"),
    )
    out_specs = (P(("groups", "ctx"), "tp"), P(("groups", "ctx"), "tp"), P(("groups", "ctx"), "tp"))
    return jax.shard_map(
        per_device, mesh=mesh, in_specs=in_specs, out_specs=out_specs, check_vma=False
    )
```

profile of v0, /device:TPU:0, one launch (start us, length us, event | category | flops | bytes accessed | tf_op | source)
XLA Modules:
  0.0 121.3 jit_solution(2577985771558663279)
XLA Ops:
  0.6 0.0 copy-start
  0.7 1.0 copy-done
  1.7 0.0 copy-start.8
  1.7 1.6 %fusion.2 = bf16[16,128,128]{2,1,0:T(8,128)(2,1)S(1)} fusion(pred[128,128]{1,0:T(8,128)(4,1)S(1)} %iota_compare_fusion, bf16[128,2048]{1,0:T(8,128)(2,1)} %param.7, bf16[128,2048]{1,0:T(8,128)(2,1)S(1)} %copy-done), kind=kOutput, calls=%fused_computation.11 | convolution fusion | flops 67633152 | bytes 1589248 | tf_op jit(solution)/shard_map/tha,sha->hts/dot_general | solution.py:30
  3.3 0.0 copy-done.8
  3.3 0.0 copy-start.11
  3.3 0.0 copy-start.4
  3.3 0.5 convolution_bitcast_fusion.4
  3.8 0.3 copy-done.11
  4.1 0.4 copy-done.4
  4.5 0.0 copy-start.14
  4.5 0.5 multiply_reduce_fusion.1
  5.0 2.6 %psum.14 = f32[128]{0:T(128)S(1)} all-reduce(f32[128]{0:T(128)S(1)} %get-tuple-element.6), channel_id=1, replica_groups=mesh['groups'=2,'ctx'=8,'tp'=2] {'tp'}, use_global_device_ids=true, to_apply=%region_1.2 | all-reduce | flops 128 | bytes 1024 | tf_op jit(solution)/shard_map/psum | solution.py:37
  7.6 0.0 copy-done.14
  7.6 0.0 copy-start.15
  7.6 0.2 copy.14
  7.8 0.5 copy-done.15
  8.3 0.3 multiply_reduce_fusion
  8.7 2.5 %psum.15 = f32[128]{0:T(128)S(1)} all-reduce(f32[128]{0:T(128)S(1)} %multiply_reduce_fusion), channel_id=1, replica_groups=mesh['groups'=2,'ctx'=8,'tp'=2] {'tp'}, use_global_device_ids=true, to_apply=%region_3.4 | all-reduce | flops 128 | bytes 1024 | tf_op jit(solution)/shard_map/psum | solution.py:40
  11.1 0.3 multiply_convert_fusion
  11.5 0.3 convolution_bitcast_fusion.2
  11.8 0.0 copy-start.9
  11.8 1.4 %collective-permute-start = (f32[16,128,128]{1,2,0:T(8,128)S(1)}, f32[16,128,128]{1,2,0:T(8,128)S(1)}, u32[]{:S(2)}, u32[]{:S(2)}) collective-permute-start(f32[16,128,128]{1,2,0:T(8,128)S(1)} %convolution_bitcast_fusion.2), channel_id=1, source_target_pairs={{2,0},{4,2},{6,4},{8,6},{10,8},{12,10},{14,12},{3,1},{5,3},{7,5},{... | collective-permute-start | bytes 3145736 | tf_op jit(solution)/shard_map/ppermute | solution.py:13
  13.2 26.9 %collective-permute-done = f32[16,128,128]{1,2,0:T(8,128)S(1)} collective-permute-done((f32[16,128,128]{1,2,0:T(8,128)S(1)}, f32[16,128,128]{1,2,0:T(8,128)S(1)}, u32[]{:S(2)}, u32[]{:S(2)}) %collective-permute-start) | collective-permute-done | bytes 1048608 | tf_op jit(solution)/shard_map/ppermute | solution.py:13
  40.1 0.1 add.37
  40.3 1.3 %collective-permute-start.1 = (f32[16,128,128]{1,2,0:T(8,128)S(1)}, f32[16,128,128]{1,2,0:T(8,128)S(1)}, u32[]{:S(2)}, u32[]{:S(2)}) collective-permute-start(f32[16,128,128]{1,2,0:T(8,128)S(1)} %add.37), channel_id=1, source_target_pairs={{4,0},{6,2},{8,4},{10,6},{12,8},{14,10},{5,1},{7,3},{9,5},{11,7},{... | collective-permute-start | bytes 3145736 | tf_op jit(solution)/shard_map/ppermute | solution.py:13
  41.6 0.0 copy-done.9
  41.6 0.5 fusion.3
  42.1 0.0 copy-start.12
  42.1 0.0 copy-start.6
  42.1 24.8 %collective-permute-done.1 = f32[16,128,128]{1,2,0:T(8,128)S(1)} collective-permute-done((f32[16,128,128]{1,2,0:T(8,128)S(1)}, f32[16,128,128]{1,2,0:T(8,128)S(1)}, u32[]{:S(2)}, u32[]{:S(2)}) %collective-permute-start.1) | collective-permute-done | bytes 1048608 | tf_op jit(solution)/shard_map/ppermute | solution.py:13
  66.9 0.1 add.38
  67.0 0.0 copy-start.1
  67.0 0.0 copy-start.5
  67.1 1.4 %collective-permute-start.2 = (f32[16,128,128]{1,2,0:T(8,128)S(1)}, f32[16,128,128]{1,2,0:T(8,128)}, u32[]{:S(2)}, u32[]{:S(2)}) collective-permute-start(f32[16,128,128]{1,2,0:T(8,128)S(1)} %add.38), channel_id=1, source_target_pairs={{8,0},{10,2},{12,4},{14,6},{9,1},{11,3},{13,5},{15,7},{24,16},{26,... | collective-permute-start | bytes 3145736 | tf_op jit(solution)/shard_map/ppermute | solution.py:13
  68.5 0.0 copy-done.12
  68.5 0.0 copy-done.6
  68.5 0.5 fusion.10
  69.0 0.0 copy-done.1
  69.0 0.0 copy-done.5
  69.0 1.1 fusion.6
  70.1 2.0 %copy.24 = bf16[128,2048]{1,0:T(8,128)(2,1)} copy(bf16[128,2048]{0,1:T(8,128)(2,1)} %bitcast.103) | data formatting | bytes 1048576
  72.2 0.0 copy-start.13
  72.2 1.4 %fusion.30 = f32[16,128,128]{2,1,0:T(8,128)S(1)} fusion(bf16[128,16,128]{0,2,1:T(8,128)(2,1)S(1)} %multiply_convert_fusion, bf16[16,128,128]{2,1,0:T(8,128)(2,1)} %copy-done.11), kind=kOutput, calls=%fused_computation.46 | convolution fusion | flops 67108864 | bytes 2097152 | tf_op jit(solution)/shard_map/hts,thb->shb/dot_general | solution.py:68
  73.6 0.0 copy-done.13
  73.6 0.0 copy-start.2
  73.6 1.3 %convolution_bitcast_fusion = f32[128,16,128]{0,2,1:T(8,128)} fusion(bf16[16,128,128]{2,1,0:T(8,128)(2,1)S(1)} %copy-done.13, bf16[128,2048]{1,0:T(8,128)(2,1)S(1)} %copy-done), kind=kOutput, calls=%fused_computation.2 | convolution fusion | flops 67108864 | bytes 2097152 | tf_op jit(solution)/shard_map/hts,tha->sha/dot_general | solution.py:62
  74.9 0.0 copy-start.7
  74.9 41.5 %collective-permute-done.2 = f32[16,128,128]{1,2,0:T(8,128)} collective-permute-done((f32[16,128,128]{1,2,0:T(8,128)S(1)}, f32[16,128,128]{1,2,0:T(8,128)}, u32[]{:S(2)}, u32[]{:S(2)}) %collective-permute-start.2) | collective-permute-done | bytes 1048608 | tf_op jit(solution)/shard_map/ppermute | solution.py:13
  116.4 0.0 copy-done.2
  116.4 1.4 %subtract_convert_fusion = bf16[16,128,128]{1,2,0:T(8,128)(2,1)S(1)} fusion(f32[16,128,128]{1,2,0:T(8,128)S(1)} %convolution_bitcast_fusion.2, f32[16,128,128]{1,2,0:T(8,128)S(1)} %copy-done.2, f32[16,128,128]{1,2,0:T(8,128)} %collective-permute-done.2), kind=kLoop, calls=%fused_computation.16 | loop fusion | flops 786432 | bytes 3670016 | tf_op jit(solution)/shard_map/convert_element_type | solution.py:51
  117.8 0.0 copy-done.7
  117.8 0.0 copy-start.10
  117.9 0.5 fusion.5
  118.4 0.0 copy-start.3
  118.4 1.0 copy.26
  119.4 0.0 copy-done.10
  119.4 0.4 copy-done.3
  119.8 0.5 fusion.4
  120.3 1.0 copy.25
  (3 shorter events, 0.0 us)
Async XLA Ops:
  0.6 1.0 copy-start
  1.7 1.6 %copy-start.8 = (bf16[128,2048]{1,0:T(8,128)(2,1)S(1)}, bf16[128,2048]{1,0:T(8,128)(2,1)}, u32[]{:S(2)}) copy-start(bf16[128,2048]{1,0:T(8,128)(2,1)} %param.8) | copy-start | bytes 1572868
  3.3 0.8 copy-start.11
  3.3 1.2 %copy-start.4 = (bf16[1,16,128,128]{3,2,1,0:T(8,128)(2,1)S(1)}, bf16[1,16,128,128]{3,2,1,0:T(8,128)(2,1)}, u32[]{:S(2)}) copy-start(bf16[1,16,128,128]{3,2,1,0:T(8,128)(2,1)} %param.10) | copy-start | bytes 1572868
  4.5 3.1 %copy-start.14 = (bf16[128,2048]{1,0:T(8,128)(2,1)S(1)}, bf16[128,2048]{1,0:T(8,128)(2,1)}, u32[]{:S(2)}) copy-start(bf16[128,2048]{1,0:T(8,128)(2,1)} %param.9) | copy-start | bytes 1572868
  7.6 0.7 copy-start.15
  11.8 29.8 %copy-start.9 = (bf16[128,2048]{1,0:T(8,128)(2,1)S(1)}, bf16[128,2048]{1,0:T(8,128)(2,1)}, u32[]{:S(2)}) copy-start(bf16[128,2048]{1,0:T(8,128)(2,1)} %param.8) | copy-start | bytes 1572868
  11.8 28.3 %collective-permute-start = (f32[16,128,128]{1,2,0:T(8,128)S(1)}, f32[16,128,128]{1,2,0:T(8,128)S(1)}, u32[]{:S(2)}, u32[]{:S(2)}) collective-permute-start(f32[16,128,128]{1,2,0:T(8,128)S(1)} %convolution_bitcast_fusion.2), channel_id=1, source_target_pairs={{2,0},{4,2},{6,4},{8,6},{10,8},{12,10},{14,12},{3,1},{5,3},{7,5},{... | collective-permute-start | bytes 3145736 | tf_op jit(solution)/shard_map/ppermute | solution.py:13
  40.3 26.6 %collective-permute-start.1 = (f32[16,128,128]{1,2,0:T(8,128)S(1)}, f32[16,128,128]{1,2,0:T(8,128)S(1)}, u32[]{:S(2)}, u32[]{:S(2)}) collective-permute-start(f32[16,128,128]{1,2,0:T(8,128)S(1)} %add.37), channel_id=1, source_target_pairs={{4,0},{6,2},{8,4},{10,6},{12,8},{14,10},{5,1},{7,3},{9,5},{11,7},{... | collective-permute-start | bytes 3145736 | tf_op jit(solution)/shard_map/ppermute | solution.py:13
  42.1 26.4 %copy-start.12 = (bf16[16,128,128]{2,1,0:T(8,128)(2,1)}, bf16[16,128,128]{2,1,0:T(8,128)(2,1)S(1)}, u32[]{:S(2)}) copy-start(bf16[16,128,128]{2,1,0:T(8,128)(2,1)S(1)} %fusion.3) | copy-start | bytes 1572868
  42.1 26.4 %copy-start.6 = (bf16[128,2048]{1,0:T(8,128)(2,1)S(1)}, bf16[128,2048]{1,0:T(8,128)(2,1)}, u32[]{:S(2)}) copy-start(bf16[128,2048]{1,0:T(8,128)(2,1)} %param.7) | copy-start | bytes 1572868
  67.0 2.0 %copy-start.1 = (f32[16,128,128]{1,2,0:T(8,128)}, f32[16,128,128]{1,2,0:T(8,128)S(1)}, u32[]{:S(2)}) copy-start(f32[16,128,128]{1,2,0:T(8,128)S(1)} %add.38) | copy-start | bytes 3145732
  67.0 2.0 %copy-start.5 = (bf16[1,16,128,128]{3,2,1,0:T(8,128)(2,1)S(1)}, bf16[1,16,128,128]{3,2,1,0:T(8,128)(2,1)}, u32[]{:S(2)}) copy-start(bf16[1,16,128,128]{3,2,1,0:T(8,128)(2,1)} %param.10) | copy-start | bytes 1572868
  67.1 49.3 %collective-permute-start.2 = (f32[16,128,128]{1,2,0:T(8,128)S(1)}, f32[16,128,128]{1,2,0:T(8,128)}, u32[]{:S(2)}, u32[]{:S(2)}) collective-permute-start(f32[16,128,128]{1,2,0:T(8,128)S(1)} %add.38), channel_id=1, source_target_pairs={{8,0},{10,2},{12,4},{14,6},{9,1},{11,3},{13,5},{15,7},{24,16},{26,... | collective-permute-start | bytes 3145736 | tf_op jit(solution)/shard_map/ppermute | solution.py:13
  72.2 1.4 %copy-start.13 = (bf16[16,128,128]{2,1,0:T(8,128)(2,1)S(1)}, bf16[16,128,128]{2,1,0:T(8,128)(2,1)}, u32[]{:S(2)}) copy-start(bf16[16,128,128]{2,1,0:T(8,128)(2,1)} %copy-done.12) | copy-start | bytes 1572868
  73.6 42.8 %copy-start.2 = (f32[16,128,128]{1,2,0:T(8,128)S(1)}, f32[16,128,128]{1,2,0:T(8,128)}, u32[]{:S(2)}) copy-start(f32[16,128,128]{1,2,0:T(8,128)} %copy-done.1) | copy-start | bytes 3145732
  74.9 42.9 %copy-start.7 = (bf16[128,2048]{1,0:T(8,128)(2,1)S(1)}, bf16[128,2048]{1,0:T(8,128)(2,1)}, u32[]{:S(2)}) copy-start(bf16[128,2048]{1,0:T(8,128)(2,1)} %param.7) | copy-start | bytes 1572868
  117.8 1.5 %copy-start.10 = (bf16[128,2048]{1,0:T(8,128)(2,1)S(1)}, bf16[128,2048]{1,0:T(8,128)(2,1)}, u32[]{:S(2)}) copy-start(bf16[128,2048]{1,0:T(8,128)(2,1)} %param.8) | copy-start | bytes 1572868
  118.4 1.5 %copy-start.3 = (f32[128,16,128]{0,2,1:T(8,128)S(1)}, f32[128,16,128]{0,2,1:T(8,128)}, u32[]{:S(2)}) copy-start(f32[128,16,128]{0,2,1:T(8,128)} %convolution_bitcast_fusion) | copy-start | bytes 3145732
where the time goes:
time: 122 us; the launch traced here: 121 us
  waiting for transfers between devices  93.2 us (76%)
  matrix products  8.72 us (7%)
  local copies, waits for them, and re-layouts  6.97 us (6%)
  blocking collectives  5.05 us (4%)
  starting transfers between devices  4.14 us (3%)
  other arithmetic  2.42 us (2%)
    ppermute x3, waiting for transfers between devices, from_behind(): lax.ppermute(value, axis, [(source, source + steps) for source in range(i...  93.2 us
    unnamed x35, local copies, waits for them, and re-layouts  6.77 us
    ppermute x3, starting transfers between devices, from_behind(): lax.ppermute(value, axis, [(source, source + steps) for source in range(i...  4.14 us
    psum x1, blocking collectives, per_device(): square_sum = lax.psum(jnp.sum(attn_out * attn_out, axis=(1, 2)), 'tp')  2.58 us
    psum x1, blocking collectives, per_device(): cross_normed = lax.psum(jnp.sum(weighted * normed, axis=(1, 2)), 'tp')  2.47 us
  transfers between devices with their start and end apart: 3, of which 3 were waited for; matrix products, arithmetic and copies ran while one was open for 6% of the time, Pallas kernels for 0%

commit v1 on v0

v1 whole, which is shorter than its diff:
```python
import functools

import jax
import jax.numpy as jnp
from jax import lax
from jax.experimental import pallas as pl
from jax.experimental.pallas import tpu as pltpu
from jax.sharding import PartitionSpec as P

HEAD = 128
QUAD = 4
CHUNKS = 1
VMEM = pl.BlockSpec(memory_space=pltpu.VMEM)
NN = (((1,), (0,)), ((), ()))
NT = (((1,), (1,)), ((), ()))
TN = (((0,), (0,)), ((), ()))


def dot(left, right, dims):
    return lax.dot_general(left, right, dims, preferred_element_type=jnp.float32)


def columns(head):
    if isinstance(head, int):
        return pl.ds(head * HEAD, HEAD)
    return pl.ds(pl.multiple_of(head * HEAD, HEAD), HEAD)


def lower(rows):
    row = lax.broadcasted_iota(jnp.int32, (rows, rows), 0)
    return row >= lax.broadcasted_iota(jnp.int32, (rows, rows), 1)


def forward_kernel(q_ref, k_ref, v_ref, s_ref, y_ref, gain_ref, out_ref, probs_ref, stat_ref):
    rows = q_ref.shape[0]
    mask = lower(rows)
    squares = jnp.zeros((rows, HEAD), jnp.float32)
    crosses = jnp.zeros((rows, HEAD), jnp.float32)
    for head in range(q_ref.shape[1] // HEAD):
        at = columns(head)
        q = q_ref[:, at]
        probs = jnp.where(mask, dot(q, k_ref[:, at], NT), 0.0).astype(jnp.bfloat16)
        probs_ref[:, at] = probs
        out = dot(probs, v_ref[:, at], NN) + dot(q, s_ref[head], NN)
        out_ref[:, at] = out
        squares += out * out
        crosses += gain_ref[:, at] * y_ref[:, at].astype(jnp.float32) * out
    lane = lax.broadcasted_iota(jnp.int32, (rows, HEAD), 1)
    square = jnp.sum(squares, axis=1, keepdims=True)
    cross = jnp.sum(crosses, axis=1, keepdims=True)
    stat_ref[...] = jnp.where(lane == 0, square, cross)


def state_kernel(
    features, chunks, where_ref, own_ref, other_ref, out_ref, y_ref, gain_ref, q_ref, g_ref, *u_refs
):
    stat = own_ref[...] + other_ref[...]
    square, cross = stat[:, 0:1], stat[:, 1:2]
    inverse = lax.rsqrt(square / features + 1e-06)
    back = cross * (inverse * inverse * inverse) / features
    me = where_ref[0]
    heads = q_ref.shape[1] // HEAD
    share = heads // (QUAD * chunks)
    for chunk in range(chunks):
        for step in (3, 1, 2, 0):
            u_ref = u_refs[chunk * QUAD + step]
            for local in range(share):
                at = columns((chunk * QUAD + (me ^ step)) * share + local)
                weighted = gain_ref[:, at] * y_ref[:, at].astype(jnp.float32)
                grad = (inverse * weighted - out_ref[:, at] * back).astype(jnp.bfloat16)
                g_ref[:, at] = grad
                u_ref[local] = dot(q_ref[:, at], grad, TN)


def local_kernel(
    q_ref, k_ref, v_ref, s_ref, g_ref, probs_ref, query_ref, key_ref, value_ref
):
    mask = lower(q_ref.shape[0])
    for head in range(q_ref.shape[1] // HEAD):
        at = columns(head)
        g = g_ref[:, at]
        grads = jnp.where(mask, dot(g, v_ref[:, at], NT), 0.0).astype(jnp.bfloat16)
        query = dot(grads, k_ref[:, at], NN) + dot(g, s_ref[head], NT)
        query_ref[:, at] = query.astype(jnp.bfloat16)
        key_ref[:, at] = dot(grads, q_ref[:, at], TN)
        value_ref[:, at] = dot(probs_ref[:, at], g, TN)


def final_kernel(chunks, where_ref, k_ref, v_ref, key_in, value_in, *refs):
    later_refs, (key_ref, value_ref) = refs[:-2], refs[-2:]
    me = where_ref[0]
    heads = k_ref.shape[1] // HEAD
    share = heads // (QUAD * chunks)
    for chunk in range(chunks):
        for step in range(QUAD):
            for local in range(share):
                at = columns((chunk * QUAD + (me ^ step)) * share + local)
                later = later_refs[chunk * QUAD + step][local].astype(jnp.bfloat16)
                key = key_in[:, at] + dot(v_ref[:, at], later, NT)
                key_ref[:, at] = key.astype(jnp.bfloat16)
                value = value_in[:, at] + dot(k_ref[:, at], later, NN)
                value_ref[:, at] = value.astype(jnp.bfloat16)


def params(mib):
    return pltpu.CompilerParams(vmem_limit_bytes=mib << 20)


def partner(value, axis, mask):
    count = lax.axis_size(axis)
    return lax.ppermute(value, axis, [(source, source ^ mask) for source in range(count)])


def per_device(queries, keys, values, grad_y, state_low, gain):
    rows, width = queries.shape
    heads = width // HEAD
    chunks = CHUNKS
    share = heads // (QUAD * chunks)
    features = width * lax.axis_size("tp")
    state = state_low[0]
    gain_row = gain.reshape(1, width)
    place = lax.axis_index("ctx")
    me = place % QUAD
    where = me.reshape(1).astype(jnp.int32)
    smem = pl.BlockSpec(memory_space=pltpu.SMEM)

    full = jax.ShapeDtypeStruct((rows, width), jnp.float32)
    half = jax.ShapeDtypeStruct((rows, width), jnp.bfloat16)
    piece = jax.ShapeDtypeStruct((share, HEAD, HEAD), jnp.float32)
    out, probs, stat = pl.pallas_call(
        forward_kernel,
        out_shape=(full, half, jax.ShapeDtypeStruct((rows, HEAD), jnp.float32)),
        in_specs=[VMEM] * 6,
        out_specs=(VMEM,) * 3,
        compiler_params=params(20),
    )(queries, keys, values, state, grad_y, gain_row)
    other = partner(stat, "tp", 1)
    grad, *own = pl.pallas_call(
        functools.partial(state_kernel, features, chunks),
        out_shape=(half,) + (piece,) * (QUAD * chunks),
        in_specs=[smem] + [VMEM] * 6,
        out_specs=(VMEM,) * (1 + QUAD * chunks),
        compiler_params=params(20),
    )(where, stat, other, out, grad_y, gain_row, queries)

    held = []
    for chunk in range(chunks):
        mine = own[chunk * QUAD : (chunk + 1) * QUAD]
        held.append([mine[0]] + [partner(mine[step], "ctx", step) for step in (1, 2, 3)])
    later = []
    for chunk in range(chunks):
        total = held[chunk][0] + held[chunk][1] + held[chunk][2] + held[chunk][3]
        behind = jnp.zeros_like(total)
        span = QUAD
        while span < lax.axis_size("ctx"):
            came = partner(total, "ctx", span)
            behind = jnp.where((place & span) == 0, behind + came, behind)
            span *= 2
            if span < lax.axis_size("ctx"):
                total = total + came
        sums = []
        for target in range(QUAD):
            value = behind
            for source in range(QUAD):
                if source != target:
                    value = value + jnp.where((me ^ source) > (me ^ target), held[chunk][source], 0.0)
            sums.append(value)
        later += [sums[0]] + [partner(sums[step], "ctx", step) for step in (1, 2, 3)]

    grad_query, key_part, value_part = pl.pallas_call(
        local_kernel,
        out_shape=(half, full, full),
        in_specs=[VMEM] * 6,
        out_specs=(VMEM,) * 3,
        compiler_params=params(20),
    )(queries, keys, values, state, grad, probs)
    grad_key, grad_value = pl.pallas_call(
        functools.partial(final_kernel, chunks),
        out_shape=(half, half),
        in_specs=[smem] + [VMEM] * (4 + QUAD * chunks),
        out_specs=(VMEM,) * 2,
        compiler_params=params(20),
    )(where, keys, values, key_part, value_part, *later)
    return grad_query, grad_key, grad_value


def solution(mesh):
    rows = P(("groups", "ctx"), "tp")
    return jax.shard_map(
        per_device,
        mesh=mesh,
        in_specs=(rows, rows, rows, rows, P(("groups", "ctx"), "tp", None, None), P("tp")),
        out_specs=(rows, rows, rows),
        check_vma=False,
    )
```

time: 122 us -> 56.5 us (0.46)
  waiting for transfers between devices: 93.2 us -> 31 us
  matrix products: 8.72 us -> 0 us
  starting transfers between devices: 4.14 us -> 11.4 us
  Pallas kernels: 0 us -> 6.76 us
  blocking collectives: 5.05 us -> 0 us
  other arithmetic: 2.42 us -> 0.27 us
    ppermute x3 -> x8, waiting for transfers between devices: 93.2 us -> 31 us  [partner(): lax.ppermute(value, axis, [(source, source ^ mask) for source in range(co...]
    dot_general x11 -> x0, matrix products: 8.72 us -> none  [the longest x1 1.58 us: per_device(): jnp.einsum('tha,sha->hts', query_rows, key_rows, preferred_element_type=j...]
    ppermute x3 -> x8, starting transfers between devices: 4.14 us -> 11.4 us  [partner(): lax.ppermute(value, axis, [(source, source ^ mask) for source in range(co...]
    pallas_call x0 -> x4, Pallas kernels: none -> 6.76 us  [the longest x1 3.38 us: per_device(): pl.pallas_call(local_kernel, out_shape=(half, full, full), in_specs=[VMEM...]
    psum x2 -> x0, blocking collectives: 5.05 us -> none  [the longest x1 2.58 us: per_device(): square_sum = lax.psum(jnp.sum(attn_out * attn_out, axis=(1, 2)), 'tp')]
    convert_element_type x2 -> x0, other arithmetic: 1.79 us -> none  [the longest x1 1.44 us: per_device(): grad_low = later_sum.astype(jnp.bfloat16)]
    unnamed x35 -> x24, local copies, waits for them, and re-layouts: 6.77 us -> 5.92 us
  transfers between devices with their start and end apart: 3 -> 8, of which waited for: 3 -> 8; matrix products, arithmetic and copies ran while one was open for 6% -> 0% of each run, Pallas kernels for 0% -> 6%
where the time goes in v1:
time: 56.5 us; the launch traced here: 56.1 us
  waiting for transfers between devices  31 us (55%)
  starting transfers between devices  11.4 us (20%)
  Pallas kernels  6.76 us (12%)
  local copies, waits for them, and re-layouts  5.92 us (10%)
  between operations  0.67 us (1%)
    ppermute x8, waiting for transfers between devices, partner(): lax.ppermute(value, axis, [(source, source ^ mask) for source in range(co...  31 us
    ppermute x8, starting transfers between devices, partner(): lax.ppermute(value, axis, [(source, source ^ mask) for source in range(co...  11.4 us
    unnamed x24, local copies, waits for them, and re-layouts  5.92 us
    pallas_call x1, Pallas kernels, per_device(): pl.pallas_call(local_kernel, out_shape=(half, full, full), in_specs=[VMEM...  3.38 us
    pallas_call x1, Pallas kernels, per_device(): pl.pallas_call(functools.partial(final_kernel, chunks), out_shape=(half,...  1.63 us
  transfers between devices with their start and end apart: 8, of which 8 were waited for; matrix products, arithmetic and copies ran while one was open for 0% of the time, Pallas kernels for 6%

profile of v1, /device:TPU:0, one launch (start us, length us, event | category | flops | bytes accessed | tf_op | source)
XLA Modules:
  0.0 56.1 jit_solution(16312034925005358808)
XLA Ops:
  0.6 0.0 copy-start
  0.6 1.0 %copy-done = bf16[128,2048]{1,0:T(8,128)(2,1)S(1)} copy-done((bf16[128,2048]{1,0:T(8,128)(2,1)S(1)}, bf16[128,2048]{1,0:T(8,128)(2,1)}, u32[]{:S(2)}) %copy-start) | copy-done | bytes 524312
  1.7 0.0 copy-start.2
  1.7 1.0 %copy-done.2 = bf16[128,2048]{1,0:T(8,128)(2,1)S(1)} copy-done((bf16[128,2048]{1,0:T(8,128)(2,1)S(1)}, bf16[128,2048]{1,0:T(8,128)(2,1)}, u32[]{:S(2)}) %copy-start.2) | copy-done | bytes 524312
  2.7 0.0 copy-start.4
  2.7 1.0 %copy-done.4 = bf16[128,2048]{1,0:T(8,128)(2,1)S(1)} copy-done((bf16[128,2048]{1,0:T(8,128)(2,1)S(1)}, bf16[128,2048]{1,0:T(8,128)(2,1)}, u32[]{:S(2)}) %copy-start.4) | copy-done | bytes 524312
  3.8 0.0 copy-start.6
  3.8 1.0 %copy-done.6 = bf16[128,2048]{1,0:T(8,128)(2,1)S(1)} copy-done((bf16[128,2048]{1,0:T(8,128)(2,1)S(1)}, bf16[128,2048]{1,0:T(8,128)(2,1)}, u32[]{:S(2)}) %copy-start.6) | copy-done | bytes 524312
  4.8 0.0 copy-start.8
  4.8 1.0 %copy-done.8 = bf16[1,16,128,128]{3,2,1,0:T(8,128)(2,1)S(1)} copy-done((bf16[1,16,128,128]{3,2,1,0:T(8,128)(2,1)S(1)}, bf16[1,16,128,128]{3,2,1,0:T(8,128)(2,1)}, u32[]{:S(2)}) %copy-start.8) | copy-done | bytes 524312
  5.8 0.0 copy-start.10
  5.8 0.7 %copy-done.10 = f32[2048]{0:T(1024)S(1)} copy-done((f32[2048]{0:T(1024)S(1)}, f32[2048]{0:T(1024)}, u32[]{:S(2)}) %copy-start.10) | copy-done | bytes 8216
  6.5 0.0 copy-start.1
  6.5 0.0 copy-start.7
  6.5 1.0 %shard_map.85 = (f32[128,2048]{1,0:T(8,128)S(1)}, bf16[128,2048]{1,0:T(8,128)(2,1)S(1)}, f32[128,128]{1,0:T(8,128)S(1)}) custom-call(bf16[128,2048]{1,0:T(8,128)(2,1)S(1)} %copy-done, bf16[128,2048]{1,0:T(8,128)(2,1)S(1)} %copy-done.2, bf16[128,2048]{1,0:T(8,128)(2,1)S(1)} %copy-done.4, bf16[16,128,128]{2,1,0:T(8,128)(2,1)S(1)} %bitcast.3, ...), custom_call_target="tpu_custom_call" | custom-call | tf_op jit(solution)/shard_map/pallas_call | solution.py:130
  7.5 0.5 collective-permute-start
  8.1 0.0 copy-start.11
  8.1 0.9 %collective-permute-done.other_ref = f32[128,128]{1,0:T(8,128)S(1)} collective-permute-done((f32[128,128]{1,0:T(8,128)S(1)}, f32[128,128]{1,0:T(8,128)S(1)}, u32[]{:S(2)}, u32[]{:S(2)}) %collective-permute-start) | collective-permute-done | bytes 65568 | tf_op jit(solution)/shard_map/ppermute | solution.py:111
  9.0 0.0 copy-done.1
  9.0 0.0 copy-done.7
  9.0 0.0 copy-done.11
  9.0 0.8 %shard_map.86 = (bf16[128,2048]{1,0:T(8,128)(2,1)S(1)}, f32[4,128,128]{2,1,0:T(8,128)S(1)}, f32[4,128,128]{2,1,0:T(8,128)S(1)}, f32[4,128,128]{2,1,0:T(8,128)S(1)}, f32[4,128,128]{2,1,0:T(8,128)S(1)}) custom-call(s32[1]{0:T(128)} %bitcast.1.where_ref, f32[128,128]{1,0:T(8,128)S(1)} %get-tuple-element.16.own_ref, ...), custom_call_target="tpu_custom_call" | custom-call | tf_op jit(solution)/shard_map/pallas_call | solution.py:138
  9.7 2.9 %collective-permute-start.1 = (f32[4,128,128]{2,1,0:T(8,128)S(1)}, f32[4,128,128]{2,1,0:T(8,128)S(1)}, u32[]{:S(2)}, u32[]{:S(2)}) collective-permute-start(f32[4,128,128]{2,1,0:T(8,128)S(1)} %get-tuple-element.24), channel_id=1, source_target_pairs={{0,2},{2,0},{4,6},{6,4},{8,10},{10,8},{12,14},{14,12},{1,3},{3,1},... | collective-permute-start | bytes 786440 | tf_op jit(solution)/shard_map/ppermute | solution.py:111
  12.6 1.6 %collective-permute-start.2 = (f32[4,128,128]{2,1,0:T(8,128)S(1)}, f32[4,128,128]{2,1,0:T(8,128)S(1)}, u32[]{:S(2)}, u32[]{:S(2)}) collective-permute-start(f32[4,128,128]{2,1,0:T(8,128)S(1)} %get-tuple-element.25), channel_id=1, source_target_pairs={{0,4},{2,6},{4,0},{6,2},{8,12},{10,14},{12,8},{14,10},{1,5},{3,7},... | collective-permute-start | bytes 786440 | tf_op jit(solution)/shard_map/ppermute | solution.py:111
  14.2 0.0 collective-permute-start.3
  14.2 5.0 %collective-permute-done.1 = f32[4,128,128]{2,1,0:T(8,128)S(1)} collective-permute-done((f32[4,128,128]{2,1,0:T(8,128)S(1)}, f32[4,128,128]{2,1,0:T(8,128)S(1)}, u32[]{:S(2)}, u32[]{:S(2)}) %collective-permute-start.1) | collective-permute-done | bytes 262176 | tf_op jit(solution)/shard_map/ppermute | solution.py:111
  19.3 2.6 %collective-permute-done.2 = f32[4,128,128]{2,1,0:T(8,128)S(1)} collective-permute-done((f32[4,128,128]{2,1,0:T(8,128)S(1)}, f32[4,128,128]{2,1,0:T(8,128)S(1)}, u32[]{:S(2)}, u32[]{:S(2)}) %collective-permute-start.2) | collective-permute-done | bytes 262176 | tf_op jit(solution)/shard_map/ppermute | solution.py:111
  21.8 4.3 %collective-permute-done.3 = f32[4,128,128]{2,1,0:T(8,128)S(1)} collective-permute-done((f32[4,128,128]{2,1,0:T(8,128)S(1)}, f32[4,128,128]{2,1,0:T(8,128)S(1)}, u32[]{:S(2)}, u32[]{:S(2)}) %collective-permute-start.3) | collective-permute-done | bytes 262176 | tf_op jit(solution)/shard_map/ppermute | solution.py:111
  26.1 0.1 add_add_fusion
  26.2 2.8 %collective-permute-start.4 = (f32[4,128,128]{2,1,0:T(8,128)S(1)}, f32[4,128,128]{2,1,0:T(8,128)S(1)}, u32[]{:S(2)}, u32[]{:S(2)}) collective-permute-start(f32[4,128,128]{2,1,0:T(8,128)S(1)} %add_add_fusion), channel_id=1, source_target_pairs={{0,8},{2,10},{4,12},{6,14},{8,0},{10,2},{12,4},{14,6},{1,9},{3,11}... | collective-permute-start | bytes 786440 | tf_op jit(solution)/shard_map/ppermute | solution.py:111
  29.0 0.0 copy-start.3
  29.0 0.0 copy-start.5
  29.0 0.0 copy-start.9
  29.0 11.3 %collective-permute-done.4 = f32[4,128,128]{2,1,0:T(8,128)S(1)} collective-permute-done((f32[4,128,128]{2,1,0:T(8,128)S(1)}, f32[4,128,128]{2,1,0:T(8,128)S(1)}, u32[]{:S(2)}, u32[]{:S(2)}) %collective-permute-start.4) | collective-permute-done | bytes 262176 | tf_op jit(solution)/shard_map/ppermute | solution.py:111
  40.3 0.2 select_add_fusion
  40.5 1.5 %collective-permute-start.7 = (f32[4,128,128]{2,1,0:T(8,128)S(1)}, f32[4,128,128]{2,1,0:T(8,128)S(1)}, u32[]{:S(2)}, u32[]{:S(2)}) collective-permute-start(f32[4,128,128]{2,1,0:T(8,128)S(1)} %get-tuple-element.29), channel_id=1, source_target_pairs={{0,6},{2,4},{4,2},{6,0},{8,14},{10,12},{12,10},{14,8},{1,7},{3,5},... | collective-permute-start | bytes 786440 | tf_op jit(solution)/shard_map/ppermute | solution.py:111
  42.0 1.4 %collective-permute-start.6 = (f32[4,128,128]{2,1,0:T(8,128)S(1)}, f32[4,128,128]{2,1,0:T(8,128)S(1)}, u32[]{:S(2)}, u32[]{:S(2)}) collective-permute-start(f32[4,128,128]{2,1,0:T(8,128)S(1)} %get-tuple-element.30), channel_id=1, source_target_pairs={{0,4},{2,6},{4,0},{6,2},{8,12},{10,14},{12,8},{14,10},{1,5},{3,7},... | collective-permute-start | bytes 786440 | tf_op jit(solution)/shard_map/ppermute | solution.py:111
  43.4 0.7 %collective-permute-start.5 = (f32[4,128,128]{2,1,0:T(8,128)S(1)}, f32[4,128,128]{2,1,0:T(8,128)S(1)}, u32[]{:S(2)}, u32[]{:S(2)}) collective-permute-start(f32[4,128,128]{2,1,0:T(8,128)S(1)} %get-tuple-element.31), channel_id=1, source_target_pairs={{0,2},{2,0},{4,6},{6,4},{8,10},{10,8},{12,14},{14,12},{1,3},{3,1},... | collective-permute-start | bytes 786440 | tf_op jit(solution)/shard_map/ppermute | solution.py:111
  44.1 0.0 copy-done.3
  44.1 0.0 copy-done.5
  44.1 0.0 copy-done.9
  44.1 3.4 %shard_map.87 = (bf16[128,2048]{1,0:T(8,128)(2,1)}, f32[128,2048]{1,0:T(8,128)S(1)}, f32[128,2048]{1,0:T(8,128)S(1)}) custom-call(bf16[128,2048]{1,0:T(8,128)(2,1)S(1)} %copy-done.1, bf16[128,2048]{1,0:T(8,128)(2,1)S(1)} %copy-done.3, bf16[128,2048]{1,0:T(8,128)(2,1)S(1)} %copy-done.5, bf16[16,128,128]{2,1,0:T(8,128)(2,1)S(1)} %bitcast.4, ...), custom_call_target="tpu_custom_call" | custom-call | tf_op jit(solution)/shard_map/pallas_call | solution.py:170
  47.5 3.3 %collective-permute-done.7.refs_3_ = f32[4,128,128]{2,1,0:T(8,128)S(1)} collective-permute-done((f32[4,128,128]{2,1,0:T(8,128)S(1)}, f32[4,128,128]{2,1,0:T(8,128)S(1)}, u32[]{:S(2)}, u32[]{:S(2)}) %collective-permute-start.7) | collective-permute-done | bytes 262176 | tf_op jit(solution)/shard_map/ppermute | solution.py:111
  50.8 3.4 %collective-permute-done.6.refs_2_ = f32[4,128,128]{2,1,0:T(8,128)S(1)} collective-permute-done((f32[4,128,128]{2,1,0:T(8,128)S(1)}, f32[4,128,128]{2,1,0:T(8,128)S(1)}, u32[]{:S(2)}, u32[]{:S(2)}) %collective-permute-start.6) | collective-permute-done | bytes 262176 | tf_op jit(solution)/shard_map/ppermute | solution.py:111
  54.2 0.2 collective-permute-done.5.refs_1_
  54.4 1.6 %shard_map.88 = (bf16[128,2048]{1,0:T(8,128)(2,1)}, bf16[128,2048]{1,0:T(8,128)(2,1)}) custom-call(s32[1]{0:T(128)} %bitcast.1.where_ref, bf16[128,2048]{1,0:T(8,128)(2,1)S(1)} %copy-done.3, bf16[128,2048]{1,0:T(8,128)(2,1)S(1)} %copy-done.5, f32[128,2048]{1,0:T(8,128)S(1)} %get-tuple-element.21.key_in, f32[128,2048]{1,0:T(8,128)S(1)} %get-tuple-element.22.value_in, ...), custom_call_target="tpu_custom_call" | custom-call | tf_op jit(solution)/shard_map/pallas_call | solution.py:177
Async XLA Ops:
  0.6 1.0 %copy-start = (bf16[128,2048]{1,0:T(8,128)(2,1)S(1)}, bf16[128,2048]{1,0:T(8,128)(2,1)}, u32[]{:S(2)}) copy-start(bf16[128,2048]{1,0:T(8,128)(2,1)} %q_ref.5) | copy-start | bytes 1572868
  1.7 1.0 %copy-start.2 = (bf16[128,2048]{1,0:T(8,128)(2,1)S(1)}, bf16[128,2048]{1,0:T(8,128)(2,1)}, u32[]{:S(2)}) copy-start(bf16[128,2048]{1,0:T(8,128)(2,1)} %k_ref.5) | copy-start | bytes 1572868
  2.7 1.0 %copy-start.4 = (bf16[128,2048]{1,0:T(8,128)(2,1)S(1)}, bf16[128,2048]{1,0:T(8,128)(2,1)}, u32[]{:S(2)}) copy-start(bf16[128,2048]{1,0:T(8,128)(2,1)} %v_ref.5) | copy-start | bytes 1572868
  3.8 1.0 %copy-start.6 = (bf16[128,2048]{1,0:T(8,128)(2,1)S(1)}, bf16[128,2048]{1,0:T(8,128)(2,1)}, u32[]{:S(2)}) copy-start(bf16[128,2048]{1,0:T(8,128)(2,1)} %y_ref.3) | copy-start | bytes 1572868
  4.8 1.0 %copy-start.8 = (bf16[1,16,128,128]{3,2,1,0:T(8,128)(2,1)S(1)}, bf16[1,16,128,128]{3,2,1,0:T(8,128)(2,1)}, u32[]{:S(2)}) copy-start(bf16[1,16,128,128]{3,2,1,0:T(8,128)(2,1)} %param.10) | copy-start | bytes 1572868
  5.8 0.7 %copy-start.10 = (f32[2048]{0:T(1024)S(1)}, f32[2048]{0:T(1024)}, u32[]{:S(2)}) copy-start(f32[2048]{0:T(1024)} %param.11) | copy-start | bytes 24580
  6.5 2.4 %copy-start.1 = (bf16[128,2048]{1,0:T(8,128)(2,1)S(1)}, bf16[128,2048]{1,0:T(8,128)(2,1)}, u32[]{:S(2)}) copy-start(bf16[128,2048]{1,0:T(8,128)(2,1)} %q_ref.5) | copy-start | bytes 1572868
  6.5 2.4 %copy-start.7 = (bf16[128,2048]{1,0:T(8,128)(2,1)S(1)}, bf16[128,2048]{1,0:T(8,128)(2,1)}, u32[]{:S(2)}) copy-start(bf16[128,2048]{1,0:T(8,128)(2,1)} %y_ref.3) | copy-start | bytes 1572868
  7.5 1.4 %collective-permute-start = (f32[128,128]{1,0:T(8,128)S(1)}, f32[128,128]{1,0:T(8,128)S(1)}, u32[]{:S(2)}, u32[]{:S(2)}) collective-permute-start(f32[128,128]{1,0:T(8,128)S(1)} %get-tuple-element.16.own_ref), channel_id=1, source_target_pairs={{0,1},{1,0},{2,3},{3,2},{4,5},{5,4},{6,7},{7,6},{8,9},{9,8},{10,11... | collective-permute-start | bytes 196616 | tf_op jit(solution)/shard_map/ppermute | solution.py:111
  8.1 0.9 %copy-start.11 = (f32[2048]{0:T(1024)S(1)}, f32[2048]{0:T(1024)}, u32[]{:S(2)}) copy-start(f32[2048]{0:T(1024)} %param.11) | copy-start | bytes 24580
  9.7 9.5 %collective-permute-start.1 = (f32[4,128,128]{2,1,0:T(8,128)S(1)}, f32[4,128,128]{2,1,0:T(8,128)S(1)}, u32[]{:S(2)}, u32[]{:S(2)}) collective-permute-start(f32[4,128,128]{2,1,0:T(8,128)S(1)} %get-tuple-element.24), channel_id=1, source_target_pairs={{0,2},{2,0},{4,6},{6,4},{8,10},{10,8},{12,14},{14,12},{1,3},{3,1},... | collective-permute-start | bytes 786440 | tf_op jit(solution)/shard_map/ppermute | solution.py:111
  12.6 9.2 %collective-permute-start.2 = (f32[4,128,128]{2,1,0:T(8,128)S(1)}, f32[4,128,128]{2,1,0:T(8,128)S(1)}, u32[]{:S(2)}, u32[]{:S(2)}) collective-permute-start(f32[4,128,128]{2,1,0:T(8,128)S(1)} %get-tuple-element.25), channel_id=1, source_target_pairs={{0,4},{2,6},{4,0},{6,2},{8,12},{10,14},{12,8},{14,10},{1,5},{3,7},... | collective-permute-start | bytes 786440 | tf_op jit(solution)/shard_map/ppermute | solution.py:111
  14.2 11.9 %collective-permute-start.3 = (f32[4,128,128]{2,1,0:T(8,128)S(1)}, f32[4,128,128]{2,1,0:T(8,128)S(1)}, u32[]{:S(2)}, u32[]{:S(2)}) collective-permute-start(f32[4,128,128]{2,1,0:T(8,128)S(1)} %get-tuple-element.26), channel_id=1, source_target_pairs={{0,6},{2,4},{4,2},{6,0},{8,14},{10,12},{12,10},{14,8},{1,7},{3,5},... | collective-permute-start | bytes 786440 | tf_op jit(solution)/shard_map/ppermute | solution.py:111
  26.2 14.1 %collective-permute-start.4 = (f32[4,128,128]{2,1,0:T(8,128)S(1)}, f32[4,128,128]{2,1,0:T(8,128)S(1)}, u32[]{:S(2)}, u32[]{:S(2)}) collective-permute-start(f32[4,128,128]{2,1,0:T(8,128)S(1)} %add_add_fusion), channel_id=1, source_target_pairs={{0,8},{2,10},{4,12},{6,14},{8,0},{10,2},{12,4},{14,6},{1,9},{3,11}... | collective-permute-start | bytes 786440 | tf_op jit(solution)/shard_map/ppermute | solution.py:111
  29.0 15.1 %copy-start.3 = (bf16[128,2048]{1,0:T(8,128)(2,1)S(1)}, bf16[128,2048]{1,0:T(8,128)(2,1)}, u32[]{:S(2)}) copy-start(bf16[128,2048]{1,0:T(8,128)(2,1)} %k_ref.5) | copy-start | bytes 1572868
  29.0 15.1 %copy-start.5 = (bf16[128,2048]{1,0:T(8,128)(2,1)S(1)}, bf16[128,2048]{1,0:T(8,128)(2,1)}, u32[]{:S(2)}) copy-start(bf16[128,2048]{1,0:T(8,128)(2,1)} %v_ref.5) | copy-start | bytes 1572868
  29.0 15.1 %copy-start.9 = (bf16[1,16,128,128]{3,2,1,0:T(8,128)(2,1)S(1)}, bf16[1,16,128,128]{3,2,1,0:T(8,128)(2,1)}, u32[]{:S(2)}) copy-start(bf16[1,16,128,128]{3,2,1,0:T(8,128)(2,1)} %param.10) | copy-start | bytes 1572868
  40.5 10.3 %collective-permute-start.7 = (f32[4,128,128]{2,1,0:T(8,128)S(1)}, f32[4,128,128]{2,1,0:T(8,128)S(1)}, u32[]{:S(2)}, u32[]{:S(2)}) collective-permute-start(f32[4,128,128]{2,1,0:T(8,128)S(1)} %get-tuple-element.29), channel_id=1, source_target_pairs={{0,6},{2,4},{4,2},{6,0},{8,14},{10,12},{12,10},{14,8},{1,7},{3,5},... | collective-permute-start | bytes 786440 | tf_op jit(solution)/shard_map/ppermute | solution.py:111
  42.0 12.1 %collective-permute-start.6 = (f32[4,128,128]{2,1,0:T(8,128)S(1)}, f32[4,128,128]{2,1,0:T(8,128)S(1)}, u32[]{:S(2)}, u32[]{:S(2)}) collective-permute-start(f32[4,128,128]{2,1,0:T(8,128)S(1)} %get-tuple-element.30), channel_id=1, source_target_pairs={{0,4},{2,6},{4,0},{6,2},{8,12},{10,14},{12,8},{14,10},{1,5},{3,7},... | collective-permute-start | bytes 786440 | tf_op jit(solution)/shard_map/ppermute | solution.py:111
  43.4 11.0 %collective-permute-start.5 = (f32[4,128,128]{2,1,0:T(8,128)S(1)}, f32[4,128,128]{2,1,0:T(8,128)S(1)}, u32[]{:S(2)}, u32[]{:S(2)}) collective-permute-start(f32[4,128,128]{2,1,0:T(8,128)S(1)} %get-tuple-element.31), channel_id=1, source_target_pairs={{0,2},{2,0},{4,6},{6,4},{8,10},{10,8},{12,14},{14,12},{1,3},{3,1},... | collective-permute-start | bytes 786440 | tf_op jit(solution)/shard_map/ppermute | solution.py:111

commit v2 on v1

v2 whole, which is shorter than its diff:
```python
import functools

import jax
import jax.numpy as jnp
from jax import lax
from jax.experimental import pallas as pl
from jax.experimental.pallas import tpu as pltpu
from jax.sharding import PartitionSpec as P

HEAD = 128
QUAD = 4
SPLIT = (2, 2)
STEPS = (3, 1, 2, 0)
GROUPS = 4
VMEM = pl.BlockSpec(memory_space=pltpu.VMEM)
ANY = pl.BlockSpec(memory_space=pl.ANY)
HBM = pl.BlockSpec(memory_space=pltpu.HBM)
NN = (((1,), (0,)), ((), ()))
NT = (((1,), (1,)), ((), ()))
TN = (((0,), (0,)), ((), ()))


def dot(left, right, dims):
    return lax.dot_general(left, right, dims, preferred_element_type=jnp.float32)


def columns(head, count=1):
    if isinstance(head, int):
        return pl.ds(head * HEAD, count * HEAD)
    return pl.ds(pl.multiple_of(head * HEAD, HEAD), count * HEAD)


def lower(rows):
    row = lax.broadcasted_iota(jnp.int32, (rows, rows), 0)
    return row >= lax.broadcasted_iota(jnp.int32, (rows, rows), 1)


def parts_of(heads):
    each = heads // QUAD
    parts, start = [], 0
    for index, count in enumerate(SPLIT):
        count = each - start if index == len(SPLIT) - 1 else count
        parts.append((start, count))
        start += count
    return each, parts


def forward_kernel(
    q_hbm, k_hbm, v_hbm, s_hbm, y_hbm, gain_hbm,
    out_ref, probs_ref, stat_ref, q_ref, k_ref, v_ref, s_ref, y_ref, gain_ref, sems, gain_sem,
):
    rows, width = q_ref.shape
    heads = width // HEAD
    count = heads // GROUPS
    gain_copy = pltpu.make_async_copy(gain_hbm, gain_ref, gain_sem)
    copies = []
    for group in range(GROUPS):
        at = columns(group * count, count)
        span = pl.ds(group * count, count)
        pairs = [(q_hbm.at[:, at], q_ref.at[:, at]), (k_hbm.at[:, at], k_ref.at[:, at])]
        pairs += [(v_hbm.at[:, at], v_ref.at[:, at]), (s_hbm.at[span], s_ref.at[span])]
        pairs += [(y_hbm.at[:, at], y_ref.at[:, at])]
        copies.append(
            [
                pltpu.make_async_copy(source, target, sems.at[group, index])
                for index, (source, target) in enumerate(pairs)
            ]
        )
    for copy in copies[0] + [gain_copy] + sum(copies[1:], []):
        copy.start()
    mask = lower(rows)
    squares = jnp.zeros((rows, HEAD), jnp.float32)
    crosses = jnp.zeros((rows, HEAD), jnp.float32)
    for group in range(GROUPS):
        for copy in copies[group]:
            copy.wait()
        if group == 0:
            gain_copy.wait()
        for head in range(group * count, (group + 1) * count):
            at = columns(head)
            q = q_ref[:, at]
            probs = jnp.where(mask, dot(q, k_ref[:, at], NT), 0.0).astype(jnp.bfloat16)
            probs_ref[:, at] = probs
            out = dot(probs, v_ref[:, at], NN) + dot(q, s_ref[head], NN)
            out_ref[:, at] = out
            squares += out * out
            crosses += gain_ref[:, at] * y_ref[:, at].astype(jnp.float32) * out
    lane = lax.broadcasted_iota(jnp.int32, (rows, HEAD), 1)
    square = jnp.sum(squares, axis=1, keepdims=True)
    cross = jnp.sum(crosses, axis=1, keepdims=True)
    stat_ref[...] = jnp.where(lane == 0, square, cross)


def state_kernel(
    features, each, start, count, own_ref, other_ref, out_ref, y_ref, gain_ref, q_ref, *refs
):
    g_ref, *u_refs = refs[-1 - QUAD :]
    stat = own_ref[...] + other_ref[...]
    square, cross = stat[:, 0:1], stat[:, 1:2]
    inverse = lax.rsqrt(square / features + 1e-06)
    back = cross * (inverse * inverse * inverse) / features
    me = lax.rem(lax.axis_index("ctx"), QUAD)
    for step in STEPS:
        for local in range(count):
            at = columns((me ^ step) * each + start + local)
            weighted = gain_ref[:, at] * y_ref[:, at].astype(jnp.float32)
            grad = (inverse * weighted - out_ref[:, at] * back).astype(jnp.bfloat16)
            g_ref[:, columns(step * count + local)] = grad
            u_refs[step][local] = dot(q_ref[:, at], grad, TN)


def suffix_kernel(*refs):
    block_refs, behind_refs, sum_refs = refs[:QUAD], refs[QUAD:-QUAD], refs[-QUAD:]
    place = lax.axis_index("ctx")
    me = lax.rem(place, QUAD)
    blocks = [ref[...] for ref in block_refs]
    behind = jnp.zeros_like(blocks[0])
    for level, ref in enumerate(behind_refs):
        behind += jnp.where((place & (QUAD << level)) == 0, ref[...], 0.0)
    for target in STEPS:
        value = behind
        for source in range(QUAD):
            if source != target:
                value += jnp.where((me ^ source) > (me ^ target), blocks[source], 0.0)
        sum_refs[target][...] = value


def local_kernel(each, parts, q_ref, k_ref, v_ref, s_ref, probs_ref, *refs):
    g_refs, query_ref = refs[: len(parts)], refs[len(parts)]
    key_refs = refs[len(parts) + 1 : 2 * len(parts) + 1]
    value_refs = refs[2 * len(parts) + 1 :]
    mask = lower(q_ref.shape[0])
    me = lax.rem(lax.axis_index("ctx"), QUAD)
    for part, (start, count) in enumerate(parts):
        for step in range(QUAD):
            for local in range(count):
                head = (me ^ step) * each + start + local
                at, slot = columns(head), columns(step * count + local)
                g = g_refs[part][:, slot]
                grads = jnp.where(mask, dot(g, v_ref[:, at], NT), 0.0).astype(jnp.bfloat16)
                query = dot(grads, k_ref[:, at], NN) + dot(g, s_ref[head], NT)
                query_ref[:, at] = query.astype(jnp.bfloat16)
                key_refs[part][:, slot] = dot(grads, q_ref[:, at], TN)
                value_refs[part][:, slot] = dot(probs_ref[:, at], g, TN)


def final_kernel(each, start, count, k_ref, v_ref, key_in, value_in, *refs):
    later_refs = refs[:QUAD]
    key_hbm, value_hbm, key_ref, value_ref, sems = refs[-5:]
    me = lax.rem(lax.axis_index("ctx"), QUAD)
    copies = []
    for step in (0, 1, 2, 3):
        slots = columns(step * count, count)
        for local in range(count):
            at = columns((me ^ step) * each + start + local)
            slot = columns(step * count + local)
            later = later_refs[step][local].astype(jnp.bfloat16)
            key = key_in[:, slot] + dot(v_ref[:, at], later, NT)
            key_ref[:, slot] = key.astype(jnp.bfloat16)
            value = value_in[:, slot] + dot(k_ref[:, at], later, NN)
            value_ref[:, slot] = value.astype(jnp.bfloat16)
        at = columns((me ^ step) * each + start, count)
        for index, (source, target) in enumerate(((key_ref, key_hbm), (value_ref, value_hbm))):
            copy = pltpu.make_async_copy(source.at[:, slots], target.at[:, at], sems.at[step, index])
            copy.start()
            copies.append(copy)
    for copy in copies:
        copy.wait()


def params(mib):
    return pltpu.CompilerParams(vmem_limit_bytes=mib << 20)


def partner(value, axis, mask):
    count = lax.axis_size(axis)
    return lax.ppermute(value, axis, [(source, source ^ mask) for source in range(count)])


def per_device(queries, keys, values, grad_y, state_low, gain):
    rows, width = queries.shape
    heads = width // HEAD
    each, parts = parts_of(heads)
    features = width * lax.axis_size("tp")
    state = state_low[0]
    gain_row = gain.reshape(1, width)

    near = pltpu.VMEM
    half = jax.ShapeDtypeStruct((rows, width), jnp.bfloat16)
    held_half = near((rows, width), jnp.bfloat16)
    operands = (queries, keys, values, state, grad_y, gain_row)
    out, probs, stat, q, k, v, s, y, gain_v = pl.pallas_call(
        forward_kernel,
        out_shape=(
            near((rows, width), jnp.float32),
            held_half,
            near((rows, HEAD), jnp.float32),
            held_half,
            held_half,
            held_half,
            near(state.shape, state.dtype),
            held_half,
            near(gain_row.shape, gain_row.dtype),
        ),
        in_specs=[HBM] * 6,
        out_specs=(VMEM,) * 9,
        scratch_shapes=[pltpu.SemaphoreType.DMA((GROUPS, 5)), pltpu.SemaphoreType.DMA],
        compiler_params=params(8),
    )(*(pltpu.with_memory_space_constraint(value, pltpu.HBM) for value in operands))
    other = partner(stat, "tp", 1)

    grads, held = [], []
    for start, count in parts:
        tokens = held[-1][1:2] if held else []
        piece = near((count, HEAD, HEAD), jnp.float32)
        grad, *own = pl.pallas_call(
            functools.partial(state_kernel, features, each, start, count),
            out_shape=(near((rows, QUAD * count * HEAD), jnp.bfloat16),) + (piece,) * QUAD,
            in_specs=[VMEM] * 6 + [ANY] * len(tokens),
            out_specs=(VMEM,) * (1 + QUAD),
            compiler_params=params(8),
        )(stat, other, out, y, gain_v, q, *tokens)
        grads.append(grad)
        came = {step: partner(own[step], "ctx", step) for step in (3, 1, 2)}
        held.append([own[0], came[1], came[2], came[3]])
    later = []
    for blocks in held:
        total = blocks[0] + blocks[1] + blocks[2] + blocks[3]
        behind = []
        span = QUAD
        while span < lax.axis_size("ctx"):
            behind.append(partner(total, "ctx", span))
            span *= 2
            if span < lax.axis_size("ctx"):
                total = total + behind[-1]
        piece = near(total.shape, jnp.float32)
        sums = pl.pallas_call(
            suffix_kernel,
            out_shape=(piece,) * QUAD,
            in_specs=[VMEM] * (QUAD + len(behind)),
            out_specs=(VMEM,) * QUAD,
            compiler_params=params(8),
        )(*blocks, *behind)
        came = {step: partner(sums[step], "ctx", step) for step in (3, 1, 2)}
        later.append([sums[0], came[1], came[2], came[3]])

    slots = [near((rows, QUAD * count * HEAD), jnp.float32) for _, count in parts]
    grad_query, *local = pl.pallas_call(
        functools.partial(local_kernel, each, parts),
        out_shape=(half, *slots, *slots),
        in_specs=[VMEM] * (5 + len(parts)),
        out_specs=(VMEM,) * (1 + 2 * len(parts)),
        compiler_params=params(8),
    )(q, k, v, s, probs, *grads)
    done = ()
    for part, (start, count) in enumerate(parts):
        stage = pltpu.VMEM((rows, QUAD * count * HEAD), jnp.bfloat16)
        done = pl.pallas_call(
            functools.partial(final_kernel, each, start, count),
            out_shape=(half, half),
            in_specs=[VMEM] * (4 + QUAD) + [HBM] * len(done),
            out_specs=(HBM,) * 2,
            scratch_shapes=[stage, stage, pltpu.SemaphoreType.DMA((QUAD, 2))],
            input_output_aliases={4 + QUAD + index: index for index in range(len(done))},
            compiler_params=params(8),
        )(k, v, local[part], local[len(parts) + part], *later[part], *done)
    return (grad_query, *done)


def solution(mesh):
    rows = P(("groups", "ctx"), "tp")
    return jax.shard_map(
        per_device,
        mesh=mesh,
        in_specs=(rows, rows, rows, rows, P(("groups", "ctx"), "tp", None, None), P("tp")),
        out_specs=(rows, rows, rows),
        check_vma=False,
    )
```

time: 56.5 us -> 44.1 us (0.78)
  waiting for transfers between devices: 31 us -> 11.1 us
  starting transfers between devices: 11.4 us -> 21.8 us
  local copies, waits for them, and re-layouts: 5.92 us -> 0 us
  Pallas kernels: 6.76 us -> 10.2 us
    ppermute x8 -> x15, waiting for transfers between devices: 31 us -> 11.1 us  [partner(): lax.ppermute(value, axis, [(source, source ^ mask) for source in range(co...]
    ppermute x8 -> x15, starting transfers between devices: 11.4 us -> 21.8 us  [partner(): lax.ppermute(value, axis, [(source, source ^ mask) for source in range(co...]
    unnamed x24 -> x0, local copies, waits for them, and re-layouts: 5.92 us -> none
    pallas_call x4 -> x8, Pallas kernels: 6.76 us -> 10.2 us  [the longest x1 3.44 us: per_device(): pl.pallas_call(forward_kernel, out_shape=(near((rows, width), jnp.float32...]
  transfers between devices with their start and end apart: 8 -> 15, of which waited for: 8 -> 8; matrix products, arithmetic and copies ran while one was open for 0% -> 0% of each run, Pallas kernels for 6% -> 12%
where the time goes in v2:
time: 44.1 us; the launch traced here: 44 us
  starting transfers between devices  21.8 us (49%)
  waiting for transfers between devices  11.1 us (25%)
  Pallas kernels  10.2 us (23%)
  between operations  0.7 us (2%)
    ppermute x15, starting transfers between devices, partner(): lax.ppermute(value, axis, [(source, source ^ mask) for source in range(co...  21.8 us
    ppermute x15, waiting for transfers between devices, partner(): lax.ppermute(value, axis, [(source, source ^ mask) for source in range(co...  11.1 us
    pallas_call x1, Pallas kernels, per_device(): pl.pallas_call(forward_kernel, out_shape=(near((rows, width), jnp.float32...  3.44 us
    pallas_call x1, Pallas kernels, per_device(): pl.pallas_call(functools.partial(local_kernel, each, parts), out_shape=(h...  3.39 us
    pallas_call x2, Pallas kernels, per_device(): pl.pallas_call(functools.partial(final_kernel, each, start, count), out_s...  2.21 us
    pallas_call x2, Pallas kernels, per_device(): pl.pallas_call(functools.partial(state_kernel, features, each, start, cou...  0.9 us
  transfers between devices with their start and end apart: 15, of which 8 were waited for; matrix products, arithmetic and copies ran while one was open for 0% of the time, Pallas kernels for 12%

profile of v2, /device:TPU:0, one launch (start us, length us, event | category | flops | bytes accessed | tf_op | source)
XLA Modules:
  0.0 44.0 jit_solution(15835394757123454184)
XLA Ops:
  0.6 3.4 %shard_map.85 = (f32[128,2048]{1,0:T(8,128)S(1)}, bf16[128,2048]{1,0:T(8,128)(2,1)S(1)}, f32[128,128]{1,0:T(8,128)S(1)}, bf16[128,2048]{1,0:T(8,128)(2,1)S(1)}, ...) custom-call(bf16[128,2048]{1,0:T(8,128)(2,1)} %q_hbm.1, ...), custom_call_target="tpu_custom_call" | custom-call | tf_op jit(solution)/shard_map/pallas_call | solution.py:192
  4.1 0.5 %collective-permute-start = (f32[128,128]{1,0:T(8,128)S(1)}, f32[128,128]{1,0:T(8,128)S(1)}, u32[]{:S(2)}, u32[]{:S(2)}) collective-permute-start(f32[128,128]{1,0:T(8,128)S(1)} %get-tuple-element.44.own_ref), channel_id=1, source_target_pairs={{0,1},{1,0},{2,3},{3,2},{4,5},{5,4},{6,7},{7,6},{8,9},{9,8},{10,11... | collective-permute-start | bytes 196616 | tf_op jit(solution)/shard_map/ppermute | solution.py:177
  4.6 0.9 %collective-permute-done.other_ref = f32[128,128]{1,0:T(8,128)S(1)} collective-permute-done((f32[128,128]{1,0:T(8,128)S(1)}, f32[128,128]{1,0:T(8,128)S(1)}, u32[]{:S(2)}, u32[]{:S(2)}) %collective-permute-start) | collective-permute-done | bytes 65568 | tf_op jit(solution)/shard_map/ppermute | solution.py:177
  5.5 0.4 %shard_map.86 = (bf16[128,1024]{1,0:T(8,128)(2,1)S(1)}, f32[2,128,128]{2,1,0:T(8,128)S(1)}, f32[2,128,128]{2,1,0:T(8,128)S(1)}, f32[2,128,128]{2,1,0:T(8,128)S(1)}, f32[2,128,128]{2,1,0:T(8,128)S(1)}) custom-call(f32[128,128]{1,0:T(8,128)S(1)} %get-tuple-element.44.own_ref, f32[128,128]{1,0:T(8,128)S(1)} %collective-permute-done.other_ref, ...), custom_call_target="tpu_custom_call" | custom-call | tf_op jit(solution)/shard_map/pallas_call | solution.py:216
  5.9 2.9 %collective-permute-start.1 = (f32[2,128,128]{2,1,0:T(8,128)S(1)}, f32[2,128,128]{2,1,0:T(8,128)S(1)}, u32[]{:S(2)}, u32[]{:S(2)}) collective-permute-start(f32[2,128,128]{2,1,0:T(8,128)S(1)} %get-tuple-element.49), channel_id=1, source_target_pairs={{0,2},{2,0},{4,6},{6,4},{8,10},{10,8},{12,14},{14,12},{1,3},{3,1},... | collective-permute-start | bytes 393224 | tf_op jit(solution)/shard_map/ppermute | solution.py:177
  8.9 1.6 %collective-permute-start.9 = (f32[2,128,128]{2,1,0:T(8,128)S(1)}, f32[2,128,128]{2,1,0:T(8,128)S(1)}, u32[]{:S(2)}, u32[]{:S(2)}) collective-permute-start(f32[2,128,128]{2,1,0:T(8,128)S(1)} %get-tuple-element.65), channel_id=1, source_target_pairs={{0,4},{2,6},{4,0},{6,2},{8,12},{10,14},{12,8},{14,10},{1,5},{3,7},... | collective-permute-start | bytes 393224 | tf_op jit(solution)/shard_map/ppermute | solution.py:177
  10.4 0.0 collective-permute-start.10
  10.4 2.2 %collective-permute-done.1.refs_0_.refs_1_ = f32[2,128,128]{2,1,0:T(8,128)S(1)} collective-permute-done((f32[2,128,128]{2,1,0:T(8,128)S(1)}, f32[2,128,128]{2,1,0:T(8,128)S(1)}, u32[]{:S(2)}, u32[]{:S(2)}) %collective-permute-start.1) | collective-permute-done | bytes 131104 | tf_op jit(solution)/shard_map/ppermute | solution.py:177
  12.7 0.5 %shard_map.87 = (bf16[128,1024]{1,0:T(8,128)(2,1)S(1)}, f32[2,128,128]{2,1,0:T(8,128)S(1)}, f32[2,128,128]{2,1,0:T(8,128)S(1)}, f32[2,128,128]{2,1,0:T(8,128)S(1)}, f32[2,128,128]{2,1,0:T(8,128)S(1)}) custom-call(f32[128,128]{1,0:T(8,128)S(1)} %get-tuple-element.44.own_ref, f32[128,128]{1,0:T(8,128)S(1)} %collective-permute-done.other_ref, ...), custom_call_target="tpu_custom_call" | custom-call | tf_op jit(solution)/shard_map/pallas_call | solution.py:216
  13.1 1.8 %collective-permute-start.2 = (f32[2,128,128]{2,1,0:T(8,128)S(1)}, f32[2,128,128]{2,1,0:T(8,128)S(1)}, u32[]{:S(2)}, u32[]{:S(2)}) collective-permute-start(f32[2,128,128]{2,1,0:T(8,128)S(1)} %get-tuple-element.55), channel_id=1, source_target_pairs={{0,2},{2,0},{4,6},{6,4},{8,10},{10,8},{12,14},{14,12},{1,3},{3,1},... | collective-permute-start | bytes 393224 | tf_op jit(solution)/shard_map/ppermute | solution.py:177
  14.9 1.6 %collective-permute-start.3 = (f32[2,128,128]{2,1,0:T(8,128)S(1)}, f32[2,128,128]{2,1,0:T(8,128)S(1)}, u32[]{:S(2)}, u32[]{:S(2)}) collective-permute-start(f32[2,128,128]{2,1,0:T(8,128)S(1)} %get-tuple-element.56), channel_id=1, source_target_pairs={{0,4},{2,6},{4,0},{6,2},{8,12},{10,14},{12,8},{14,10},{1,5},{3,7},... | collective-permute-start | bytes 393224 | tf_op jit(solution)/shard_map/ppermute | solution.py:177
  16.5 0.2 collective-permute-start.4
  16.7 0.0 collective-permute-done.9.refs_2_
  16.7 0.1 collective-permute-done.10.refs_3_
  16.9 3.0 %collective-permute-start.11 = (f32[2,128,128]{2,1,0:T(8,128)S(1)}, f32[2,128,128]{2,1,0:T(8,128)S(1)}, u32[]{:S(2)}, u32[]{:S(2)}) collective-permute-start(f32[2,128,128]{2,1,0:T(8,128)S(1)} %add_add_fusion), channel_id=1, source_target_pairs={{0,8},{2,10},{4,12},{6,14},{8,0},{10,2},{12,4},{14,6},{1,9},{3,11}... | collective-permute-start | bytes 393224 | tf_op jit(solution)/shard_map/ppermute | solution.py:177
  19.9 0.5 %collective-permute-done.2.refs_1_ = f32[2,128,128]{2,1,0:T(8,128)S(1)} collective-permute-done((f32[2,128,128]{2,1,0:T(8,128)S(1)}, f32[2,128,128]{2,1,0:T(8,128)S(1)}, u32[]{:S(2)}, u32[]{:S(2)}) %collective-permute-start.2) | collective-permute-done | bytes 131104 | tf_op jit(solution)/shard_map/ppermute | solution.py:177
  20.4 3.6 %collective-permute-done.3.refs_2_ = f32[2,128,128]{2,1,0:T(8,128)S(1)} collective-permute-done((f32[2,128,128]{2,1,0:T(8,128)S(1)}, f32[2,128,128]{2,1,0:T(8,128)S(1)}, u32[]{:S(2)}, u32[]{:S(2)}) %collective-permute-start.3) | collective-permute-done | bytes 131104 | tf_op jit(solution)/shard_map/ppermute | solution.py:177
  24.0 1.3 %collective-permute-done.4.refs_3_ = f32[2,128,128]{2,1,0:T(8,128)S(1)} collective-permute-done((f32[2,128,128]{2,1,0:T(8,128)S(1)}, f32[2,128,128]{2,1,0:T(8,128)S(1)}, u32[]{:S(2)}, u32[]{:S(2)}) %collective-permute-start.4) | collective-permute-done | bytes 131104 | tf_op jit(solution)/shard_map/ppermute | solution.py:177
  25.3 1.7 %collective-permute-start.5 = (f32[2,128,128]{2,1,0:T(8,128)S(1)}, f32[2,128,128]{2,1,0:T(8,128)S(1)}, u32[]{:S(2)}, u32[]{:S(2)}) collective-permute-start(f32[2,128,128]{2,1,0:T(8,128)S(1)} %add_add_fusion.1), channel_id=1, source_target_pairs={{0,8},{2,10},{4,12},{6,14},{8,0},{10,2},{12,4},{14,6},{1,9},{3,11}... | collective-permute-start | bytes 393224 | tf_op jit(solution)/shard_map/ppermute | solution.py:177
  26.9 0.0 collective-permute-done.11.refs_4_
  26.9 0.1 shard_map.90
  27.1 1.2 %collective-permute-start.12 = (f32[2,128,128]{2,1,0:T(8,128)S(1)}, f32[2,128,128]{2,1,0:T(8,128)S(1)}, u32[]{:S(2)}, u32[]{:S(2)}) collective-permute-start(f32[2,128,128]{2,1,0:T(8,128)S(1)} %get-tuple-element.68), channel_id=1, source_target_pairs={{0,2},{2,0},{4,6},{6,4},{8,10},{10,8},{12,14},{14,12},{1,3},{3,1},... | collective-permute-start | bytes 393224 | tf_op jit(solution)/shard_map/ppermute | solution.py:177
  28.3 2.8 %collective-permute-start.13 = (f32[2,128,128]{2,1,0:T(8,128)S(1)}, f32[2,128,128]{2,1,0:T(8,128)S(1)}, u32[]{:S(2)}, u32[]{:S(2)}) collective-permute-start(f32[2,128,128]{2,1,0:T(8,128)S(1)} %get-tuple-element.69), channel_id=1, source_target_pairs={{0,4},{2,6},{4,0},{6,2},{8,12},{10,14},{12,8},{14,10},{1,5},{3,7},... | collective-permute-start | bytes 393224 | tf_op jit(solution)/shard_map/ppermute | solution.py:177
  31.1 0.0 collective-permute-start.14
  31.1 1.9 %collective-permute-done.5.refs_4_ = f32[2,128,128]{2,1,0:T(8,128)S(1)} collective-permute-done((f32[2,128,128]{2,1,0:T(8,128)S(1)}, f32[2,128,128]{2,1,0:T(8,128)S(1)}, u32[]{:S(2)}, u32[]{:S(2)}) %collective-permute-start.5) | collective-permute-done | bytes 131104 | tf_op jit(solution)/shard_map/ppermute | solution.py:177
  33.0 0.1 shard_map.89
  33.2 1.5 %collective-permute-start.6 = (f32[2,128,128]{2,1,0:T(8,128)S(1)}, f32[2,128,128]{2,1,0:T(8,128)S(1)}, u32[]{:S(2)}, u32[]{:S(2)}) collective-permute-start(f32[2,128,128]{2,1,0:T(8,128)S(1)} %get-tuple-element.59), channel_id=1, source_target_pairs={{0,2},{2,0},{4,6},{6,4},{8,10},{10,8},{12,14},{14,12},{1,3},{3,1},... | collective-permute-start | bytes 393224 | tf_op jit(solution)/shard_map/ppermute | solution.py:177
  34.7 0.8 %collective-permute-start.7 = (f32[2,128,128]{2,1,0:T(8,128)S(1)}, f32[2,128,128]{2,1,0:T(8,128)S(1)}, u32[]{:S(2)}, u32[]{:S(2)}) collective-permute-start(f32[2,128,128]{2,1,0:T(8,128)S(1)} %get-tuple-element.60), channel_id=1, source_target_pairs={{0,4},{2,6},{4,0},{6,2},{8,12},{10,14},{12,8},{14,10},{1,5},{3,7},... | collective-permute-start | bytes 393224 | tf_op jit(solution)/shard_map/ppermute | solution.py:177
  35.5 0.0 collective-permute-done.12.refs_1_
  35.5 2.3 %collective-permute-start.8 = (f32[2,128,128]{2,1,0:T(8,128)S(1)}, f32[2,128,128]{2,1,0:T(8,128)S(1)}, u32[]{:S(2)}, u32[]{:S(2)}) collective-permute-start(f32[2,128,128]{2,1,0:T(8,128)S(1)} %get-tuple-element.61), channel_id=1, source_target_pairs={{0,6},{2,4},{4,2},{6,0},{8,14},{10,12},{12,10},{14,8},{1,7},{3,5},... | collective-permute-start | bytes 393224 | tf_op jit(solution)/shard_map/ppermute | solution.py:177
  37.8 3.4 %shard_map.88 = (bf16[128,2048]{1,0:T(8,128)(2,1)}, f32[128,1024]{1,0:T(8,128)S(1)}, f32[128,1024]{1,0:T(8,128)S(1)}, f32[128,1024]{1,0:T(8,128)S(1)}, f32[128,1024]{1,0:T(8,128)S(1)}) custom-call(bf16[128,2048]{1,0:T(8,128)(2,1)S(1)} %get-tuple-element.39.q_ref, bf16[128,2048]{1,0:T(8,128)(2,1)S(1)} %get-tuple-element.40.k_ref, ...), custom_call_target="tpu_custom_call" | custom-call | tf_op jit(solution)/shard_map/pallas_call | solution.py:248
  41.2 0.0 collective-permute-done.13.refs_2_
  41.2 0.0 collective-permute-done.14.refs_3_
  41.2 1.1 %shard_map.91 = (bf16[128,2048]{1,0:T(8,128)(2,1)}, bf16[128,2048]{1,0:T(8,128)(2,1)}) custom-call(bf16[128,2048]{1,0:T(8,128)(2,1)S(1)} %get-tuple-element.40.k_ref, bf16[128,2048]{1,0:T(8,128)(2,1)S(1)} %get-tuple-element.41.v_ref, f32[128,1024]{1,0:T(8,128)S(1)} %get-tuple-element.62.key_in, f32[128,1024]{1,0:T(8,128)S(1)} %get-tuple-element.63.value_in, ...), custom_call_target="tpu_custom_call" | custom-call | tf_op jit(solution)/shard_map/pallas_call | solution.py:258
  42.3 0.0 collective-permute-done.6.refs_1_
  42.3 0.0 collective-permute-done.7.refs_2_
  42.3 0.5 %collective-permute-done.8.refs_3_ = f32[2,128,128]{2,1,0:T(8,128)S(1)} collective-permute-done((f32[2,128,128]{2,1,0:T(8,128)S(1)}, f32[2,128,128]{2,1,0:T(8,128)S(1)}, u32[]{:S(2)}, u32[]{:S(2)}) %collective-permute-start.8) | collective-permute-done | bytes 131104 | tf_op jit(solution)/shard_map/ppermute | solution.py:177
  42.9 1.1 %shard_map.92 = (bf16[128,2048]{1,0:T(8,128)(2,1)}, bf16[128,2048]{1,0:T(8,128)(2,1)}) custom-call(bf16[128,2048]{1,0:T(8,128)(2,1)S(1)} %get-tuple-element.40.k_ref, bf16[128,2048]{1,0:T(8,128)(2,1)S(1)} %get-tuple-element.41.v_ref, f32[128,1024]{1,0:T(8,128)S(1)} %get-tuple-element.52.key_in, ...), custom_call_target="tpu_custom_call", output_to_operand_aliasing={{0}: (8, {}), {1}: (9, {})} | custom-call | tf_op jit(solution)/shard_map/pallas_call | solution.py:258
  (2 shorter events, 0.1 us)
Async XLA Ops:
  4.1 1.4 %collective-permute-start = (f32[128,128]{1,0:T(8,128)S(1)}, f32[128,128]{1,0:T(8,128)S(1)}, u32[]{:S(2)}, u32[]{:S(2)}) collective-permute-start(f32[128,128]{1,0:T(8,128)S(1)} %get-tuple-element.44.own_ref), channel_id=1, source_target_pairs={{0,1},{1,0},{2,3},{3,2},{4,5},{5,4},{6,7},{7,6},{8,9},{9,8},{10,11... | collective-permute-start | bytes 196616 | tf_op jit(solution)/shard_map/ppermute | solution.py:177
  5.9 6.7 %collective-permute-start.1 = (f32[2,128,128]{2,1,0:T(8,128)S(1)}, f32[2,128,128]{2,1,0:T(8,128)S(1)}, u32[]{:S(2)}, u32[]{:S(2)}) collective-permute-start(f32[2,128,128]{2,1,0:T(8,128)S(1)} %get-tuple-element.49), channel_id=1, source_target_pairs={{0,2},{2,0},{4,6},{6,4},{8,10},{10,8},{12,14},{14,12},{1,3},{3,1},... | collective-permute-start | bytes 393224 | tf_op jit(solution)/shard_map/ppermute | solution.py:177
  8.9 7.8 %collective-permute-start.9 = (f32[2,128,128]{2,1,0:T(8,128)S(1)}, f32[2,128,128]{2,1,0:T(8,128)S(1)}, u32[]{:S(2)}, u32[]{:S(2)}) collective-permute-start(f32[2,128,128]{2,1,0:T(8,128)S(1)} %get-tuple-element.65), channel_id=1, source_target_pairs={{0,4},{2,6},{4,0},{6,2},{8,12},{10,14},{12,8},{14,10},{1,5},{3,7},... | collective-permute-start | bytes 393224 | tf_op jit(solution)/shard_map/ppermute | solution.py:177
  10.4 6.4 %collective-permute-start.10 = (f32[2,128,128]{2,1,0:T(8,128)S(1)}, f32[2,128,128]{2,1,0:T(8,128)S(1)}, u32[]{:S(2)}, u32[]{:S(2)}) collective-permute-start(f32[2,128,128]{2,1,0:T(8,128)S(1)} %get-tuple-element.66), channel_id=1, source_target_pairs={{0,6},{2,4},{4,2},{6,0},{8,14},{10,12},{12,10},{14,8},{1,7},{3,5},... | collective-permute-start | bytes 393224 | tf_op jit(solution)/shard_map/ppermute | solution.py:177
  13.1 7.2 %collective-permute-start.2 = (f32[2,128,128]{2,1,0:T(8,128)S(1)}, f32[2,128,128]{2,1,0:T(8,128)S(1)}, u32[]{:S(2)}, u32[]{:S(2)}) collective-permute-start(f32[2,128,128]{2,1,0:T(8,128)S(1)} %get-tuple-element.55), channel_id=1, source_target_pairs={{0,2},{2,0},{4,6},{6,4},{8,10},{10,8},{12,14},{14,12},{1,3},{3,1},... | collective-permute-start | bytes 393224 | tf_op jit(solution)/shard_map/ppermute | solution.py:177
  14.9 9.0 %collective-permute-start.3 = (f32[2,128,128]{2,1,0:T(8,128)S(1)}, f32[2,128,128]{2,1,0:T(8,128)S(1)}, u32[]{:S(2)}, u32[]{:S(2)}) collective-permute-start(f32[2,128,128]{2,1,0:T(8,128)S(1)} %get-tuple-element.56), channel_id=1, source_target_pairs={{0,4},{2,6},{4,0},{6,2},{8,12},{10,14},{12,8},{14,10},{1,5},{3,7},... | collective-permute-start | bytes 393224 | tf_op jit(solution)/shard_map/ppermute | solution.py:177
  16.5 8.7 %collective-permute-start.4 = (f32[2,128,128]{2,1,0:T(8,128)S(1)}, f32[2,128,128]{2,1,0:T(8,128)S(1)}, u32[]{:S(2)}, u32[]{:S(2)}) collective-permute-start(f32[2,128,128]{2,1,0:T(8,128)S(1)} %get-tuple-element.57), channel_id=1, source_target_pairs={{0,6},{2,4},{4,2},{6,0},{8,14},{10,12},{12,10},{14,8},{1,7},{3,5},... | collective-permute-start | bytes 393224 | tf_op jit(solution)/shard_map/ppermute | solution.py:177
  16.9 10.1 %collective-permute-start.11 = (f32[2,128,128]{2,1,0:T(8,128)S(1)}, f32[2,128,128]{2,1,0:T(8,128)S(1)}, u32[]{:S(2)}, u32[]{:S(2)}) collective-permute-start(f32[2,128,128]{2,1,0:T(8,128)S(1)} %add_add_fusion), channel_id=1, source_target_pairs={{0,8},{2,10},{4,12},{6,14},{8,0},{10,2},{12,4},{14,6},{1,9},{3,11}... | collective-permute-start | bytes 393224 | tf_op jit(solution)/shard_map/ppermute | solution.py:177
  25.3 7.7 %collective-permute-start.5 = (f32[2,128,128]{2,1,0:T(8,128)S(1)}, f32[2,128,128]{2,1,0:T(8,128)S(1)}, u32[]{:S(2)}, u32[]{:S(2)}) collective-permute-start(f32[2,128,128]{2,1,0:T(8,128)S(1)} %add_add_fusion.1), channel_id=1, source_target_pairs={{0,8},{2,10},{4,12},{6,14},{8,0},{10,2},{12,4},{14,6},{1,9},{3,11}... | collective-permute-start | bytes 393224 | tf_op jit(solution)/shard_map/ppermute | solution.py:177
  27.1 8.4 %collective-permute-start.12 = (f32[2,128,128]{2,1,0:T(8,128)S(1)}, f32[2,128,128]{2,1,0:T(8,128)S(1)}, u32[]{:S(2)}, u32[]{:S(2)}) collective-permute-start(f32[2,128,128]{2,1,0:T(8,128)S(1)} %get-tuple-element.68), channel_id=1, source_target_pairs={{0,2},{2,0},{4,6},{6,4},{8,10},{10,8},{12,14},{14,12},{1,3},{3,1},... | collective-permute-start | bytes 393224 | tf_op jit(solution)/shard_map/ppermute | solution.py:177
  28.3 12.9 %collective-permute-start.13 = (f32[2,128,128]{2,1,0:T(8,128)S(1)}, f32[2,128,128]{2,1,0:T(8,128)S(1)}, u32[]{:S(2)}, u32[]{:S(2)}) collective-permute-start(f32[2,128,128]{2,1,0:T(8,128)S(1)} %get-tuple-element.69), channel_id=1, source_target_pairs={{0,4},{2,6},{4,0},{6,2},{8,12},{10,14},{12,8},{14,10},{1,5},{3,7},... | collective-permute-start | bytes 393224 | tf_op jit(solution)/shard_map/ppermute | solution.py:177
  31.1 10.1 %collective-permute-start.14 = (f32[2,128,128]{2,1,0:T(8,128)S(1)}, f32[2,128,128]{2,1,0:T(8,128)S(1)}, u32[]{:S(2)}, u32[]{:S(2)}) collective-permute-start(f32[2,128,128]{2,1,0:T(8,128)S(1)} %get-tuple-element.70), channel_id=1, source_target_pairs={{0,6},{2,4},{4,2},{6,0},{8,14},{10,12},{12,10},{14,8},{1,7},{3,5},... | collective-permute-start | bytes 393224 | tf_op jit(solution)/shard_map/ppermute | solution.py:177
  33.2 9.1 %collective-permute-start.6 = (f32[2,128,128]{2,1,0:T(8,128)S(1)}, f32[2,128,128]{2,1,0:T(8,128)S(1)}, u32[]{:S(2)}, u32[]{:S(2)}) collective-permute-start(f32[2,128,128]{2,1,0:T(8,128)S(1)} %get-tuple-element.59), channel_id=1, source_target_pairs={{0,2},{2,0},{4,6},{6,4},{8,10},{10,8},{12,14},{14,12},{1,3},{3,1},... | collective-permute-start | bytes 393224 | tf_op jit(solution)/shard_map/ppermute | solution.py:177
  34.7 7.6 %collective-permute-start.7 = (f32[2,128,128]{2,1,0:T(8,128)S(1)}, f32[2,128,128]{2,1,0:T(8,128)S(1)}, u32[]{:S(2)}, u32[]{:S(2)}) collective-permute-start(f32[2,128,128]{2,1,0:T(8,128)S(1)} %get-tuple-element.60), channel_id=1, source_target_pairs={{0,4},{2,6},{4,0},{6,2},{8,12},{10,14},{12,8},{14,10},{1,5},{3,7},... | collective-permute-start | bytes 393224 | tf_op jit(solution)/shard_map/ppermute | solution.py:177
  35.5 7.4 %collective-permute-start.8 = (f32[2,128,128]{2,1,0:T(8,128)S(1)}, f32[2,128,128]{2,1,0:T(8,128)S(1)}, u32[]{:S(2)}, u32[]{:S(2)}) collective-permute-start(f32[2,128,128]{2,1,0:T(8,128)S(1)} %get-tuple-element.61), channel_id=1, source_target_pairs={{0,6},{2,4},{4,2},{6,0},{8,14},{10,12},{12,10},{14,8},{1,7},{3,5},... | collective-permute-start | bytes 393224 | tf_op jit(solution)/shard_map/ppermute | solution.py:177

commit v3 on v2

--- a/solution.py
+++ b/solution.py
@@ -10,8 +10,8 @@
 HEAD = 128
 QUAD = 4
 SPLIT = (2, 2)
-STEPS = (3, 1, 2, 0)
-GROUPS = 4
+STEPS = (2, 1, 3, 0)
+TOKEN = 0
 VMEM = pl.BlockSpec(memory_space=pltpu.VMEM)
 ANY = pl.BlockSpec(memory_space=pl.ANY)
 HBM = pl.BlockSpec(memory_space=pltpu.HBM)
@@ -47,44 +47,33 @@
 
 def forward_kernel(
     q_hbm, k_hbm, v_hbm, s_hbm, y_hbm, gain_hbm,
-    out_ref, probs_ref, stat_ref, q_ref, k_ref, v_ref, s_ref, y_ref, gain_ref, sems, gain_sem,
+    out_ref, probs_ref, stat_ref, q_ref, k_ref, v_ref, s_ref, y_ref, gain_ref, sems,
 ):
     rows, width = q_ref.shape
-    heads = width // HEAD
-    count = heads // GROUPS
-    gain_copy = pltpu.make_async_copy(gain_hbm, gain_ref, gain_sem)
-    copies = []
-    for group in range(GROUPS):
-        at = columns(group * count, count)
-        span = pl.ds(group * count, count)
-        pairs = [(q_hbm.at[:, at], q_ref.at[:, at]), (k_hbm.at[:, at], k_ref.at[:, at])]
-        pairs += [(v_hbm.at[:, at], v_ref.at[:, at]), (s_hbm.at[span], s_ref.at[span])]
-        pairs += [(y_hbm.at[:, at], y_ref.at[:, at])]
-        copies.append(
-            [
-                pltpu.make_async_copy(source, target, sems.at[group, index])
-                for index, (source, target) in enumerate(pairs)
-            ]
-        )
-    for copy in copies[0] + [gain_copy] + sum(copies[1:], []):
+    pairs = ((q_hbm, q_ref), (k_hbm, k_ref), (v_hbm, v_ref), (s_hbm, s_ref), (gain_hbm, gain_ref))
+    pairs += ((y_hbm, y_ref),)
+    copies = [
+        pltpu.make_async_copy(source, target, sems.at[index])
+        for index, (source, target) in enumerate(pairs)
+    ]
+    for copy in copies:
         copy.start()
     mask = lower(rows)
+    heads = [(head, columns(head)) for head in range(width // HEAD)]
+    for copy in copies[:2]:
+        copy.wait()
+    for head, at in heads:
+        scores = dot(q_ref[:, at], k_ref[:, at], NT)
+        probs_ref[:, at] = jnp.where(mask, scores, 0.0).astype(jnp.bfloat16)
+    for copy in copies[2:]:
+        copy.wait()
     squares = jnp.zeros((rows, HEAD), jnp.float32)
     crosses = jnp.zeros((rows, HEAD), jnp.float32)
-    for group in range(GROUPS):
-        for copy in copies[group]:
-            copy.wait()
-        if group == 0:
-            gain_copy.wait()
-        for head in range(group * count, (group + 1) * count):
-            at = columns(head)
-            q = q_ref[:, at]
-            probs = jnp.where(mask, dot(q, k_ref[:, at], NT), 0.0).astype(jnp.bfloat16)
-            probs_ref[:, at] = probs
-            out = dot(probs, v_ref[:, at], NN) + dot(q, s_ref[head], NN)
-            out_ref[:, at] = out
-            squares += out * out
-            crosses += gain_ref[:, at] * y_ref[:, at].astype(jnp.float32) * out
+    for head, at in heads:
+        out = dot(probs_ref[:, at], v_ref[:, at], NN) + dot(q_ref[:, at], s_ref[head], NN)
+        out_ref[:, at] = out
+        squares += out * out
+        crosses += gain_ref[:, at] * y_ref[:, at].astype(jnp.float32) * out
     lane = lax.broadcasted_iota(jnp.int32, (rows, HEAD), 1)
     square = jnp.sum(squares, axis=1, keepdims=True)
     cross = jnp.sum(crosses, axis=1, keepdims=True)
@@ -100,13 +89,13 @@
     inverse = lax.rsqrt(square / features + 1e-06)
     back = cross * (inverse * inverse * inverse) / features
     me = lax.rem(lax.axis_index("ctx"), QUAD)
-    for step in STEPS:
+    for index, step in enumerate(STEPS):
         for local in range(count):
             at = columns((me ^ step) * each + start + local)
             weighted = gain_ref[:, at] * y_ref[:, at].astype(jnp.float32)
             grad = (inverse * weighted - out_ref[:, at] * back).astype(jnp.bfloat16)
-            g_ref[:, columns(step * count + local)] = grad
-            u_refs[step][local] = dot(q_ref[:, at], grad, TN)
+            g_ref[:, columns(index * count + local)] = grad
+            u_refs[index][local] = dot(q_ref[:, at], grad, TN)
 
 
 def suffix_kernel(*refs):
@@ -117,11 +106,11 @@
     behind = jnp.zeros_like(blocks[0])
     for level, ref in enumerate(behind_refs):
         behind += jnp.where((place & (QUAD << level)) == 0, ref[...], 0.0)
-    for target in STEPS:
+    for target, step in enumerate(STEPS):
         value = behind
-        for source in range(QUAD):
+        for source, other in enumerate(STEPS):
             if source != target:
-                value += jnp.where((me ^ source) > (me ^ target), blocks[source], 0.0)
+                value += jnp.where((me ^ other) > (me ^ step), blocks[source], 0.0)
         sum_refs[target][...] = value
 
 
@@ -132,10 +121,10 @@
     mask = lower(q_ref.shape[0])
     me = lax.rem(lax.axis_index("ctx"), QUAD)
     for part, (start, count) in enumerate(parts):
-        for step in range(QUAD):
+        for index, step in enumerate(STEPS):
             for local in range(count):
                 head = (me ^ step) * each + start + local
-                at, slot = columns(head), columns(step * count + local)
+                at, slot = columns(head), columns(index * count + local)
                 g = g_refs[part][:, slot]
                 grads = jnp.where(mask, dot(g, v_ref[:, at], NT), 0.0).astype(jnp.bfloat16)
                 query = dot(grads, k_ref[:, at], NN) + dot(g, s_ref[head], NT)
@@ -149,19 +138,19 @@
     key_hbm, value_hbm, key_ref, value_ref, sems = refs[-5:]
     me = lax.rem(lax.axis_index("ctx"), QUAD)
     copies = []
-    for step in (0, 1, 2, 3):
-        slots = columns(step * count, count)
+    for index, step in enumerate(STEPS):
+        slots = columns(index * count, count)
         for local in range(count):
             at = columns((me ^ step) * each + start + local)
-            slot = columns(step * count + local)
-            later = later_refs[step][local].astype(jnp.bfloat16)
+            slot = columns(index * count + local)
+            later = later_refs[index][local].astype(jnp.bfloat16)
             key = key_in[:, slot] + dot(v_ref[:, at], later, NT)
             key_ref[:, slot] = key.astype(jnp.bfloat16)
             value = value_in[:, slot] + dot(k_ref[:, at], later, NN)
             value_ref[:, slot] = value.astype(jnp.bfloat16)
         at = columns((me ^ step) * each + start, count)
-        for index, (source, target) in enumerate(((key_ref, key_hbm), (value_ref, value_hbm))):
-            copy = pltpu.make_async_copy(source.at[:, slots], target.at[:, at], sems.at[step, index])
+        for pair, (source, target) in enumerate(((key_ref, key_hbm), (value_ref, value_hbm))):
+            copy = pltpu.make_async_copy(source.at[:, slots], target.at[:, at], sems.at[index, pair])
             copy.start()
             copies.append(copy)
     for copy in copies:
@@ -175,6 +164,12 @@
 def partner(value, axis, mask):
     count = lax.axis_size(axis)
     return lax.ppermute(value, axis, [(source, source ^ mask) for source in range(count)])
+
+
+def quad_swap(pieces):
+    return [
+        partner(piece, "ctx", step) if step else piece for piece, step in zip(pieces, STEPS)
+    ]
 
 
 def per_device(queries, keys, values, grad_y, state_low, gain):
@@ -204,14 +199,14 @@
         ),
         in_specs=[HBM] * 6,
         out_specs=(VMEM,) * 9,
-        scratch_shapes=[pltpu.SemaphoreType.DMA((GROUPS, 5)), pltpu.SemaphoreType.DMA],
+        scratch_shapes=[pltpu.SemaphoreType.DMA((6,))],
         compiler_params=params(8),
     )(*(pltpu.with_memory_space_constraint(value, pltpu.HBM) for value in operands))
     other = partner(stat, "tp", 1)
 
     grads, held = [], []
     for start, count in parts:
-        tokens = held[-1][1:2] if held else []
+        tokens = [held[-1][TOKEN]] if held else []
         piece = near((count, HEAD, HEAD), jnp.float32)
         grad, *own = pl.pallas_call(
             functools.partial(state_kernel, features, each, start, count),
@@ -221,8 +216,7 @@
             compiler_params=params(8),
         )(stat, other, out, y, gain_v, q, *tokens)
         grads.append(grad)
-        came = {step: partner(own[step], "ctx", step) for step in (3, 1, 2)}
-        held.append([own[0], came[1], came[2], came[3]])
+        held.append(quad_swap(own))
     later = []
     for blocks in held:
         total = blocks[0] + blocks[1] + blocks[2] + blocks[3]
@@ -241,8 +235,7 @@
             out_specs=(VMEM,) * QUAD,
             compiler_params=params(8),
         )(*blocks, *behind)
-        came = {step: partner(sums[step], "ctx", step) for step in (3, 1, 2)}
-        later.append([sums[0], came[1], came[2], came[3]])
+        later.append(quad_swap(sums))
 
     slots = [near((rows, QUAD * count * HEAD), jnp.float32) for _, count in parts]
     grad_query, *local = pl.pallas_call(

time: 44.1 us -> 42 us (0.952)
  Pallas kernels: 10.2 us -> 9.08 us
  starting transfers between devices: 21.8 us -> 21.1 us
    pallas_call x1, Pallas kernels: 3.44 us -> 2.32 us  [per_device(): pl.pallas_call(forward_kernel, out_shape=(near((rows, width), jnp.float32...]
    ppermute x15, starting transfers between devices: 21.8 us -> 21.1 us  [partner(): lax.ppermute(value, axis, [(source, source ^ mask) for source in range(co...]
  transfers between devices with their start and end apart: 15 -> 15, of which waited for: 8 -> 9; matrix products, arithmetic and copies ran while one was open for 0% -> 0% of each run, Pallas kernels for 12% -> 12%
where the time goes in v3:
time: 42 us; the launch traced here: 41.8 us
  starting transfers between devices  21.1 us (50%)
  waiting for transfers between devices  10.9 us (26%)
  Pallas kernels  9.08 us (22%)
  between operations  0.7 us (2%)
    ppermute x15, starting transfers between devices, partner(): lax.ppermute(value, axis, [(source, source ^ mask) for source in range(co...  21.1 us
    ppermute x15, waiting for transfers between devices, partner(): lax.ppermute(value, axis, [(source, source ^ mask) for source in range(co...  10.9 us
    pallas_call x1, Pallas kernels, per_device(): pl.pallas_call(functools.partial(local_kernel, each, parts), out_shape=(h...  3.39 us
    pallas_call x1, Pallas kernels, per_device(): pl.pallas_call(forward_kernel, out_shape=(near((rows, width), jnp.float32...  2.32 us
    pallas_call x2, Pallas kernels, per_device(): pl.pallas_call(functools.partial(final_kernel, each, start, count), out_s...  2.19 us
    pallas_call x2, Pallas kernels, per_device(): pl.pallas_call(functools.partial(state_kernel, features, each, start, cou...  0.9 us
  transfers between devices with their start and end apart: 15, of which 9 were waited for; matrix products, arithmetic and copies ran while one was open for 0% of the time, Pallas kernels for 12%

profile of v3, /device:TPU:0, one launch (start us, length us, event | category | flops | bytes accessed | tf_op | source)
XLA Modules:
  0.0 41.8 jit_solution(5849437616512104389)
XLA Ops:
  0.6 2.3 %shard_map.85 = (f32[128,2048]{1,0:T(8,128)S(1)}, bf16[128,2048]{1,0:T(8,128)(2,1)S(1)}, f32[128,128]{1,0:T(8,128)S(1)}, bf16[128,2048]{1,0:T(8,128)(2,1)S(1)}, ...) custom-call(bf16[128,2048]{1,0:T(8,128)(2,1)} %q_hbm.1, ...), custom_call_target="tpu_custom_call" | custom-call | tf_op jit(solution)/shard_map/pallas_call | solution.py:187
  3.0 0.5 %collective-permute-start = (f32[128,128]{1,0:T(8,128)S(1)}, f32[128,128]{1,0:T(8,128)S(1)}, u32[]{:S(2)}, u32[]{:S(2)}) collective-permute-start(f32[128,128]{1,0:T(8,128)S(1)} %get-tuple-element.44.own_ref), channel_id=1, source_target_pairs={{0,1},{1,0},{2,3},{3,2},{4,5},{5,4},{6,7},{7,6},{8,9},{9,8},{10,11... | collective-permute-start | bytes 196616 | tf_op jit(solution)/shard_map/ppermute | solution.py:166
  3.5 0.9 %collective-permute-done.other_ref = f32[128,128]{1,0:T(8,128)S(1)} collective-permute-done((f32[128,128]{1,0:T(8,128)S(1)}, f32[128,128]{1,0:T(8,128)S(1)}, u32[]{:S(2)}, u32[]{:S(2)}) %collective-permute-start) | collective-permute-done | bytes 65568 | tf_op jit(solution)/shard_map/ppermute | solution.py:166
  4.4 0.4 %shard_map.86 = (bf16[128,1024]{1,0:T(8,128)(2,1)S(1)}, f32[2,128,128]{2,1,0:T(8,128)S(1)}, f32[2,128,128]{2,1,0:T(8,128)S(1)}, f32[2,128,128]{2,1,0:T(8,128)S(1)}, f32[2,128,128]{2,1,0:T(8,128)S(1)}) custom-call(f32[128,128]{1,0:T(8,128)S(1)} %get-tuple-element.44.own_ref, f32[128,128]{1,0:T(8,128)S(1)} %collective-permute-done.other_ref, ...), custom_call_target="tpu_custom_call" | custom-call | tf_op jit(solution)/shard_map/pallas_call | solution.py:211
  4.8 3.0 %collective-permute-start.1 = (f32[2,128,128]{2,1,0:T(8,128)S(1)}, f32[2,128,128]{2,1,0:T(8,128)S(1)}, u32[]{:S(2)}, u32[]{:S(2)}) collective-permute-start(f32[2,128,128]{2,1,0:T(8,128)S(1)} %get-tuple-element.49), channel_id=1, source_target_pairs={{0,4},{2,6},{4,0},{6,2},{8,12},{10,14},{12,8},{14,10},{1,5},{3,7},... | collective-permute-start | bytes 393224 | tf_op jit(solution)/shard_map/ppermute | solution.py:166
  7.8 1.5 %collective-permute-start.9 = (f32[2,128,128]{2,1,0:T(8,128)S(1)}, f32[2,128,128]{2,1,0:T(8,128)S(1)}, u32[]{:S(2)}, u32[]{:S(2)}) collective-permute-start(f32[2,128,128]{2,1,0:T(8,128)S(1)} %get-tuple-element.64), channel_id=1, source_target_pairs={{0,2},{2,0},{4,6},{6,4},{8,10},{10,8},{12,14},{14,12},{1,3},{3,1},... | collective-permute-start | bytes 393224 | tf_op jit(solution)/shard_map/ppermute | solution.py:166
  9.3 0.0 collective-permute-start.10
  9.4 2.4 %collective-permute-done.1.refs_0_ = f32[2,128,128]{2,1,0:T(8,128)S(1)} collective-permute-done((f32[2,128,128]{2,1,0:T(8,128)S(1)}, f32[2,128,128]{2,1,0:T(8,128)S(1)}, u32[]{:S(2)}, u32[]{:S(2)}) %collective-permute-start.1) | collective-permute-done | bytes 131104 | tf_op jit(solution)/shard_map/ppermute | solution.py:166
  11.7 0.5 %shard_map.87 = (bf16[128,1024]{1,0:T(8,128)(2,1)S(1)}, f32[2,128,128]{2,1,0:T(8,128)S(1)}, f32[2,128,128]{2,1,0:T(8,128)S(1)}, f32[2,128,128]{2,1,0:T(8,128)S(1)}, f32[2,128,128]{2,1,0:T(8,128)S(1)}) custom-call(f32[128,128]{1,0:T(8,128)S(1)} %get-tuple-element.44.own_ref, f32[128,128]{1,0:T(8,128)S(1)} %collective-permute-done.other_ref, ...), custom_call_target="tpu_custom_call" | custom-call | tf_op jit(solution)/shard_map/pallas_call | solution.py:211
  12.2 2.5 %collective-permute-start.2 = (f32[2,128,128]{2,1,0:T(8,128)S(1)}, f32[2,128,128]{2,1,0:T(8,128)S(1)}, u32[]{:S(2)}, u32[]{:S(2)}) collective-permute-start(f32[2,128,128]{2,1,0:T(8,128)S(1)} %get-tuple-element.54), channel_id=1, source_target_pairs={{0,4},{2,6},{4,0},{6,2},{8,12},{10,14},{12,8},{14,10},{1,5},{3,7},... | collective-permute-start | bytes 393224 | tf_op jit(solution)/shard_map/ppermute | solution.py:166
  14.7 1.5 %collective-permute-start.3 = (f32[2,128,128]{2,1,0:T(8,128)S(1)}, f32[2,128,128]{2,1,0:T(8,128)S(1)}, u32[]{:S(2)}, u32[]{:S(2)}) collective-permute-start(f32[2,128,128]{2,1,0:T(8,128)S(1)} %get-tuple-element.55), channel_id=1, source_target_pairs={{0,2},{2,0},{4,6},{6,4},{8,10},{10,8},{12,14},{14,12},{1,3},{3,1},... | collective-permute-start | bytes 393224 | tf_op jit(solution)/shard_map/ppermute | solution.py:166
  16.2 0.0 collective-permute-start.4
  16.2 0.0 collective-permute-done.9.refs_1_
  16.2 0.0 collective-permute-done.10.refs_2_
  16.3 2.6 %collective-permute-start.11 = (f32[2,128,128]{2,1,0:T(8,128)S(1)}, f32[2,128,128]{2,1,0:T(8,128)S(1)}, u32[]{:S(2)}, u32[]{:S(2)}) collective-permute-start(f32[2,128,128]{2,1,0:T(8,128)S(1)} %add_add_fusion), channel_id=1, source_target_pairs={{0,8},{2,10},{4,12},{6,14},{8,0},{10,2},{12,4},{14,6},{1,9},{3,11}... | collective-permute-start | bytes 393224 | tf_op jit(solution)/shard_map/ppermute | solution.py:166
  18.9 1.1 %collective-permute-done.2.refs_0_ = f32[2,128,128]{2,1,0:T(8,128)S(1)} collective-permute-done((f32[2,128,128]{2,1,0:T(8,128)S(1)}, f32[2,128,128]{2,1,0:T(8,128)S(1)}, u32[]{:S(2)}, u32[]{:S(2)}) %collective-permute-start.2) | collective-permute-done | bytes 131104 | tf_op jit(solution)/shard_map/ppermute | solution.py:166
  20.0 0.3 collective-permute-done.3.refs_1_
  20.3 3.1 %collective-permute-done.4.refs_2_ = f32[2,128,128]{2,1,0:T(8,128)S(1)} collective-permute-done((f32[2,128,128]{2,1,0:T(8,128)S(1)}, f32[2,128,128]{2,1,0:T(8,128)S(1)}, u32[]{:S(2)}, u32[]{:S(2)}) %collective-permute-start.4) | collective-permute-done | bytes 131104 | tf_op jit(solution)/shard_map/ppermute | solution.py:166
  23.4 2.3 %collective-permute-start.5 = (f32[2,128,128]{2,1,0:T(8,128)S(1)}, f32[2,128,128]{2,1,0:T(8,128)S(1)}, u32[]{:S(2)}, u32[]{:S(2)}) collective-permute-start(f32[2,128,128]{2,1,0:T(8,128)S(1)} %add_add_fusion.1), channel_id=1, source_target_pairs={{0,8},{2,10},{4,12},{6,14},{8,0},{10,2},{12,4},{14,6},{1,9},{3,11}... | collective-permute-start | bytes 393224 | tf_op jit(solution)/shard_map/ppermute | solution.py:166
  25.7 0.0 collective-permute-done.11.refs_4_
  25.7 0.1 shard_map.90
  25.9 1.5 %collective-permute-start.12 = (f32[2,128,128]{2,1,0:T(8,128)S(1)}, f32[2,128,128]{2,1,0:T(8,128)S(1)}, u32[]{:S(2)}, u32[]{:S(2)}) collective-permute-start(f32[2,128,128]{2,1,0:T(8,128)S(1)} %get-tuple-element.67), channel_id=1, source_target_pairs={{0,4},{2,6},{4,0},{6,2},{8,12},{10,14},{12,8},{14,10},{1,5},{3,7},... | collective-permute-start | bytes 393224 | tf_op jit(solution)/shard_map/ppermute | solution.py:166
  27.4 1.9 %collective-permute-start.13 = (f32[2,128,128]{2,1,0:T(8,128)S(1)}, f32[2,128,128]{2,1,0:T(8,128)S(1)}, u32[]{:S(2)}, u32[]{:S(2)}) collective-permute-start(f32[2,128,128]{2,1,0:T(8,128)S(1)} %get-tuple-element.68), channel_id=1, source_target_pairs={{0,2},{2,0},{4,6},{6,4},{8,10},{10,8},{12,14},{14,12},{1,3},{3,1},... | collective-permute-start | bytes 393224 | tf_op jit(solution)/shard_map/ppermute | solution.py:166
  29.2 0.2 collective-permute-start.14
  29.4 1.4 %collective-permute-done.5.refs_4_ = f32[2,128,128]{2,1,0:T(8,128)S(1)} collective-permute-done((f32[2,128,128]{2,1,0:T(8,128)S(1)}, f32[2,128,128]{2,1,0:T(8,128)S(1)}, u32[]{:S(2)}, u32[]{:S(2)}) %collective-permute-start.5) | collective-permute-done | bytes 131104 | tf_op jit(solution)/shard_map/ppermute | solution.py:166
  30.9 0.1 shard_map.89
  31.0 0.7 %collective-permute-start.6 = (f32[2,128,128]{2,1,0:T(8,128)S(1)}, f32[2,128,128]{2,1,0:T(8,128)S(1)}, u32[]{:S(2)}, u32[]{:S(2)}) collective-permute-start(f32[2,128,128]{2,1,0:T(8,128)S(1)} %get-tuple-element.58), channel_id=1, source_target_pairs={{0,4},{2,6},{4,0},{6,2},{8,12},{10,14},{12,8},{14,10},{1,5},{3,7},... | collective-permute-start | bytes 393224 | tf_op jit(solution)/shard_map/ppermute | solution.py:166
  31.7 1.3 %collective-permute-start.7 = (f32[2,128,128]{2,1,0:T(8,128)S(1)}, f32[2,128,128]{2,1,0:T(8,128)S(1)}, u32[]{:S(2)}, u32[]{:S(2)}) collective-permute-start(f32[2,128,128]{2,1,0:T(8,128)S(1)} %get-tuple-element.59), channel_id=1, source_target_pairs={{0,2},{2,0},{4,6},{6,4},{8,10},{10,8},{12,14},{14,12},{1,3},{3,1},... | collective-permute-start | bytes 393224 | tf_op jit(solution)/shard_map/ppermute | solution.py:166
  32.9 0.1 collective-permute-done.12.refs_0_
  33.1 1.5 %collective-permute-start.8 = (f32[2,128,128]{2,1,0:T(8,128)S(1)}, f32[2,128,128]{2,1,0:T(8,128)S(1)}, u32[]{:S(2)}, u32[]{:S(2)}) collective-permute-start(f32[2,128,128]{2,1,0:T(8,128)S(1)} %get-tuple-element.60), channel_id=1, source_target_pairs={{0,6},{2,4},{4,2},{6,0},{8,14},{10,12},{12,10},{14,8},{1,7},{3,5},... | collective-permute-start | bytes 393224 | tf_op jit(solution)/shard_map/ppermute | solution.py:166
  34.6 3.4 %shard_map.88 = (bf16[128,2048]{1,0:T(8,128)(2,1)}, f32[128,1024]{1,0:T(8,128)S(1)}, f32[128,1024]{1,0:T(8,128)S(1)}, f32[128,1024]{1,0:T(8,128)S(1)}, f32[128,1024]{1,0:T(8,128)S(1)}) custom-call(bf16[128,2048]{1,0:T(8,128)(2,1)S(1)} %get-tuple-element.39.q_ref, bf16[128,2048]{1,0:T(8,128)(2,1)S(1)} %get-tuple-element.40.k_ref, ...), custom_call_target="tpu_custom_call" | custom-call | tf_op jit(solution)/shard_map/pallas_call | solution.py:241
  38.0 0.0 collective-permute-done.13.refs_1_
  38.0 0.0 collective-permute-done.14.refs_2_
  38.0 1.1 %shard_map.91 = (bf16[128,2048]{1,0:T(8,128)(2,1)}, bf16[128,2048]{1,0:T(8,128)(2,1)}) custom-call(bf16[128,2048]{1,0:T(8,128)(2,1)S(1)} %get-tuple-element.40.k_ref, bf16[128,2048]{1,0:T(8,128)(2,1)S(1)} %get-tuple-element.41.v_ref, f32[128,1024]{1,0:T(8,128)S(1)} %get-tuple-element.62.key_in, f32[128,1024]{1,0:T(8,128)S(1)} %get-tuple-element.63.value_in, ...), custom_call_target="tpu_custom_call" | custom-call | tf_op jit(solution)/shard_map/pallas_call | solution.py:251
  39.1 0.0 collective-permute-done.6.refs_0_
  39.1 0.3 collective-permute-done.7.refs_1_
  39.4 1.4 %collective-permute-done.8.refs_2_ = f32[2,128,128]{2,1,0:T(8,128)S(1)} collective-permute-done((f32[2,128,128]{2,1,0:T(8,128)S(1)}, f32[2,128,128]{2,1,0:T(8,128)S(1)}, u32[]{:S(2)}, u32[]{:S(2)}) %collective-permute-start.8) | collective-permute-done | bytes 131104 | tf_op jit(solution)/shard_map/ppermute | solution.py:166
  40.7 1.1 %shard_map.92 = (bf16[128,2048]{1,0:T(8,128)(2,1)}, bf16[128,2048]{1,0:T(8,128)(2,1)}) custom-call(bf16[128,2048]{1,0:T(8,128)(2,1)S(1)} %get-tuple-element.40.k_ref, bf16[128,2048]{1,0:T(8,128)(2,1)S(1)} %get-tuple-element.41.v_ref, f32[128,1024]{1,0:T(8,128)S(1)} %get-tuple-element.52.key_in, ...), custom_call_target="tpu_custom_call", output_to_operand_aliasing={{0}: (8, {}), {1}: (9, {})} | custom-call | tf_op jit(solution)/shard_map/pallas_call | solution.py:251
  (2 shorter events, 0.1 us)
Async XLA Ops:
  3.0 1.4 %collective-permute-start = (f32[128,128]{1,0:T(8,128)S(1)}, f32[128,128]{1,0:T(8,128)S(1)}, u32[]{:S(2)}, u32[]{:S(2)}) collective-permute-start(f32[128,128]{1,0:T(8,128)S(1)} %get-tuple-element.44.own_ref), channel_id=1, source_target_pairs={{0,1},{1,0},{2,3},{3,2},{4,5},{5,4},{6,7},{7,6},{8,9},{9,8},{10,11... | collective-permute-start | bytes 196616 | tf_op jit(solution)/shard_map/ppermute | solution.py:166
  4.8 6.9 %collective-permute-start.1 = (f32[2,128,128]{2,1,0:T(8,128)S(1)}, f32[2,128,128]{2,1,0:T(8,128)S(1)}, u32[]{:S(2)}, u32[]{:S(2)}) collective-permute-start(f32[2,128,128]{2,1,0:T(8,128)S(1)} %get-tuple-element.49), channel_id=1, source_target_pairs={{0,4},{2,6},{4,0},{6,2},{8,12},{10,14},{12,8},{14,10},{1,5},{3,7},... | collective-permute-start | bytes 393224 | tf_op jit(solution)/shard_map/ppermute | solution.py:166
  7.8 8.4 %collective-permute-start.9 = (f32[2,128,128]{2,1,0:T(8,128)S(1)}, f32[2,128,128]{2,1,0:T(8,128)S(1)}, u32[]{:S(2)}, u32[]{:S(2)}) collective-permute-start(f32[2,128,128]{2,1,0:T(8,128)S(1)} %get-tuple-element.64), channel_id=1, source_target_pairs={{0,2},{2,0},{4,6},{6,4},{8,10},{10,8},{12,14},{14,12},{1,3},{3,1},... | collective-permute-start | bytes 393224 | tf_op jit(solution)/shard_map/ppermute | solution.py:166
  9.3 6.9 %collective-permute-start.10 = (f32[2,128,128]{2,1,0:T(8,128)S(1)}, f32[2,128,128]{2,1,0:T(8,128)S(1)}, u32[]{:S(2)}, u32[]{:S(2)}) collective-permute-start(f32[2,128,128]{2,1,0:T(8,128)S(1)} %get-tuple-element.65), channel_id=1, source_target_pairs={{0,6},{2,4},{4,2},{6,0},{8,14},{10,12},{12,10},{14,8},{1,7},{3,5},... | collective-permute-start | bytes 393224 | tf_op jit(solution)/shard_map/ppermute | solution.py:166
  12.2 7.8 %collective-permute-start.2 = (f32[2,128,128]{2,1,0:T(8,128)S(1)}, f32[2,128,128]{2,1,0:T(8,128)S(1)}, u32[]{:S(2)}, u32[]{:S(2)}) collective-permute-start(f32[2,128,128]{2,1,0:T(8,128)S(1)} %get-tuple-element.54), channel_id=1, source_target_pairs={{0,4},{2,6},{4,0},{6,2},{8,12},{10,14},{12,8},{14,10},{1,5},{3,7},... | collective-permute-start | bytes 393224 | tf_op jit(solution)/shard_map/ppermute | solution.py:166
  14.7 5.6 %collective-permute-start.3 = (f32[2,128,128]{2,1,0:T(8,128)S(1)}, f32[2,128,128]{2,1,0:T(8,128)S(1)}, u32[]{:S(2)}, u32[]{:S(2)}) collective-permute-start(f32[2,128,128]{2,1,0:T(8,128)S(1)} %get-tuple-element.55), channel_id=1, source_target_pairs={{0,2},{2,0},{4,6},{6,4},{8,10},{10,8},{12,14},{14,12},{1,3},{3,1},... | collective-permute-start | bytes 393224 | tf_op jit(solution)/shard_map/ppermute | solution.py:166
  16.2 7.2 %collective-permute-start.4 = (f32[2,128,128]{2,1,0:T(8,128)S(1)}, f32[2,128,128]{2,1,0:T(8,128)S(1)}, u32[]{:S(2)}, u32[]{:S(2)}) collective-permute-start(f32[2,128,128]{2,1,0:T(8,128)S(1)} %get-tuple-element.56), channel_id=1, source_target_pairs={{0,6},{2,4},{4,2},{6,0},{8,14},{10,12},{12,10},{14,8},{1,7},{3,5},... | collective-permute-start | bytes 393224 | tf_op jit(solution)/shard_map/ppermute | solution.py:166
  16.3 9.5 %collective-permute-start.11 = (f32[2,128,128]{2,1,0:T(8,128)S(1)}, f32[2,128,128]{2,1,0:T(8,128)S(1)}, u32[]{:S(2)}, u32[]{:S(2)}) collective-permute-start(f32[2,128,128]{2,1,0:T(8,128)S(1)} %add_add_fusion), channel_id=1, source_target_pairs={{0,8},{2,10},{4,12},{6,14},{8,0},{10,2},{12,4},{14,6},{1,9},{3,11}... | collective-permute-start | bytes 393224 | tf_op jit(solution)/shard_map/ppermute | solution.py:166
  23.4 7.5 %collective-permute-start.5 = (f32[2,128,128]{2,1,0:T(8,128)S(1)}, f32[2,128,128]{2,1,0:T(8,128)S(1)}, u32[]{:S(2)}, u32[]{:S(2)}) collective-permute-start(f32[2,128,128]{2,1,0:T(8,128)S(1)} %add_add_fusion.1), channel_id=1, source_target_pairs={{0,8},{2,10},{4,12},{6,14},{8,0},{10,2},{12,4},{14,6},{1,9},{3,11}... | collective-permute-start | bytes 393224 | tf_op jit(solution)/shard_map/ppermute | solution.py:166
  25.9 7.2 %collective-permute-start.12 = (f32[2,128,128]{2,1,0:T(8,128)S(1)}, f32[2,128,128]{2,1,0:T(8,128)S(1)}, u32[]{:S(2)}, u32[]{:S(2)}) collective-permute-start(f32[2,128,128]{2,1,0:T(8,128)S(1)} %get-tuple-element.67), channel_id=1, source_target_pairs={{0,4},{2,6},{4,0},{6,2},{8,12},{10,14},{12,8},{14,10},{1,5},{3,7},... | collective-permute-start | bytes 393224 | tf_op jit(solution)/shard_map/ppermute | solution.py:166
  27.4 10.6 %collective-permute-start.13 = (f32[2,128,128]{2,1,0:T(8,128)S(1)}, f32[2,128,128]{2,1,0:T(8,128)S(1)}, u32[]{:S(2)}, u32[]{:S(2)}) collective-permute-start(f32[2,128,128]{2,1,0:T(8,128)S(1)} %get-tuple-element.68), channel_id=1, source_target_pairs={{0,2},{2,0},{4,6},{6,4},{8,10},{10,8},{12,14},{14,12},{1,3},{3,1},... | collective-permute-start | bytes 393224 | tf_op jit(solution)/shard_map/ppermute | solution.py:166
  29.2 8.7 %collective-permute-start.14 = (f32[2,128,128]{2,1,0:T(8,128)S(1)}, f32[2,128,128]{2,1,0:T(8,128)S(1)}, u32[]{:S(2)}, u32[]{:S(2)}) collective-permute-start(f32[2,128,128]{2,1,0:T(8,128)S(1)} %get-tuple-element.69), channel_id=1, source_target_pairs={{0,6},{2,4},{4,2},{6,0},{8,14},{10,12},{12,10},{14,8},{1,7},{3,5},... | collective-permute-start | bytes 393224 | tf_op jit(solution)/shard_map/ppermute | solution.py:166
  31.0 8.1 %collective-permute-start.6 = (f32[2,128,128]{2,1,0:T(8,128)S(1)}, f32[2,128,128]{2,1,0:T(8,128)S(1)}, u32[]{:S(2)}, u32[]{:S(2)}) collective-permute-start(f32[2,128,128]{2,1,0:T(8,128)S(1)} %get-tuple-element.58), channel_id=1, source_target_pairs={{0,4},{2,6},{4,0},{6,2},{8,12},{10,14},{12,8},{14,10},{1,5},{3,7},... | collective-permute-start | bytes 393224 | tf_op jit(solution)/shard_map/ppermute | solution.py:166
  31.7 7.7 %collective-permute-start.7 = (f32[2,128,128]{2,1,0:T(8,128)S(1)}, f32[2,128,128]{2,1,0:T(8,128)S(1)}, u32[]{:S(2)}, u32[]{:S(2)}) collective-permute-start(f32[2,128,128]{2,1,0:T(8,128)S(1)} %get-tuple-element.59), channel_id=1, source_target_pairs={{0,2},{2,0},{4,6},{6,4},{8,10},{10,8},{12,14},{14,12},{1,3},{3,1},... | collective-permute-start | bytes 393224 | tf_op jit(solution)/shard_map/ppermute | solution.py:166
  33.1 7.7 %collective-permute-start.8 = (f32[2,128,128]{2,1,0:T(8,128)S(1)}, f32[2,128,128]{2,1,0:T(8,128)S(1)}, u32[]{:S(2)}, u32[]{:S(2)}) collective-permute-start(f32[2,128,128]{2,1,0:T(8,128)S(1)} %get-tuple-element.60), channel_id=1, source_target_pairs={{0,6},{2,4},{4,2},{6,0},{8,14},{10,12},{12,10},{14,8},{1,7},{3,5},... | collective-permute-start | bytes 393224 | tf_op jit(solution)/shard_map/ppermute | solution.py:166

commit v4 on v3

--- a/solution.py
+++ b/solution.py
@@ -11,7 +11,11 @@
 QUAD = 4
 SPLIT = (2, 2)
 STEPS = (2, 1, 3, 0)
-TOKEN = 0
+FINALS = ((0, (2, 1, 3, 0)), (1, (0, 2, 1)), (1, (3,)))
+CALLS = (
+    (((0, 1), (0, 2), (0, 3), (0, 0)), None),
+    (((1, 3), (1, 2), (1, 1), (1, 0)), (0, 2)),
+)
 VMEM = pl.BlockSpec(memory_space=pltpu.VMEM)
 ANY = pl.BlockSpec(memory_space=pl.ANY)
 HBM = pl.BlockSpec(memory_space=pltpu.HBM)
@@ -80,22 +84,23 @@
     stat_ref[...] = jnp.where(lane == 0, square, cross)
 
 
-def state_kernel(
-    features, each, start, count, own_ref, other_ref, out_ref, y_ref, gain_ref, q_ref, *refs
-):
-    g_ref, *u_refs = refs[-1 - QUAD :]
+def state_kernel(features, each, parts, pieces, own_ref, other_ref, out_ref, y_ref, gain_ref, q_ref, *refs):
+    g_ref, *u_refs = refs[-1 - len(pieces) :]
     stat = own_ref[...] + other_ref[...]
     square, cross = stat[:, 0:1], stat[:, 1:2]
     inverse = lax.rsqrt(square / features + 1e-06)
     back = cross * (inverse * inverse * inverse) / features
     me = lax.rem(lax.axis_index("ctx"), QUAD)
-    for index, step in enumerate(STEPS):
+    slot = 0
+    for (part, step), u_ref in zip(pieces, u_refs):
+        start, count = parts[part]
         for local in range(count):
             at = columns((me ^ step) * each + start + local)
             weighted = gain_ref[:, at] * y_ref[:, at].astype(jnp.float32)
             grad = (inverse * weighted - out_ref[:, at] * back).astype(jnp.bfloat16)
-            g_ref[:, columns(index * count + local)] = grad
-            u_refs[index][local] = dot(q_ref[:, at], grad, TN)
+            g_ref[:, columns(slot)] = grad
+            slot += 1
+            u_ref[local] = dot(q_ref[:, at], grad, TN)
 
 
 def suffix_kernel(*refs):
@@ -115,17 +120,20 @@
 
 
 def local_kernel(each, parts, q_ref, k_ref, v_ref, s_ref, probs_ref, *refs):
-    g_refs, query_ref = refs[: len(parts)], refs[len(parts)]
-    key_refs = refs[len(parts) + 1 : 2 * len(parts) + 1]
-    value_refs = refs[2 * len(parts) + 1 :]
+    g_refs, query_ref = refs[: len(CALLS)], refs[len(CALLS)]
+    key_refs = refs[len(CALLS) + 1 : len(CALLS) + 1 + len(parts)]
+    value_refs = refs[len(CALLS) + 1 + len(parts) :]
     mask = lower(q_ref.shape[0])
     me = lax.rem(lax.axis_index("ctx"), QUAD)
-    for part, (start, count) in enumerate(parts):
-        for index, step in enumerate(STEPS):
+    for (pieces, _), g_ref in zip(CALLS, g_refs):
+        place = 0
+        for part, step in pieces:
+            start, count = parts[part]
             for local in range(count):
                 head = (me ^ step) * each + start + local
-                at, slot = columns(head), columns(index * count + local)
-                g = g_refs[part][:, slot]
+                at, slot = columns(head), columns(STEPS.index(step) * count + local)
+                g = g_ref[:, columns(place)]
+                place += 1
                 grads = jnp.where(mask, dot(g, v_ref[:, at], NT), 0.0).astype(jnp.bfloat16)
                 query = dot(grads, k_ref[:, at], NN) + dot(g, s_ref[head], NT)
                 query_ref[:, at] = query.astype(jnp.bfloat16)
@@ -133,21 +141,22 @@
                 value_refs[part][:, slot] = dot(probs_ref[:, at], g, TN)
 
 
-def final_kernel(each, start, count, k_ref, v_ref, key_in, value_in, *refs):
-    later_refs = refs[:QUAD]
+def final_kernel(each, start, count, steps, k_ref, v_ref, key_in, value_in, *refs):
+    later_refs = refs[: len(steps)]
     key_hbm, value_hbm, key_ref, value_ref, sems = refs[-5:]
     me = lax.rem(lax.axis_index("ctx"), QUAD)
     copies = []
-    for index, step in enumerate(STEPS):
-        slots = columns(index * count, count)
+    for index, step in enumerate(steps):
         for local in range(count):
             at = columns((me ^ step) * each + start + local)
+            source = columns(STEPS.index(step) * count + local)
             slot = columns(index * count + local)
             later = later_refs[index][local].astype(jnp.bfloat16)
-            key = key_in[:, slot] + dot(v_ref[:, at], later, NT)
+            key = key_in[:, source] + dot(v_ref[:, at], later, NT)
             key_ref[:, slot] = key.astype(jnp.bfloat16)
-            value = value_in[:, slot] + dot(k_ref[:, at], later, NN)
+            value = value_in[:, source] + dot(k_ref[:, at], later, NN)
             value_ref[:, slot] = value.astype(jnp.bfloat16)
+        slots = columns(index * count, count)
         at = columns((me ^ step) * each + start, count)
         for pair, (source, target) in enumerate(((key_ref, key_hbm), (value_ref, value_hbm))):
             copy = pltpu.make_async_copy(source.at[:, slots], target.at[:, at], sems.at[index, pair])
@@ -204,19 +213,22 @@
     )(*(pltpu.with_memory_space_constraint(value, pltpu.HBM) for value in operands))
     other = partner(stat, "tp", 1)
 
-    grads, held = [], []
-    for start, count in parts:
-        tokens = [held[-1][TOKEN]] if held else []
-        piece = near((count, HEAD, HEAD), jnp.float32)
+    grads, found = [], {}
+    for pieces, token in CALLS:
+        tokens = [found[token]] if token else []
+        shapes = [near((parts[part][1], HEAD, HEAD), jnp.float32) for part, _ in pieces]
+        wide = sum(shape.shape[0] for shape in shapes) * HEAD
         grad, *own = pl.pallas_call(
-            functools.partial(state_kernel, features, each, start, count),
-            out_shape=(near((rows, QUAD * count * HEAD), jnp.bfloat16),) + (piece,) * QUAD,
+            functools.partial(state_kernel, features, each, parts, pieces),
+            out_shape=(near((rows, wide), jnp.bfloat16), *shapes),
             in_specs=[VMEM] * 6 + [ANY] * len(tokens),
-            out_specs=(VMEM,) * (1 + QUAD),
+            out_specs=(VMEM,) * (1 + len(pieces)),
             compiler_params=params(8),
         )(stat, other, out, y, gain_v, q, *tokens)
         grads.append(grad)
-        held.append(quad_swap(own))
+        for (part, step), piece in zip(pieces, own):
+            found[part, step] = partner(piece, "ctx", step) if step else piece
+    held = [[found[part, step] for step in STEPS] for part in range(len(parts))]
     later = []
     for blocks in held:
         total = blocks[0] + blocks[1] + blocks[2] + blocks[3]
@@ -241,22 +253,24 @@
     grad_query, *local = pl.pallas_call(
         functools.partial(local_kernel, each, parts),
         out_shape=(half, *slots, *slots),
-        in_specs=[VMEM] * (5 + len(parts)),
+        in_specs=[VMEM] * (5 + len(grads)),
         out_specs=(VMEM,) * (1 + 2 * len(parts)),
         compiler_params=params(8),
     )(q, k, v, s, probs, *grads)
     done = ()
-    for part, (start, count) in enumerate(parts):
-        stage = pltpu.VMEM((rows, QUAD * count * HEAD), jnp.bfloat16)
+    for part, steps in FINALS:
+        start, count = parts[part]
+        stage = pltpu.VMEM((rows, len(steps) * count * HEAD), jnp.bfloat16)
+        pieces = [later[part][STEPS.index(step)] for step in steps]
         done = pl.pallas_call(
-            functools.partial(final_kernel, each, start, count),
+            functools.partial(final_kernel, each, start, count, steps),
             out_shape=(half, half),
-            in_specs=[VMEM] * (4 + QUAD) + [HBM] * len(done),
+            in_specs=[VMEM] * (4 + len(steps)) + [HBM] * len(done),
             out_specs=(HBM,) * 2,
             scratch_shapes=[stage, stage, pltpu.SemaphoreType.DMA((QUAD, 2))],
-            input_output_aliases={4 + QUAD + index: index for index in range(len(done))},
+            input_output_aliases={4 + len(steps) + index: index for index in range(len(done))},
             compiler_params=params(8),
-        )(k, v, local[part], local[len(parts) + part], *later[part], *done)
+        )(k, v, local[part], local[len(parts) + part], *pieces, *done)
     return (grad_query, *done)
 
 

time: 42 us -> 41.8 us (level)
  waiting for transfers between devices: 10.9 us -> 9.88 us
  Pallas kernels: 9.08 us -> 9.92 us
    ppermute x15, waiting for transfers between devices: 10.9 us -> 9.88 us  [partner(): lax.ppermute(value, axis, [(source, source ^ mask) for source in range(co...]
    pallas_call x4 -> x5, Pallas kernels: 3.09 us -> 3.93 us  [the longest x3 3.03 us: per_device(): pl.pallas_call(functools.partial(final_kernel, each, start, count, steps)...]
  transfers between devices with their start and end apart: 15 -> 15, of which waited for: 9 -> 9; matrix products, arithmetic and copies ran while one was open for 0% -> 0% of each run, Pallas kernels for 12% -> 15%
where the time goes in v4:
time: 41.8 us; the launch traced here: 41.6 us
  starting transfers between devices  21.1 us (50%)
  Pallas kernels  9.92 us (24%)
  waiting for transfers between devices  9.88 us (24%)
  between operations  0.7 us (2%)
    ppermute x15, starting transfers between devices, partner(): lax.ppermute(value, axis, [(source, source ^ mask) for source in range(co...  21.1 us
    ppermute x15, waiting for transfers between devices, partner(): lax.ppermute(value, axis, [(source, source ^ mask) for source in range(co...  9.88 us
    pallas_call x1, Pallas kernels, per_device(): pl.pallas_call(functools.partial(local_kernel, each, parts), out_shape=(h...  3.4 us
    pallas_call x3, Pallas kernels, per_device(): pl.pallas_call(functools.partial(final_kernel, each, start, count, steps)...  3.03 us
    pallas_call x1, Pallas kernels, per_device(): pl.pallas_call(forward_kernel, out_shape=(near((rows, width), jnp.float32...  2.32 us
    pallas_call x2, Pallas kernels, per_device(): pl.pallas_call(functools.partial(state_kernel, features, each, parts, pie...  0.9 us
  transfers between devices with their start and end apart: 15, of which 9 were waited for; matrix products, arithmetic and copies ran while one was open for 0% of the time, Pallas kernels for 15%

profile of v4, /device:TPU:0, one launch (start us, length us, event | category | flops | bytes accessed | tf_op | source)
XLA Modules:
  0.0 41.6 jit_solution(6209012816580004580)
XLA Ops:
  0.6 2.3 %shard_map.85 = (f32[128,2048]{1,0:T(8,128)S(1)}, bf16[128,2048]{1,0:T(8,128)(2,1)S(1)}, f32[128,128]{1,0:T(8,128)S(1)}, bf16[128,2048]{1,0:T(8,128)(2,1)S(1)}, ...) custom-call(bf16[128,2048]{1,0:T(8,128)(2,1)} %q_hbm.1, ...), custom_call_target="tpu_custom_call" | custom-call | tf_op jit(solution)/shard_map/pallas_call | solution.py:196
  3.0 0.5 %collective-permute-start = (f32[128,128]{1,0:T(8,128)S(1)}, f32[128,128]{1,0:T(8,128)S(1)}, u32[]{:S(2)}, u32[]{:S(2)}) collective-permute-start(f32[128,128]{1,0:T(8,128)S(1)} %get-tuple-element.46.own_ref), channel_id=1, source_target_pairs={{0,1},{1,0},{2,3},{3,2},{4,5},{5,4},{6,7},{7,6},{8,9},{9,8},{10,11... | collective-permute-start | bytes 196616 | tf_op jit(solution)/shard_map/ppermute | solution.py:175
  3.5 0.9 %collective-permute-done.other_ref = f32[128,128]{1,0:T(8,128)S(1)} collective-permute-done((f32[128,128]{1,0:T(8,128)S(1)}, f32[128,128]{1,0:T(8,128)S(1)}, u32[]{:S(2)}, u32[]{:S(2)}) %collective-permute-start) | collective-permute-done | bytes 65568 | tf_op jit(solution)/shard_map/ppermute | solution.py:175
  4.4 0.4 %shard_map.86 = (bf16[128,1024]{1,0:T(8,128)(2,1)S(1)}, f32[2,128,128]{2,1,0:T(8,128)S(1)}, f32[2,128,128]{2,1,0:T(8,128)S(1)}, f32[2,128,128]{2,1,0:T(8,128)S(1)}, f32[2,128,128]{2,1,0:T(8,128)S(1)}) custom-call(f32[128,128]{1,0:T(8,128)S(1)} %get-tuple-element.46.own_ref, f32[128,128]{1,0:T(8,128)S(1)} %collective-permute-done.other_ref, ...), custom_call_target="tpu_custom_call" | custom-call | tf_op jit(solution)/shard_map/pallas_call | solution.py:221
  4.8 3.0 %collective-permute-start.1 = (f32[2,128,128]{2,1,0:T(8,128)S(1)}, f32[2,128,128]{2,1,0:T(8,128)S(1)}, u32[]{:S(2)}, u32[]{:S(2)}) collective-permute-start(f32[2,128,128]{2,1,0:T(8,128)S(1)} %get-tuple-element.51), channel_id=1, source_target_pairs={{0,4},{2,6},{4,0},{6,2},{8,12},{10,14},{12,8},{14,10},{1,5},{3,7},... | collective-permute-start | bytes 393224 | tf_op jit(solution)/shard_map/ppermute | solution.py:175
  7.8 1.5 %collective-permute-start.9 = (f32[2,128,128]{2,1,0:T(8,128)S(1)}, f32[2,128,128]{2,1,0:T(8,128)S(1)}, u32[]{:S(2)}, u32[]{:S(2)}) collective-permute-start(f32[2,128,128]{2,1,0:T(8,128)S(1)} %get-tuple-element.66), channel_id=1, source_target_pairs={{0,2},{2,0},{4,6},{6,4},{8,10},{10,8},{12,14},{14,12},{1,3},{3,1},... | collective-permute-start | bytes 393224 | tf_op jit(solution)/shard_map/ppermute | solution.py:175
  9.3 0.0 collective-permute-start.10
  9.4 2.4 %collective-permute-done.1.refs_0_ = f32[2,128,128]{2,1,0:T(8,128)S(1)} collective-permute-done((f32[2,128,128]{2,1,0:T(8,128)S(1)}, f32[2,128,128]{2,1,0:T(8,128)S(1)}, u32[]{:S(2)}, u32[]{:S(2)}) %collective-permute-start.1) | collective-permute-done | bytes 131104 | tf_op jit(solution)/shard_map/ppermute | solution.py:175
  11.7 0.5 %shard_map.87 = (bf16[128,1024]{1,0:T(8,128)(2,1)S(1)}, f32[2,128,128]{2,1,0:T(8,128)S(1)}, f32[2,128,128]{2,1,0:T(8,128)S(1)}, f32[2,128,128]{2,1,0:T(8,128)S(1)}, f32[2,128,128]{2,1,0:T(8,128)S(1)}) custom-call(f32[128,128]{1,0:T(8,128)S(1)} %get-tuple-element.46.own_ref, f32[128,128]{1,0:T(8,128)S(1)} %collective-permute-done.other_ref, ...), custom_call_target="tpu_custom_call" | custom-call | tf_op jit(solution)/shard_map/pallas_call | solution.py:221
  12.2 2.5 %collective-permute-start.2 = (f32[2,128,128]{2,1,0:T(8,128)S(1)}, f32[2,128,128]{2,1,0:T(8,128)S(1)}, u32[]{:S(2)}, u32[]{:S(2)}) collective-permute-start(f32[2,128,128]{2,1,0:T(8,128)S(1)} %get-tuple-element.56), channel_id=1, source_target_pairs={{0,4},{2,6},{4,0},{6,2},{8,12},{10,14},{12,8},{14,10},{1,5},{3,7},... | collective-permute-start | bytes 393224 | tf_op jit(solution)/shard_map/ppermute | solution.py:175
  14.7 1.5 %collective-permute-start.3 = (f32[2,128,128]{2,1,0:T(8,128)S(1)}, f32[2,128,128]{2,1,0:T(8,128)S(1)}, u32[]{:S(2)}, u32[]{:S(2)}) collective-permute-start(f32[2,128,128]{2,1,0:T(8,128)S(1)} %get-tuple-element.57), channel_id=1, source_target_pairs={{0,2},{2,0},{4,6},{6,4},{8,10},{10,8},{12,14},{14,12},{1,3},{3,1},... | collective-permute-start | bytes 393224 | tf_op jit(solution)/shard_map/ppermute | solution.py:175
  16.2 0.0 collective-permute-start.4
  16.2 0.0 collective-permute-done.9.refs_1_
  16.2 0.0 collective-permute-done.10.refs_2_
  16.3 2.6 %collective-permute-start.11 = (f32[2,128,128]{2,1,0:T(8,128)S(1)}, f32[2,128,128]{2,1,0:T(8,128)S(1)}, u32[]{:S(2)}, u32[]{:S(2)}) collective-permute-start(f32[2,128,128]{2,1,0:T(8,128)S(1)} %add_add_fusion), channel_id=1, source_target_pairs={{0,8},{2,10},{4,12},{6,14},{8,0},{10,2},{12,4},{14,6},{1,9},{3,11}... | collective-permute-start | bytes 393224 | tf_op jit(solution)/shard_map/ppermute | solution.py:175
  18.9 1.1 %collective-permute-done.2.refs_0_ = f32[2,128,128]{2,1,0:T(8,128)S(1)} collective-permute-done((f32[2,128,128]{2,1,0:T(8,128)S(1)}, f32[2,128,128]{2,1,0:T(8,128)S(1)}, u32[]{:S(2)}, u32[]{:S(2)}) %collective-permute-start.2) | collective-permute-done | bytes 131104 | tf_op jit(solution)/shard_map/ppermute | solution.py:175
  20.0 0.3 collective-permute-done.3.refs_1_
  20.3 3.1 %collective-permute-done.4.refs_2_ = f32[2,128,128]{2,1,0:T(8,128)S(1)} collective-permute-done((f32[2,128,128]{2,1,0:T(8,128)S(1)}, f32[2,128,128]{2,1,0:T(8,128)S(1)}, u32[]{:S(2)}, u32[]{:S(2)}) %collective-permute-start.4) | collective-permute-done | bytes 131104 | tf_op jit(solution)/shard_map/ppermute | solution.py:175
  23.4 2.3 %collective-permute-start.5 = (f32[2,128,128]{2,1,0:T(8,128)S(1)}, f32[2,128,128]{2,1,0:T(8,128)S(1)}, u32[]{:S(2)}, u32[]{:S(2)}) collective-permute-start(f32[2,128,128]{2,1,0:T(8,128)S(1)} %add_add_fusion.1), channel_id=1, source_target_pairs={{0,8},{2,10},{4,12},{6,14},{8,0},{10,2},{12,4},{14,6},{1,9},{3,11}... | collective-permute-start | bytes 393224 | tf_op jit(solution)/shard_map/ppermute | solution.py:175
  25.7 0.0 collective-permute-done.11.refs_4_
  25.7 0.1 shard_map.90
  25.9 1.5 %collective-permute-start.12 = (f32[2,128,128]{2,1,0:T(8,128)S(1)}, f32[2,128,128]{2,1,0:T(8,128)S(1)}, u32[]{:S(2)}, u32[]{:S(2)}) collective-permute-start(f32[2,128,128]{2,1,0:T(8,128)S(1)} %get-tuple-element.69), channel_id=1, source_target_pairs={{0,4},{2,6},{4,0},{6,2},{8,12},{10,14},{12,8},{14,10},{1,5},{3,7},... | collective-permute-start | bytes 393224 | tf_op jit(solution)/shard_map/ppermute | solution.py:175
  27.4 1.9 %collective-permute-start.13 = (f32[2,128,128]{2,1,0:T(8,128)S(1)}, f32[2,128,128]{2,1,0:T(8,128)S(1)}, u32[]{:S(2)}, u32[]{:S(2)}) collective-permute-start(f32[2,128,128]{2,1,0:T(8,128)S(1)} %get-tuple-element.70), channel_id=1, source_target_pairs={{0,2},{2,0},{4,6},{6,4},{8,10},{10,8},{12,14},{14,12},{1,3},{3,1},... | collective-permute-start | bytes 393224 | tf_op jit(solution)/shard_map/ppermute | solution.py:175
  29.2 0.2 collective-permute-start.14
  29.4 1.4 %collective-permute-done.5.refs_4_ = f32[2,128,128]{2,1,0:T(8,128)S(1)} collective-permute-done((f32[2,128,128]{2,1,0:T(8,128)S(1)}, f32[2,128,128]{2,1,0:T(8,128)S(1)}, u32[]{:S(2)}, u32[]{:S(2)}) %collective-permute-start.5) | collective-permute-done | bytes 131104 | tf_op jit(solution)/shard_map/ppermute | solution.py:175
  30.9 0.1 shard_map.89
  31.0 0.7 %collective-permute-start.7 = (f32[2,128,128]{2,1,0:T(8,128)S(1)}, f32[2,128,128]{2,1,0:T(8,128)S(1)}, u32[]{:S(2)}, u32[]{:S(2)}) collective-permute-start(f32[2,128,128]{2,1,0:T(8,128)S(1)} %get-tuple-element.62), channel_id=1, source_target_pairs={{0,4},{2,6},{4,0},{6,2},{8,12},{10,14},{12,8},{14,10},{1,5},{3,7},... | collective-permute-start | bytes 393224 | tf_op jit(solution)/shard_map/ppermute | solution.py:175
  31.7 1.3 %collective-permute-start.8 = (f32[2,128,128]{2,1,0:T(8,128)S(1)}, f32[2,128,128]{2,1,0:T(8,128)S(1)}, u32[]{:S(2)}, u32[]{:S(2)}) collective-permute-start(f32[2,128,128]{2,1,0:T(8,128)S(1)} %get-tuple-element.63), channel_id=1, source_target_pairs={{0,2},{2,0},{4,6},{6,4},{8,10},{10,8},{12,14},{14,12},{1,3},{3,1},... | collective-permute-start | bytes 393224 | tf_op jit(solution)/shard_map/ppermute | solution.py:175
  32.9 0.1 collective-permute-done.12.refs_0_
  33.1 1.5 %collective-permute-start.6 = (f32[2,128,128]{2,1,0:T(8,128)S(1)}, f32[2,128,128]{2,1,0:T(8,128)S(1)}, u32[]{:S(2)}, u32[]{:S(2)}) collective-permute-start(f32[2,128,128]{2,1,0:T(8,128)S(1)} %get-tuple-element.60), channel_id=1, source_target_pairs={{0,6},{2,4},{4,2},{6,0},{8,14},{10,12},{12,10},{14,8},{1,7},{3,5},... | collective-permute-start | bytes 393224 | tf_op jit(solution)/shard_map/ppermute | solution.py:175
  34.6 3.4 %shard_map.88 = (bf16[128,2048]{1,0:T(8,128)(2,1)}, f32[128,1024]{1,0:T(8,128)S(1)}, f32[128,1024]{1,0:T(8,128)S(1)}, f32[128,1024]{1,0:T(8,128)S(1)}, f32[128,1024]{1,0:T(8,128)S(1)}) custom-call(bf16[128,2048]{1,0:T(8,128)(2,1)S(1)} %get-tuple-element.41.q_ref, bf16[128,2048]{1,0:T(8,128)(2,1)S(1)} %get-tuple-element.42.k_ref, ...), custom_call_target="tpu_custom_call" | custom-call | tf_op jit(solution)/shard_map/pallas_call | solution.py:253
  38.0 0.0 collective-permute-done.13.refs_1_
  38.0 0.0 collective-permute-done.14.refs_2_
  38.0 1.1 %shard_map.91 = (bf16[128,2048]{1,0:T(8,128)(2,1)}, bf16[128,2048]{1,0:T(8,128)(2,1)}) custom-call(bf16[128,2048]{1,0:T(8,128)(2,1)S(1)} %get-tuple-element.42.k_ref, bf16[128,2048]{1,0:T(8,128)(2,1)S(1)} %get-tuple-element.43.v_ref, f32[128,1024]{1,0:T(8,128)S(1)} %get-tuple-element.64.key_in, f32[128,1024]{1,0:T(8,128)S(1)} %get-tuple-element.65.value_in, ...), custom_call_target="tpu_custom_call" | custom-call | tf_op jit(solution)/shard_map/pallas_call | solution.py:265
  39.1 0.0 collective-permute-done.7.refs_1_
  39.1 0.3 collective-permute-done.8.refs_2_
  39.4 1.0 %shard_map.92 = (bf16[128,2048]{1,0:T(8,128)(2,1)}, bf16[128,2048]{1,0:T(8,128)(2,1)}) custom-call(bf16[128,2048]{1,0:T(8,128)(2,1)S(1)} %get-tuple-element.42.k_ref, bf16[128,2048]{1,0:T(8,128)(2,1)S(1)} %get-tuple-element.43.v_ref, f32[128,1024]{1,0:T(8,128)S(1)} %get-tuple-element.54.key_in, ...), custom_call_target="tpu_custom_call", output_to_operand_aliasing={{0}: (7, {}), {1}: (8, {})} | custom-call | tf_op jit(solution)/shard_map/pallas_call | solution.py:265
  40.4 0.3 collective-permute-done.6.refs_0_
  40.7 0.9 %shard_map.93 = (bf16[128,2048]{1,0:T(8,128)(2,1)}, bf16[128,2048]{1,0:T(8,128)(2,1)}) custom-call(bf16[128,2048]{1,0:T(8,128)(2,1)S(1)} %get-tuple-element.42.k_ref, bf16[128,2048]{1,0:T(8,128)(2,1)S(1)} %get-tuple-element.43.v_ref, f32[128,1024]{1,0:T(8,128)S(1)} %get-tuple-element.54.key_in, ...), custom_call_target="tpu_custom_call", output_to_operand_aliasing={{0}: (5, {}), {1}: (6, {})} | custom-call | tf_op jit(solution)/shard_map/pallas_call | solution.py:265
  (2 shorter events, 0.1 us)
Async XLA Ops:
  3.0 1.4 %collective-permute-start = (f32[128,128]{1,0:T(8,128)S(1)}, f32[128,128]{1,0:T(8,128)S(1)}, u32[]{:S(2)}, u32[]{:S(2)}) collective-permute-start(f32[128,128]{1,0:T(8,128)S(1)} %get-tuple-element.46.own_ref), channel_id=1, source_target_pairs={{0,1},{1,0},{2,3},{3,2},{4,5},{5,4},{6,7},{7,6},{8,9},{9,8},{10,11... | collective-permute-start | bytes 196616 | tf_op jit(solution)/shard_map/ppermute | solution.py:175
  4.8 6.9 %collective-permute-start.1 = (f32[2,128,128]{2,1,0:T(8,128)S(1)}, f32[2,128,128]{2,1,0:T(8,128)S(1)}, u32[]{:S(2)}, u32[]{:S(2)}) collective-permute-start(f32[2,128,128]{2,1,0:T(8,128)S(1)} %get-tuple-element.51), channel_id=1, source_target_pairs={{0,4},{2,6},{4,0},{6,2},{8,12},{10,14},{12,8},{14,10},{1,5},{3,7},... | collective-permute-start | bytes 393224 | tf_op jit(solution)/shard_map/ppermute | solution.py:175
  7.8 8.4 %collective-permute-start.9 = (f32[2,128,128]{2,1,0:T(8,128)S(1)}, f32[2,128,128]{2,1,0:T(8,128)S(1)}, u32[]{:S(2)}, u32[]{:S(2)}) collective-permute-start(f32[2,128,128]{2,1,0:T(8,128)S(1)} %get-tuple-element.66), channel_id=1, source_target_pairs={{0,2},{2,0},{4,6},{6,4},{8,10},{10,8},{12,14},{14,12},{1,3},{3,1},... | collective-permute-start | bytes 393224 | tf_op jit(solution)/shard_map/ppermute | solution.py:175
  9.3 6.9 %collective-permute-start.10 = (f32[2,128,128]{2,1,0:T(8,128)S(1)}, f32[2,128,128]{2,1,0:T(8,128)S(1)}, u32[]{:S(2)}, u32[]{:S(2)}) collective-permute-start(f32[2,128,128]{2,1,0:T(8,128)S(1)} %get-tuple-element.67), channel_id=1, source_target_pairs={{0,6},{2,4},{4,2},{6,0},{8,14},{10,12},{12,10},{14,8},{1,7},{3,5},... | collective-permute-start | bytes 393224 | tf_op jit(solution)/shard_map/ppermute | solution.py:175
  12.2 7.8 %collective-permute-start.2 = (f32[2,128,128]{2,1,0:T(8,128)S(1)}, f32[2,128,128]{2,1,0:T(8,128)S(1)}, u32[]{:S(2)}, u32[]{:S(2)}) collective-permute-start(f32[2,128,128]{2,1,0:T(8,128)S(1)} %get-tuple-element.56), channel_id=1, source_target_pairs={{0,4},{2,6},{4,0},{6,2},{8,12},{10,14},{12,8},{14,10},{1,5},{3,7},... | collective-permute-start | bytes 393224 | tf_op jit(solution)/shard_map/ppermute | solution.py:175
  14.7 5.6 %collective-permute-start.3 = (f32[2,128,128]{2,1,0:T(8,128)S(1)}, f32[2,128,128]{2,1,0:T(8,128)S(1)}, u32[]{:S(2)}, u32[]{:S(2)}) collective-permute-start(f32[2,128,128]{2,1,0:T(8,128)S(1)} %get-tuple-element.57), channel_id=1, source_target_pairs={{0,2},{2,0},{4,6},{6,4},{8,10},{10,8},{12,14},{14,12},{1,3},{3,1},... | collective-permute-start | bytes 393224 | tf_op jit(solution)/shard_map/ppermute | solution.py:175
  16.2 7.2 %collective-permute-start.4 = (f32[2,128,128]{2,1,0:T(8,128)S(1)}, f32[2,128,128]{2,1,0:T(8,128)S(1)}, u32[]{:S(2)}, u32[]{:S(2)}) collective-permute-start(f32[2,128,128]{2,1,0:T(8,128)S(1)} %get-tuple-element.58), channel_id=1, source_target_pairs={{0,6},{2,4},{4,2},{6,0},{8,14},{10,12},{12,10},{14,8},{1,7},{3,5},... | collective-permute-start | bytes 393224 | tf_op jit(solution)/shard_map/ppermute | solution.py:175
  16.3 9.5 %collective-permute-start.11 = (f32[2,128,128]{2,1,0:T(8,128)S(1)}, f32[2,128,128]{2,1,0:T(8,128)S(1)}, u32[]{:S(2)}, u32[]{:S(2)}) collective-permute-start(f32[2,128,128]{2,1,0:T(8,128)S(1)} %add_add_fusion), channel_id=1, source_target_pairs={{0,8},{2,10},{4,12},{6,14},{8,0},{10,2},{12,4},{14,6},{1,9},{3,11}... | collective-permute-start | bytes 393224 | tf_op jit(solution)/shard_map/ppermute | solution.py:175
  23.4 7.5 %collective-permute-start.5 = (f32[2,128,128]{2,1,0:T(8,128)S(1)}, f32[2,128,128]{2,1,0:T(8,128)S(1)}, u32[]{:S(2)}, u32[]{:S(2)}) collective-permute-start(f32[2,128,128]{2,1,0:T(8,128)S(1)} %add_add_fusion.1), channel_id=1, source_target_pairs={{0,8},{2,10},{4,12},{6,14},{8,0},{10,2},{12,4},{14,6},{1,9},{3,11}... | collective-permute-start | bytes 393224 | tf_op jit(solution)/shard_map/ppermute | solution.py:175
  25.9 7.2 %collective-permute-start.12 = (f32[2,128,128]{2,1,0:T(8,128)S(1)}, f32[2,128,128]{2,1,0:T(8,128)S(1)}, u32[]{:S(2)}, u32[]{:S(2)}) collective-permute-start(f32[2,128,128]{2,1,0:T(8,128)S(1)} %get-tuple-element.69), channel_id=1, source_target_pairs={{0,4},{2,6},{4,0},{6,2},{8,12},{10,14},{12,8},{14,10},{1,5},{3,7},... | collective-permute-start | bytes 393224 | tf_op jit(solution)/shard_map/ppermute | solution.py:175
  27.4 10.6 %collective-permute-start.13 = (f32[2,128,128]{2,1,0:T(8,128)S(1)}, f32[2,128,128]{2,1,0:T(8,128)S(1)}, u32[]{:S(2)}, u32[]{:S(2)}) collective-permute-start(f32[2,128,128]{2,1,0:T(8,128)S(1)} %get-tuple-element.70), channel_id=1, source_target_pairs={{0,2},{2,0},{4,6},{6,4},{8,10},{10,8},{12,14},{14,12},{1,3},{3,1},... | collective-permute-start | bytes 393224 | tf_op jit(solution)/shard_map/ppermute | solution.py:175
  29.2 8.7 %collective-permute-start.14 = (f32[2,128,128]{2,1,0:T(8,128)S(1)}, f32[2,128,128]{2,1,0:T(8,128)S(1)}, u32[]{:S(2)}, u32[]{:S(2)}) collective-permute-start(f32[2,128,128]{2,1,0:T(8,128)S(1)} %get-tuple-element.71), channel_id=1, source_target_pairs={{0,6},{2,4},{4,2},{6,0},{8,14},{10,12},{12,10},{14,8},{1,7},{3,5},... | collective-permute-start | bytes 393224 | tf_op jit(solution)/shard_map/ppermute | solution.py:175
  31.0 8.1 %collective-permute-start.7 = (f32[2,128,128]{2,1,0:T(8,128)S(1)}, f32[2,128,128]{2,1,0:T(8,128)S(1)}, u32[]{:S(2)}, u32[]{:S(2)}) collective-permute-start(f32[2,128,128]{2,1,0:T(8,128)S(1)} %get-tuple-element.62), channel_id=1, source_target_pairs={{0,4},{2,6},{4,0},{6,2},{8,12},{10,14},{12,8},{14,10},{1,5},{3,7},... | collective-permute-start | bytes 393224 | tf_op jit(solution)/shard_map/ppermute | solution.py:175
  31.7 7.7 %collective-permute-start.8 = (f32[2,128,128]{2,1,0:T(8,128)S(1)}, f32[2,128,128]{2,1,0:T(8,128)S(1)}, u32[]{:S(2)}, u32[]{:S(2)}) collective-permute-start(f32[2,128,128]{2,1,0:T(8,128)S(1)} %get-tuple-element.63), channel_id=1, source_target_pairs={{0,2},{2,0},{4,6},{6,4},{8,10},{10,8},{12,14},{14,12},{1,3},{3,1},... | collective-permute-start | bytes 393224 | tf_op jit(solution)/shard_map/ppermute | solution.py:175
  33.1 7.7 %collective-permute-start.6 = (f32[2,128,128]{2,1,0:T(8,128)S(1)}, f32[2,128,128]{2,1,0:T(8,128)S(1)}, u32[]{:S(2)}, u32[]{:S(2)}) collective-permute-start(f32[2,128,128]{2,1,0:T(8,128)S(1)} %get-tuple-element.60), channel_id=1, source_target_pairs={{0,6},{2,4},{4,2},{6,0},{8,14},{10,12},{12,10},{14,8},{1,7},{3,5},... | collective-permute-start | bytes 393224 | tf_op jit(solution)/shard_map/ppermute | solution.py:175

commit v5 on v3

--- a/solution.py
+++ b/solution.py
@@ -28,6 +28,11 @@
     if isinstance(head, int):
         return pl.ds(head * HEAD, count * HEAD)
     return pl.ds(pl.multiple_of(head * HEAD, HEAD), count * HEAD)
+
+
+def turn(step):
+    core = lax.rem(lax.axis_index("tp"), 2)
+    return {0: 0, 1: 1 + core, 2: 2 - core, 3: 3}[step]
 
 
 def lower(rows):
@@ -109,8 +114,7 @@
     for target, step in enumerate(STEPS):
         value = behind
         for source, other in enumerate(STEPS):
-            if source != target:
-                value += jnp.where((me ^ other) > (me ^ step), blocks[source], 0.0)
+            value += jnp.where((me ^ other) > (me ^ turn(step)), blocks[source], 0.0)
         sum_refs[target][...] = value
 
 
@@ -123,9 +127,10 @@
     for part, (start, count) in enumerate(parts):
         for index, step in enumerate(STEPS):
             for local in range(count):
-                head = (me ^ step) * each + start + local
+                head = (me ^ turn(step)) * each + start + local
                 at, slot = columns(head), columns(index * count + local)
-                g = g_refs[part][:, slot]
+                held = index if index > 1 else lax.rem(lax.axis_index("tp") + index, 2)
+                g = g_refs[part][:, columns(held * count + local)]
                 grads = jnp.where(mask, dot(g, v_ref[:, at], NT), 0.0).astype(jnp.bfloat16)
                 query = dot(grads, k_ref[:, at], NN) + dot(g, s_ref[head], NT)
                 query_ref[:, at] = query.astype(jnp.bfloat16)
@@ -141,14 +146,14 @@
     for index, step in enumerate(STEPS):
         slots = columns(index * count, count)
         for local in range(count):
-            at = columns((me ^ step) * each + start + local)
+            at = columns((me ^ turn(step)) * each + start + local)
             slot = columns(index * count + local)
             later = later_refs[index][local].astype(jnp.bfloat16)
             key = key_in[:, slot] + dot(v_ref[:, at], later, NT)
             key_ref[:, slot] = key.astype(jnp.bfloat16)
             value = value_in[:, slot] + dot(k_ref[:, at], later, NN)
             value_ref[:, slot] = value.astype(jnp.bfloat16)
-        at = columns((me ^ step) * each + start, count)
+        at = columns((me ^ turn(step)) * each + start, count)
         for pair, (source, target) in enumerate(((key_ref, key_hbm), (value_ref, value_hbm))):
             copy = pltpu.make_async_copy(source.at[:, slots], target.at[:, at], sems.at[index, pair])
             copy.start()
@@ -170,6 +175,20 @@
     return [
         partner(piece, "ctx", step) if step else piece for piece, step in zip(pieces, STEPS)
     ]
+
+
+def return_swap(pieces):
+    cores = lax.axis_size("tp")
+    places = range(lax.axis_size("ctx"))
+    came = []
+    for piece, step in zip(pieces, STEPS):
+        pairs = []
+        for place in places:
+            for core in range(cores):
+                other = {0: 0, 1: 1 + core % 2, 2: 2 - core % 2, 3: 3}[step]
+                pairs.append((place * cores + core, (place ^ other) * cores + core))
+        came.append(lax.ppermute(piece, ("ctx", "tp"), pairs) if step else piece)
+    return came
 
 
 def per_device(queries, keys, values, grad_y, state_low, gain):
@@ -235,7 +254,7 @@
             out_specs=(VMEM,) * QUAD,
             compiler_params=params(8),
         )(*blocks, *behind)
-        later.append(quad_swap(sums))
+        later.append(return_swap(sums))
 
     slots = [near((rows, QUAD * count * HEAD), jnp.float32) for _, count in parts]
     grad_query, *local = pl.pallas_call(

time: 42 us -> 41.8 us (level)
    ppermute x0 -> x6, starting transfers between devices: none -> 7.1 us  [return_swap(): came.append(lax.ppermute(piece, ('ctx', 'tp'), pairs) if step else piece)]
    ppermute x15 -> x9, starting transfers between devices: 21.1 us -> 14.1 us  [partner(): lax.ppermute(value, axis, [(source, source ^ mask) for source in range(co...]
    ppermute x15 -> x9, waiting for transfers between devices: 10.9 us -> 9.22 us  [partner(): lax.ppermute(value, axis, [(source, source ^ mask) for source in range(co...]
    ppermute x0 -> x6, waiting for transfers between devices: none -> 1.42 us  [return_swap(): came.append(lax.ppermute(piece, ('ctx', 'tp'), pairs) if step else piece)]
  transfers between devices with their start and end apart: 15 -> 15, of which waited for: 9 -> 7; matrix products, arithmetic and copies ran while one was open for 0% -> 0% of each run, Pallas kernels for 12% -> 13%
where the time goes in v5:
time: 41.8 us; the launch traced here: 41.7 us
  starting transfers between devices  21.2 us (51%)
  waiting for transfers between devices  10.6 us (25%)
  Pallas kernels  9.11 us (22%)
  between operations  0.7 us (2%)
    ppermute x9, starting transfers between devices, partner(): lax.ppermute(value, axis, [(source, source ^ mask) for source in range(co...  14.1 us
    ppermute x9, waiting for transfers between devices, partner(): lax.ppermute(value, axis, [(source, source ^ mask) for source in range(co...  9.22 us
    ppermute x6, starting transfers between devices, return_swap(): came.append(lax.ppermute(piece, ('ctx', 'tp'), pairs) if step else piece)  7.1 us
    pallas_call x1, Pallas kernels, per_device(): pl.pallas_call(functools.partial(local_kernel, each, parts), out_shape=(h...  3.38 us
    pallas_call x1, Pallas kernels, per_device(): pl.pallas_call(forward_kernel, out_shape=(near((rows, width), jnp.float32...  2.32 us
    pallas_call x2, Pallas kernels, per_device(): pl.pallas_call(functools.partial(final_kernel, each, start, count), out_s...  2.19 us
    ppermute x6, waiting for transfers between devices, return_swap(): came.append(lax.ppermute(piece, ('ctx', 'tp'), pairs) if step else piece)  1.42 us
    pallas_call x2, Pallas kernels, per_device(): pl.pallas_call(functools.partial(state_kernel, features, each, start, cou...  0.9 us
  transfers between devices with their start and end apart: 15, of which 7 were waited for; matrix products, arithmetic and copies ran while one was open for 0% of the time, Pallas kernels for 13%

profile of v5, /device:TPU:0, one launch (start us, length us, event | category | flops | bytes accessed | tf_op | source)
XLA Modules:
  0.0 41.7 jit_solution(2834538762629453517)
XLA Ops:
  0.6 2.3 %shard_map.85 = (f32[128,2048]{1,0:T(8,128)S(1)}, bf16[128,2048]{1,0:T(8,128)(2,1)S(1)}, f32[128,128]{1,0:T(8,128)S(1)}, bf16[128,2048]{1,0:T(8,128)(2,1)S(1)}, ...) custom-call(bf16[128,2048]{1,0:T(8,128)(2,1)} %q_hbm.1, ...), custom_call_target="tpu_custom_call" | custom-call | tf_op jit(solution)/shard_map/pallas_call | solution.py:206
  3.0 0.5 %collective-permute-start = (f32[128,128]{1,0:T(8,128)S(1)}, f32[128,128]{1,0:T(8,128)S(1)}, u32[]{:S(2)}, u32[]{:S(2)}) collective-permute-start(f32[128,128]{1,0:T(8,128)S(1)} %get-tuple-element.44.own_ref), channel_id=1, source_target_pairs={{0,1},{1,0},{2,3},{3,2},{4,5},{5,4},{6,7},{7,6},{8,9},{9,8},{10,11... | collective-permute-start | bytes 196616 | tf_op jit(solution)/shard_map/ppermute | solution.py:171
  3.5 0.9 %collective-permute-done.other_ref = f32[128,128]{1,0:T(8,128)S(1)} collective-permute-done((f32[128,128]{1,0:T(8,128)S(1)}, f32[128,128]{1,0:T(8,128)S(1)}, u32[]{:S(2)}, u32[]{:S(2)}) %collective-permute-start) | collective-permute-done | bytes 65568 | tf_op jit(solution)/shard_map/ppermute | solution.py:171
  4.4 0.4 %shard_map.86 = (bf16[128,1024]{1,0:T(8,128)(2,1)S(1)}, f32[2,128,128]{2,1,0:T(8,128)S(1)}, f32[2,128,128]{2,1,0:T(8,128)S(1)}, f32[2,128,128]{2,1,0:T(8,128)S(1)}, f32[2,128,128]{2,1,0:T(8,128)S(1)}) custom-call(f32[128,128]{1,0:T(8,128)S(1)} %get-tuple-element.44.own_ref, f32[128,128]{1,0:T(8,128)S(1)} %collective-permute-done.other_ref, ...), custom_call_target="tpu_custom_call" | custom-call | tf_op jit(solution)/shard_map/pallas_call | solution.py:230
  4.8 3.0 %collective-permute-start.1 = (f32[2,128,128]{2,1,0:T(8,128)S(1)}, f32[2,128,128]{2,1,0:T(8,128)S(1)}, u32[]{:S(2)}, u32[]{:S(2)}) collective-permute-start(f32[2,128,128]{2,1,0:T(8,128)S(1)} %get-tuple-element.49), channel_id=1, source_target_pairs={{0,4},{2,6},{4,0},{6,2},{8,12},{10,14},{12,8},{14,10},{1,5},{3,7},... | collective-permute-start | bytes 393224 | tf_op jit(solution)/shard_map/ppermute | solution.py:171
  7.8 1.5 %collective-permute-start.9 = (f32[2,128,128]{2,1,0:T(8,128)S(1)}, f32[2,128,128]{2,1,0:T(8,128)S(1)}, u32[]{:S(2)}, u32[]{:S(2)}) collective-permute-start(f32[2,128,128]{2,1,0:T(8,128)S(1)} %get-tuple-element.64), channel_id=1, source_target_pairs={{0,2},{2,0},{4,6},{6,4},{8,10},{10,8},{12,14},{14,12},{1,3},{3,1},... | collective-permute-start | bytes 393224 | tf_op jit(solution)/shard_map/ppermute | solution.py:171
  9.3 0.0 collective-permute-start.10
  9.4 2.4 %collective-permute-done.1.refs_0_ = f32[2,128,128]{2,1,0:T(8,128)S(1)} collective-permute-done((f32[2,128,128]{2,1,0:T(8,128)S(1)}, f32[2,128,128]{2,1,0:T(8,128)S(1)}, u32[]{:S(2)}, u32[]{:S(2)}) %collective-permute-start.1) | collective-permute-done | bytes 131104 | tf_op jit(solution)/shard_map/ppermute | solution.py:171
  11.7 0.5 %shard_map.87 = (bf16[128,1024]{1,0:T(8,128)(2,1)S(1)}, f32[2,128,128]{2,1,0:T(8,128)S(1)}, f32[2,128,128]{2,1,0:T(8,128)S(1)}, f32[2,128,128]{2,1,0:T(8,128)S(1)}, f32[2,128,128]{2,1,0:T(8,128)S(1)}) custom-call(f32[128,128]{1,0:T(8,128)S(1)} %get-tuple-element.44.own_ref, f32[128,128]{1,0:T(8,128)S(1)} %collective-permute-done.other_ref, ...), custom_call_target="tpu_custom_call" | custom-call | tf_op jit(solution)/shard_map/pallas_call | solution.py:230
  12.2 2.5 %collective-permute-start.2 = (f32[2,128,128]{2,1,0:T(8,128)S(1)}, f32[2,128,128]{2,1,0:T(8,128)S(1)}, u32[]{:S(2)}, u32[]{:S(2)}) collective-permute-start(f32[2,128,128]{2,1,0:T(8,128)S(1)} %get-tuple-element.54), channel_id=1, source_target_pairs={{0,4},{2,6},{4,0},{6,2},{8,12},{10,14},{12,8},{14,10},{1,5},{3,7},... | collective-permute-start | bytes 393224 | tf_op jit(solution)/shard_map/ppermute | solution.py:171
  14.7 1.5 %collective-permute-start.3 = (f32[2,128,128]{2,1,0:T(8,128)S(1)}, f32[2,128,128]{2,1,0:T(8,128)S(1)}, u32[]{:S(2)}, u32[]{:S(2)}) collective-permute-start(f32[2,128,128]{2,1,0:T(8,128)S(1)} %get-tuple-element.55), channel_id=1, source_target_pairs={{0,2},{2,0},{4,6},{6,4},{8,10},{10,8},{12,14},{14,12},{1,3},{3,1},... | collective-permute-start | bytes 393224 | tf_op jit(solution)/shard_map/ppermute | solution.py:171
  16.2 0.0 collective-permute-start.4
  16.2 0.0 collective-permute-done.9.refs_1_
  16.2 0.0 collective-permute-done.10.refs_2_
  16.3 2.6 %collective-permute-start.11 = (f32[2,128,128]{2,1,0:T(8,128)S(1)}, f32[2,128,128]{2,1,0:T(8,128)S(1)}, u32[]{:S(2)}, u32[]{:S(2)}) collective-permute-start(f32[2,128,128]{2,1,0:T(8,128)S(1)} %add_add_fusion), channel_id=1, source_target_pairs={{0,8},{2,10},{4,12},{6,14},{8,0},{10,2},{12,4},{14,6},{1,9},{3,11}... | collective-permute-start | bytes 393224 | tf_op jit(solution)/shard_map/ppermute | solution.py:171
  18.9 1.1 %collective-permute-done.2.refs_0_ = f32[2,128,128]{2,1,0:T(8,128)S(1)} collective-permute-done((f32[2,128,128]{2,1,0:T(8,128)S(1)}, f32[2,128,128]{2,1,0:T(8,128)S(1)}, u32[]{:S(2)}, u32[]{:S(2)}) %collective-permute-start.2) | collective-permute-done | bytes 131104 | tf_op jit(solution)/shard_map/ppermute | solution.py:171
  20.0 0.3 collective-permute-done.3.refs_1_
  20.3 3.1 %collective-permute-done.4.refs_2_ = f32[2,128,128]{2,1,0:T(8,128)S(1)} collective-permute-done((f32[2,128,128]{2,1,0:T(8,128)S(1)}, f32[2,128,128]{2,1,0:T(8,128)S(1)}, u32[]{:S(2)}, u32[]{:S(2)}) %collective-permute-start.4) | collective-permute-done | bytes 131104 | tf_op jit(solution)/shard_map/ppermute | solution.py:171
  23.4 2.3 %collective-permute-start.5 = (f32[2,128,128]{2,1,0:T(8,128)S(1)}, f32[2,128,128]{2,1,0:T(8,128)S(1)}, u32[]{:S(2)}, u32[]{:S(2)}) collective-permute-start(f32[2,128,128]{2,1,0:T(8,128)S(1)} %add_add_fusion.1), channel_id=1, source_target_pairs={{0,8},{2,10},{4,12},{6,14},{8,0},{10,2},{12,4},{14,6},{1,9},{3,11}... | collective-permute-start | bytes 393224 | tf_op jit(solution)/shard_map/ppermute | solution.py:171
  25.7 0.0 collective-permute-done.11.refs_4_
  25.7 0.1 shard_map.90
  25.9 1.5 %collective-permute-start.12 = (f32[2,128,128]{2,1,0:T(8,128)S(1)}, f32[2,128,128]{2,1,0:T(8,128)S(1)}, u32[]{:S(2)}, u32[]{:S(2)}) collective-permute-start(f32[2,128,128]{2,1,0:T(8,128)S(1)} %get-tuple-element.67), channel_id=1, source_target_pairs={{0,4},{1,3},{2,6},{3,1},{4,0},{5,7},{6,2},{7,5},{8,12},{9,11},{10,... | collective-permute-start | bytes 393224 | tf_op jit(solution)/shard_map/ppermute | solution.py:190
  27.4 1.7 %collective-permute-start.13 = (f32[2,128,128]{2,1,0:T(8,128)S(1)}, f32[2,128,128]{2,1,0:T(8,128)S(1)}, u32[]{:S(2)}, u32[]{:S(2)}) collective-permute-start(f32[2,128,128]{2,1,0:T(8,128)S(1)} %get-tuple-element.68), channel_id=1, source_target_pairs={{0,2},{1,5},{2,0},{3,7},{4,6},{5,1},{6,4},{7,3},{8,10},{9,13},{10,... | collective-permute-start | bytes 393224 | tf_op jit(solution)/shard_map/ppermute | solution.py:190
  29.1 0.4 collective-permute-start.14
  29.4 1.5 %collective-permute-done.5.refs_4_ = f32[2,128,128]{2,1,0:T(8,128)S(1)} collective-permute-done((f32[2,128,128]{2,1,0:T(8,128)S(1)}, f32[2,128,128]{2,1,0:T(8,128)S(1)}, u32[]{:S(2)}, u32[]{:S(2)}) %collective-permute-start.5) | collective-permute-done | bytes 131104 | tf_op jit(solution)/shard_map/ppermute | solution.py:171
  30.9 0.2 shard_map.89
  31.1 0.6 %collective-permute-start.6 = (f32[2,128,128]{2,1,0:T(8,128)S(1)}, f32[2,128,128]{2,1,0:T(8,128)S(1)}, u32[]{:S(2)}, u32[]{:S(2)}) collective-permute-start(f32[2,128,128]{2,1,0:T(8,128)S(1)} %get-tuple-element.58), channel_id=1, source_target_pairs={{0,4},{1,3},{2,6},{3,1},{4,0},{5,7},{6,2},{7,5},{8,12},{9,11},{10,... | collective-permute-start | bytes 393224 | tf_op jit(solution)/shard_map/ppermute | solution.py:190
  31.7 1.1 %collective-permute-start.7 = (f32[2,128,128]{2,1,0:T(8,128)S(1)}, f32[2,128,128]{2,1,0:T(8,128)S(1)}, u32[]{:S(2)}, u32[]{:S(2)}) collective-permute-start(f32[2,128,128]{2,1,0:T(8,128)S(1)} %get-tuple-element.59), channel_id=1, source_target_pairs={{0,2},{1,5},{2,0},{3,7},{4,6},{5,1},{6,4},{7,3},{8,10},{9,13},{10,... | collective-permute-start | bytes 393224 | tf_op jit(solution)/shard_map/ppermute | solution.py:190
  32.8 0.0 collective-permute-done.12.refs_0_
  32.8 1.9 %collective-permute-start.8 = (f32[2,128,128]{2,1,0:T(8,128)S(1)}, f32[2,128,128]{2,1,0:T(8,128)S(1)}, u32[]{:S(2)}, u32[]{:S(2)}) collective-permute-start(f32[2,128,128]{2,1,0:T(8,128)S(1)} %get-tuple-element.60), channel_id=1, source_target_pairs={{0,6},{1,7},{2,4},{3,5},{4,2},{5,3},{6,0},{7,1},{8,14},{9,15},{10,... | collective-permute-start | bytes 393224 | tf_op jit(solution)/shard_map/ppermute | solution.py:190
  34.7 3.4 %shard_map.88 = (bf16[128,2048]{1,0:T(8,128)(2,1)}, f32[128,1024]{1,0:T(8,128)S(1)}, f32[128,1024]{1,0:T(8,128)S(1)}, f32[128,1024]{1,0:T(8,128)S(1)}, f32[128,1024]{1,0:T(8,128)S(1)}) custom-call(bf16[128,2048]{1,0:T(8,128)(2,1)S(1)} %get-tuple-element.39.q_ref, bf16[128,2048]{1,0:T(8,128)(2,1)S(1)} %get-tuple-element.40.k_ref, ...), custom_call_target="tpu_custom_call" | custom-call | tf_op jit(solution)/shard_map/pallas_call | solution.py:260
  38.1 0.0 collective-permute-done.13.refs_1_
  38.1 0.0 collective-permute-done.14.refs_2_
  38.1 1.1 %shard_map.91 = (bf16[128,2048]{1,0:T(8,128)(2,1)}, bf16[128,2048]{1,0:T(8,128)(2,1)}) custom-call(bf16[128,2048]{1,0:T(8,128)(2,1)S(1)} %get-tuple-element.40.k_ref, bf16[128,2048]{1,0:T(8,128)(2,1)S(1)} %get-tuple-element.41.v_ref, f32[128,1024]{1,0:T(8,128)S(1)} %get-tuple-element.62.key_in, f32[128,1024]{1,0:T(8,128)S(1)} %get-tuple-element.63.value_in, ...), custom_call_target="tpu_custom_call" | custom-call | tf_op jit(solution)/shard_map/pallas_call | solution.py:270
  39.2 0.0 collective-permute-done.6.refs_0_
  39.2 0.0 collective-permute-done.7.refs_1_
  39.2 1.4 %collective-permute-done.8.refs_2_ = f32[2,128,128]{2,1,0:T(8,128)S(1)} collective-permute-done((f32[2,128,128]{2,1,0:T(8,128)S(1)}, f32[2,128,128]{2,1,0:T(8,128)S(1)}, u32[]{:S(2)}, u32[]{:S(2)}) %collective-permute-start.8) | collective-permute-done | bytes 131104 | tf_op jit(solution)/shard_map/ppermute | solution.py:190
  40.6 1.1 %shard_map.92 = (bf16[128,2048]{1,0:T(8,128)(2,1)}, bf16[128,2048]{1,0:T(8,128)(2,1)}) custom-call(bf16[128,2048]{1,0:T(8,128)(2,1)S(1)} %get-tuple-element.40.k_ref, bf16[128,2048]{1,0:T(8,128)(2,1)S(1)} %get-tuple-element.41.v_ref, f32[128,1024]{1,0:T(8,128)S(1)} %get-tuple-element.52.key_in, ...), custom_call_target="tpu_custom_call", output_to_operand_aliasing={{0}: (8, {}), {1}: (9, {})} | custom-call | tf_op jit(solution)/shard_map/pallas_call | solution.py:270
  (2 shorter events, 0.1 us)
Async XLA Ops:
  3.0 1.4 %collective-permute-start = (f32[128,128]{1,0:T(8,128)S(1)}, f32[128,128]{1,0:T(8,128)S(1)}, u32[]{:S(2)}, u32[]{:S(2)}) collective-permute-start(f32[128,128]{1,0:T(8,128)S(1)} %get-tuple-element.44.own_ref), channel_id=1, source_target_pairs={{0,1},{1,0},{2,3},{3,2},{4,5},{5,4},{6,7},{7,6},{8,9},{9,8},{10,11... | collective-permute-start | bytes 196616 | tf_op jit(solution)/shard_map/ppermute | solution.py:171
  4.8 6.9 %collective-permute-start.1 = (f32[2,128,128]{2,1,0:T(8,128)S(1)}, f32[2,128,128]{2,1,0:T(8,128)S(1)}, u32[]{:S(2)}, u32[]{:S(2)}) collective-permute-start(f32[2,128,128]{2,1,0:T(8,128)S(1)} %get-tuple-element.49), channel_id=1, source_target_pairs={{0,4},{2,6},{4,0},{6,2},{8,12},{10,14},{12,8},{14,10},{1,5},{3,7},... | collective-permute-start | bytes 393224 | tf_op jit(solution)/shard_map/ppermute | solution.py:171
  7.8 8.4 %collective-permute-start.9 = (f32[2,128,128]{2,1,0:T(8,128)S(1)}, f32[2,128,128]{2,1,0:T(8,128)S(1)}, u32[]{:S(2)}, u32[]{:S(2)}) collective-permute-start(f32[2,128,128]{2,1,0:T(8,128)S(1)} %get-tuple-element.64), channel_id=1, source_target_pairs={{0,2},{2,0},{4,6},{6,4},{8,10},{10,8},{12,14},{14,12},{1,3},{3,1},... | collective-permute-start | bytes 393224 | tf_op jit(solution)/shard_map/ppermute | solution.py:171
  9.3 6.9 %collective-permute-start.10 = (f32[2,128,128]{2,1,0:T(8,128)S(1)}, f32[2,128,128]{2,1,0:T(8,128)S(1)}, u32[]{:S(2)}, u32[]{:S(2)}) collective-permute-start(f32[2,128,128]{2,1,0:T(8,128)S(1)} %get-tuple-element.65), channel_id=1, source_target_pairs={{0,6},{2,4},{4,2},{6,0},{8,14},{10,12},{12,10},{14,8},{1,7},{3,5},... | collective-permute-start | bytes 393224 | tf_op jit(solution)/shard_map/ppermute | solution.py:171
  12.2 7.8 %collective-permute-start.2 = (f32[2,128,128]{2,1,0:T(8,128)S(1)}, f32[2,128,128]{2,1,0:T(8,128)S(1)}, u32[]{:S(2)}, u32[]{:S(2)}) collective-permute-start(f32[2,128,128]{2,1,0:T(8,128)S(1)} %get-tuple-element.54), channel_id=1, source_target_pairs={{0,4},{2,6},{4,0},{6,2},{8,12},{10,14},{12,8},{14,10},{1,5},{3,7},... | collective-permute-start | bytes 393224 | tf_op jit(solution)/shard_map/ppermute | solution.py:171
  14.7 5.6 %collective-permute-start.3 = (f32[2,128,128]{2,1,0:T(8,128)S(1)}, f32[2,128,128]{2,1,0:T(8,128)S(1)}, u32[]{:S(2)}, u32[]{:S(2)}) collective-permute-start(f32[2,128,128]{2,1,0:T(8,128)S(1)} %get-tuple-element.55), channel_id=1, source_target_pairs={{0,2},{2,0},{4,6},{6,4},{8,10},{10,8},{12,14},{14,12},{1,3},{3,1},... | collective-permute-start | bytes 393224 | tf_op jit(solution)/shard_map/ppermute | solution.py:171
  16.2 7.2 %collective-permute-start.4 = (f32[2,128,128]{2,1,0:T(8,128)S(1)}, f32[2,128,128]{2,1,0:T(8,128)S(1)}, u32[]{:S(2)}, u32[]{:S(2)}) collective-permute-start(f32[2,128,128]{2,1,0:T(8,128)S(1)} %get-tuple-element.56), channel_id=1, source_target_pairs={{0,6},{2,4},{4,2},{6,0},{8,14},{10,12},{12,10},{14,8},{1,7},{3,5},... | collective-permute-start | bytes 393224 | tf_op jit(solution)/shard_map/ppermute | solution.py:171
  16.3 9.5 %collective-permute-start.11 = (f32[2,128,128]{2,1,0:T(8,128)S(1)}, f32[2,128,128]{2,1,0:T(8,128)S(1)}, u32[]{:S(2)}, u32[]{:S(2)}) collective-permute-start(f32[2,128,128]{2,1,0:T(8,128)S(1)} %add_add_fusion), channel_id=1, source_target_pairs={{0,8},{2,10},{4,12},{6,14},{8,0},{10,2},{12,4},{14,6},{1,9},{3,11}... | collective-permute-start | bytes 393224 | tf_op jit(solution)/shard_map/ppermute | solution.py:171
  23.4 7.5 %collective-permute-start.5 = (f32[2,128,128]{2,1,0:T(8,128)S(1)}, f32[2,128,128]{2,1,0:T(8,128)S(1)}, u32[]{:S(2)}, u32[]{:S(2)}) collective-permute-start(f32[2,128,128]{2,1,0:T(8,128)S(1)} %add_add_fusion.1), channel_id=1, source_target_pairs={{0,8},{2,10},{4,12},{6,14},{8,0},{10,2},{12,4},{14,6},{1,9},{3,11}... | collective-permute-start | bytes 393224 | tf_op jit(solution)/shard_map/ppermute | solution.py:171
  25.9 6.9 %collective-permute-start.12 = (f32[2,128,128]{2,1,0:T(8,128)S(1)}, f32[2,128,128]{2,1,0:T(8,128)S(1)}, u32[]{:S(2)}, u32[]{:S(2)}) collective-permute-start(f32[2,128,128]{2,1,0:T(8,128)S(1)} %get-tuple-element.67), channel_id=1, source_target_pairs={{0,4},{1,3},{2,6},{3,1},{4,0},{5,7},{6,2},{7,5},{8,12},{9,11},{10,... | collective-permute-start | bytes 393224 | tf_op jit(solution)/shard_map/ppermute | solution.py:190
  27.4 10.7 %collective-permute-start.13 = (f32[2,128,128]{2,1,0:T(8,128)S(1)}, f32[2,128,128]{2,1,0:T(8,128)S(1)}, u32[]{:S(2)}, u32[]{:S(2)}) collective-permute-start(f32[2,128,128]{2,1,0:T(8,128)S(1)} %get-tuple-element.68), channel_id=1, source_target_pairs={{0,2},{1,5},{2,0},{3,7},{4,6},{5,1},{6,4},{7,3},{8,10},{9,13},{10,... | collective-permute-start | bytes 393224 | tf_op jit(solution)/shard_map/ppermute | solution.py:190
  29.1 9.0 %collective-permute-start.14 = (f32[2,128,128]{2,1,0:T(8,128)S(1)}, f32[2,128,128]{2,1,0:T(8,128)S(1)}, u32[]{:S(2)}, u32[]{:S(2)}) collective-permute-start(f32[2,128,128]{2,1,0:T(8,128)S(1)} %get-tuple-element.69), channel_id=1, source_target_pairs={{0,6},{1,7},{2,4},{3,5},{4,2},{5,3},{6,0},{7,1},{8,14},{9,15},{10,... | collective-permute-start | bytes 393224 | tf_op jit(solution)/shard_map/ppermute | solution.py:190
  31.1 8.1 %collective-permute-start.6 = (f32[2,128,128]{2,1,0:T(8,128)S(1)}, f32[2,128,128]{2,1,0:T(8,128)S(1)}, u32[]{:S(2)}, u32[]{:S(2)}) collective-permute-start(f32[2,128,128]{2,1,0:T(8,128)S(1)} %get-tuple-element.58), channel_id=1, source_target_pairs={{0,4},{1,3},{2,6},{3,1},{4,0},{5,7},{6,2},{7,5},{8,12},{9,11},{10,... | collective-permute-start | bytes 393224 | tf_op jit(solution)/shard_map/ppermute | solution.py:190
  31.7 7.4 %collective-permute-start.7 = (f32[2,128,128]{2,1,0:T(8,128)S(1)}, f32[2,128,128]{2,1,0:T(8,128)S(1)}, u32[]{:S(2)}, u32[]{:S(2)}) collective-permute-start(f32[2,128,128]{2,1,0:T(8,128)S(1)} %get-tuple-element.59), channel_id=1, source_target_pairs={{0,2},{1,5},{2,0},{3,7},{4,6},{5,1},{6,4},{7,3},{8,10},{9,13},{10,... | collective-permute-start | bytes 393224 | tf_op jit(solution)/shard_map/ppermute | solution.py:190
  32.8 7.8 %collective-permute-start.8 = (f32[2,128,128]{2,1,0:T(8,128)S(1)}, f32[2,128,128]{2,1,0:T(8,128)S(1)}, u32[]{:S(2)}, u32[]{:S(2)}) collective-permute-start(f32[2,128,128]{2,1,0:T(8,128)S(1)} %get-tuple-element.60), channel_id=1, source_target_pairs={{0,6},{1,7},{2,4},{3,5},{4,2},{5,3},{6,0},{7,1},{8,14},{9,15},{10,... | collective-permute-start | bytes 393224 | tf_op jit(solution)/shard_map/ppermute | solution.py:190

commit v6 on v4

--- a/solution.py
+++ b/solution.py
@@ -11,10 +11,10 @@
 QUAD = 4
 SPLIT = (2, 2)
 STEPS = (2, 1, 3, 0)
-FINALS = ((0, (2, 1, 3, 0)), (1, (0, 2, 1)), (1, (3,)))
 CALLS = (
-    (((0, 1), (0, 2), (0, 3), (0, 0)), None),
-    (((1, 3), (1, 2), (1, 1), (1, 0)), (0, 2)),
+    (((0, 2),), None),
+    (((0, 1), (0, 3), (0, 0)), None),
+    (((1, 2), (1, 1), (1, 3), (1, 0)), (0, 2)),
 )
 VMEM = pl.BlockSpec(memory_space=pltpu.VMEM)
 ANY = pl.BlockSpec(memory_space=pl.ANY)
@@ -141,22 +141,21 @@
                 value_refs[part][:, slot] = dot(probs_ref[:, at], g, TN)
 
 
-def final_kernel(each, start, count, steps, k_ref, v_ref, key_in, value_in, *refs):
-    later_refs = refs[: len(steps)]
+def final_kernel(each, start, count, k_ref, v_ref, key_in, value_in, *refs):
+    later_refs = refs[:QUAD]
     key_hbm, value_hbm, key_ref, value_ref, sems = refs[-5:]
     me = lax.rem(lax.axis_index("ctx"), QUAD)
     copies = []
-    for index, step in enumerate(steps):
+    for index, step in enumerate(STEPS):
+        slots = columns(index * count, count)
         for local in range(count):
             at = columns((me ^ step) * each + start + local)
-            source = columns(STEPS.index(step) * count + local)
             slot = columns(index * count + local)
             later = later_refs[index][local].astype(jnp.bfloat16)
-            key = key_in[:, source] + dot(v_ref[:, at], later, NT)
+            key = key_in[:, slot] + dot(v_ref[:, at], later, NT)
             key_ref[:, slot] = key.astype(jnp.bfloat16)
-            value = value_in[:, source] + dot(k_ref[:, at], later, NN)
+            value = value_in[:, slot] + dot(k_ref[:, at], later, NN)
             value_ref[:, slot] = value.astype(jnp.bfloat16)
-        slots = columns(index * count, count)
         at = columns((me ^ step) * each + start, count)
         for pair, (source, target) in enumerate(((key_ref, key_hbm), (value_ref, value_hbm))):
             copy = pltpu.make_async_copy(source.at[:, slots], target.at[:, at], sems.at[index, pair])
@@ -258,19 +257,17 @@
         compiler_params=params(8),
     )(q, k, v, s, probs, *grads)
     done = ()
-    for part, steps in FINALS:
-        start, count = parts[part]
-        stage = pltpu.VMEM((rows, len(steps) * count * HEAD), jnp.bfloat16)
-        pieces = [later[part][STEPS.index(step)] for step in steps]
+    for part, (start, count) in enumerate(parts):
+        stage = pltpu.VMEM((rows, QUAD * count * HEAD), jnp.bfloat16)
         done = pl.pallas_call(
-            functools.partial(final_kernel, each, start, count, steps),
+            functools.partial(final_kernel, each, start, count),
             out_shape=(half, half),
-            in_specs=[VMEM] * (4 + len(steps)) + [HBM] * len(done),
+            in_specs=[VMEM] * (4 + QUAD) + [HBM] * len(done),
             out_specs=(HBM,) * 2,
             scratch_shapes=[stage, stage, pltpu.SemaphoreType.DMA((QUAD, 2))],
-            input_output_aliases={4 + len(steps) + index: index for index in range(len(done))},
+            input_output_aliases={4 + QUAD + index: index for index in range(len(done))},
             compiler_params=params(8),
-        )(k, v, local[part], local[len(parts) + part], *pieces, *done)
+        )(k, v, local[part], local[len(parts) + part], *later[part], *done)
     return (grad_query, *done)
 
 

time: 41.8 us -> 41.8 us (level)
  starting transfers between devices: 21.1 us -> 21.9 us
  Pallas kernels: 9.92 us -> 9.34 us
    pallas_call x3 -> x2, Pallas kernels: 3.03 us -> 2.21 us  [per_device(): pl.pallas_call(functools.partial(final_kernel, each, start, count), out_s...]
    ppermute x15, starting transfers between devices: 21.1 us -> 21.9 us  [partner(): lax.ppermute(value, axis, [(source, source ^ mask) for source in range(co...]
    pallas_call x2 -> x3, Pallas kernels: 0.9 us -> 1.14 us  [per_device(): pl.pallas_call(functools.partial(state_kernel, features, each, parts, pie...]
  transfers between devices with their start and end apart: 15 -> 15, of which waited for: 9 -> 10; matrix products, arithmetic and copies ran while one was open for 0% -> 0% of each run, Pallas kernels for 15% -> 14%
where the time goes in v6:
time: 41.8 us; the launch traced here: 41.6 us
  starting transfers between devices  21.9 us (52%)
  waiting for transfers between devices  9.66 us (23%)
  Pallas kernels  9.34 us (22%)
  between operations  0.7 us (2%)
    ppermute x15, starting transfers between devices, partner(): lax.ppermute(value, axis, [(source, source ^ mask) for source in range(co...  21.9 us
    ppermute x15, waiting for transfers between devices, partner(): lax.ppermute(value, axis, [(source, source ^ mask) for source in range(co...  9.66 us
    pallas_call x1, Pallas kernels, per_device(): pl.pallas_call(functools.partial(local_kernel, each, parts), out_shape=(h...  3.39 us
    pallas_call x1, Pallas kernels, per_device(): pl.pallas_call(forward_kernel, out_shape=(near((rows, width), jnp.float32...  2.32 us
    pallas_call x2, Pallas kernels, per_device(): pl.pallas_call(functools.partial(final_kernel, each, start, count), out_s...  2.21 us
    pallas_call x3, Pallas kernels, per_device(): pl.pallas_call(functools.partial(state_kernel, features, each, parts, pie...  1.14 us
  transfers between devices with their start and end apart: 15, of which 10 were waited for; matrix products, arithmetic and copies ran while one was open for 0% of the time, Pallas kernels for 14%

profile of v6, /device:TPU:0, one launch (start us, length us, event | category | flops | bytes accessed | tf_op | source)
XLA Modules:
  0.0 41.6 jit_solution(17500275008653317904)
XLA Ops:
  0.6 2.3 %shard_map.85 = (f32[128,2048]{1,0:T(8,128)S(1)}, bf16[128,2048]{1,0:T(8,128)(2,1)S(1)}, f32[128,128]{1,0:T(8,128)S(1)}, bf16[128,2048]{1,0:T(8,128)(2,1)S(1)}, ...) custom-call(bf16[128,2048]{1,0:T(8,128)(2,1)} %q_hbm.1, ...), custom_call_target="tpu_custom_call" | custom-call | tf_op jit(solution)/shard_map/pallas_call | solution.py:195
  3.0 0.5 %collective-permute-start = (f32[128,128]{1,0:T(8,128)S(1)}, f32[128,128]{1,0:T(8,128)S(1)}, u32[]{:S(2)}, u32[]{:S(2)}) collective-permute-start(f32[128,128]{1,0:T(8,128)S(1)} %get-tuple-element.45.own_ref), channel_id=1, source_target_pairs={{0,1},{1,0},{2,3},{3,2},{4,5},{5,4},{6,7},{7,6},{8,9},{9,8},{10,11... | collective-permute-start | bytes 196616 | tf_op jit(solution)/shard_map/ppermute | solution.py:174
  3.5 0.9 %collective-permute-done.other_ref = f32[128,128]{1,0:T(8,128)S(1)} collective-permute-done((f32[128,128]{1,0:T(8,128)S(1)}, f32[128,128]{1,0:T(8,128)S(1)}, u32[]{:S(2)}, u32[]{:S(2)}) %collective-permute-start) | collective-permute-done | bytes 65568 | tf_op jit(solution)/shard_map/ppermute | solution.py:174
  4.4 0.3 shard_map.86
  4.7 3.0 %collective-permute-start.1 = (f32[2,128,128]{2,1,0:T(8,128)S(1)}, f32[2,128,128]{2,1,0:T(8,128)S(1)}, u32[]{:S(2)}, u32[]{:S(2)}) collective-permute-start(f32[2,128,128]{2,1,0:T(8,128)S(1)} %get-tuple-element.51), channel_id=1, source_target_pairs={{0,4},{2,6},{4,0},{6,2},{8,12},{10,14},{12,8},{14,10},{1,5},{3,7},... | collective-permute-start | bytes 393224 | tf_op jit(solution)/shard_map/ppermute | solution.py:174
  7.7 0.4 shard_map.87
  8.1 1.6 %collective-permute-start.9 = (f32[2,128,128]{2,1,0:T(8,128)S(1)}, f32[2,128,128]{2,1,0:T(8,128)S(1)}, u32[]{:S(2)}, u32[]{:S(2)}) collective-permute-start(f32[2,128,128]{2,1,0:T(8,128)S(1)} %get-tuple-element.66), channel_id=1, source_target_pairs={{0,2},{2,0},{4,6},{6,4},{8,10},{10,8},{12,14},{14,12},{1,3},{3,1},... | collective-permute-start | bytes 393224 | tf_op jit(solution)/shard_map/ppermute | solution.py:174
  9.6 0.0 collective-permute-start.10
  9.6 1.9 %collective-permute-done.1.refs_0_ = f32[2,128,128]{2,1,0:T(8,128)S(1)} collective-permute-done((f32[2,128,128]{2,1,0:T(8,128)S(1)}, f32[2,128,128]{2,1,0:T(8,128)S(1)}, u32[]{:S(2)}, u32[]{:S(2)}) %collective-permute-start.1) | collective-permute-done | bytes 131104 | tf_op jit(solution)/shard_map/ppermute | solution.py:174
  11.5 0.5 %shard_map.88 = (bf16[128,1024]{1,0:T(8,128)(2,1)S(1)}, f32[2,128,128]{2,1,0:T(8,128)S(1)}, f32[2,128,128]{2,1,0:T(8,128)S(1)}, f32[2,128,128]{2,1,0:T(8,128)S(1)}, f32[2,128,128]{2,1,0:T(8,128)S(1)}) custom-call(f32[128,128]{1,0:T(8,128)S(1)} %get-tuple-element.45.own_ref, f32[128,128]{1,0:T(8,128)S(1)} %collective-permute-done.other_ref, ...), custom_call_target="tpu_custom_call" | custom-call | tf_op jit(solution)/shard_map/pallas_call | solution.py:220
  12.0 2.5 %collective-permute-start.2 = (f32[2,128,128]{2,1,0:T(8,128)S(1)}, f32[2,128,128]{2,1,0:T(8,128)S(1)}, u32[]{:S(2)}, u32[]{:S(2)}) collective-permute-start(f32[2,128,128]{2,1,0:T(8,128)S(1)} %get-tuple-element.56), channel_id=1, source_target_pairs={{0,4},{2,6},{4,0},{6,2},{8,12},{10,14},{12,8},{14,10},{1,5},{3,7},... | collective-permute-start | bytes 393224 | tf_op jit(solution)/shard_map/ppermute | solution.py:174
  14.5 1.5 %collective-permute-start.3 = (f32[2,128,128]{2,1,0:T(8,128)S(1)}, f32[2,128,128]{2,1,0:T(8,128)S(1)}, u32[]{:S(2)}, u32[]{:S(2)}) collective-permute-start(f32[2,128,128]{2,1,0:T(8,128)S(1)} %get-tuple-element.57), channel_id=1, source_target_pairs={{0,2},{2,0},{4,6},{6,4},{8,10},{10,8},{12,14},{14,12},{1,3},{3,1},... | collective-permute-start | bytes 393224 | tf_op jit(solution)/shard_map/ppermute | solution.py:174
  16.0 0.1 collective-permute-start.4
  16.1 0.5 %collective-permute-done.9.refs_1_ = f32[2,128,128]{2,1,0:T(8,128)S(1)} collective-permute-done((f32[2,128,128]{2,1,0:T(8,128)S(1)}, f32[2,128,128]{2,1,0:T(8,128)S(1)}, u32[]{:S(2)}, u32[]{:S(2)}) %collective-permute-start.9) | collective-permute-done | bytes 131104 | tf_op jit(solution)/shard_map/ppermute | solution.py:174
  16.6 0.0 collective-permute-done.10.refs_2_
  16.7 2.7 %collective-permute-start.11 = (f32[2,128,128]{2,1,0:T(8,128)S(1)}, f32[2,128,128]{2,1,0:T(8,128)S(1)}, u32[]{:S(2)}, u32[]{:S(2)}) collective-permute-start(f32[2,128,128]{2,1,0:T(8,128)S(1)} %add_add_fusion), channel_id=1, source_target_pairs={{0,8},{2,10},{4,12},{6,14},{8,0},{10,2},{12,4},{14,6},{1,9},{3,11}... | collective-permute-start | bytes 393224 | tf_op jit(solution)/shard_map/ppermute | solution.py:174
  19.3 0.6 %collective-permute-done.2.refs_0_ = f32[2,128,128]{2,1,0:T(8,128)S(1)} collective-permute-done((f32[2,128,128]{2,1,0:T(8,128)S(1)}, f32[2,128,128]{2,1,0:T(8,128)S(1)}, u32[]{:S(2)}, u32[]{:S(2)}) %collective-permute-start.2) | collective-permute-done | bytes 131104 | tf_op jit(solution)/shard_map/ppermute | solution.py:174
  19.9 0.7 %collective-permute-done.3.refs_1_ = f32[2,128,128]{2,1,0:T(8,128)S(1)} collective-permute-done((f32[2,128,128]{2,1,0:T(8,128)S(1)}, f32[2,128,128]{2,1,0:T(8,128)S(1)}, u32[]{:S(2)}, u32[]{:S(2)}) %collective-permute-start.3) | collective-permute-done | bytes 131104 | tf_op jit(solution)/shard_map/ppermute | solution.py:174
  20.6 2.0 %collective-permute-done.4.refs_2_ = f32[2,128,128]{2,1,0:T(8,128)S(1)} collective-permute-done((f32[2,128,128]{2,1,0:T(8,128)S(1)}, f32[2,128,128]{2,1,0:T(8,128)S(1)}, u32[]{:S(2)}, u32[]{:S(2)}) %collective-permute-start.4) | collective-permute-done | bytes 131104 | tf_op jit(solution)/shard_map/ppermute | solution.py:174
  22.7 3.2 %collective-permute-start.5 = (f32[2,128,128]{2,1,0:T(8,128)S(1)}, f32[2,128,128]{2,1,0:T(8,128)S(1)}, u32[]{:S(2)}, u32[]{:S(2)}) collective-permute-start(f32[2,128,128]{2,1,0:T(8,128)S(1)} %add_add_fusion.1), channel_id=1, source_target_pairs={{0,8},{2,10},{4,12},{6,14},{8,0},{10,2},{12,4},{14,6},{1,9},{3,11}... | collective-permute-start | bytes 393224 | tf_op jit(solution)/shard_map/ppermute | solution.py:174
  25.9 1.0 %collective-permute-done.11.refs_4_ = f32[2,128,128]{2,1,0:T(8,128)S(1)} collective-permute-done((f32[2,128,128]{2,1,0:T(8,128)S(1)}, f32[2,128,128]{2,1,0:T(8,128)S(1)}, u32[]{:S(2)}, u32[]{:S(2)}) %collective-permute-start.11) | collective-permute-done | bytes 131104 | tf_op jit(solution)/shard_map/ppermute | solution.py:174
  26.9 0.1 shard_map.91
  27.1 0.6 %collective-permute-start.12 = (f32[2,128,128]{2,1,0:T(8,128)S(1)}, f32[2,128,128]{2,1,0:T(8,128)S(1)}, u32[]{:S(2)}, u32[]{:S(2)}) collective-permute-start(f32[2,128,128]{2,1,0:T(8,128)S(1)} %get-tuple-element.69), channel_id=1, source_target_pairs={{0,4},{2,6},{4,0},{6,2},{8,12},{10,14},{12,8},{14,10},{1,5},{3,7},... | collective-permute-start | bytes 393224 | tf_op jit(solution)/shard_map/ppermute | solution.py:174
  27.7 1.3 %collective-permute-start.13 = (f32[2,128,128]{2,1,0:T(8,128)S(1)}, f32[2,128,128]{2,1,0:T(8,128)S(1)}, u32[]{:S(2)}, u32[]{:S(2)}) collective-permute-start(f32[2,128,128]{2,1,0:T(8,128)S(1)} %get-tuple-element.70), channel_id=1, source_target_pairs={{0,2},{2,0},{4,6},{6,4},{8,10},{10,8},{12,14},{14,12},{1,3},{3,1},... | collective-permute-start | bytes 393224 | tf_op jit(solution)/shard_map/ppermute | solution.py:174
  29.0 1.6 %collective-permute-start.14 = (f32[2,128,128]{2,1,0:T(8,128)S(1)}, f32[2,128,128]{2,1,0:T(8,128)S(1)}, u32[]{:S(2)}, u32[]{:S(2)}) collective-permute-start(f32[2,128,128]{2,1,0:T(8,128)S(1)} %get-tuple-element.71), channel_id=1, source_target_pairs={{0,6},{2,4},{4,2},{6,0},{8,14},{10,12},{12,10},{14,8},{1,7},{3,5},... | collective-permute-start | bytes 393224 | tf_op jit(solution)/shard_map/ppermute | solution.py:174
  30.6 0.0 collective-permute-done.5.refs_4_
  30.6 0.1 shard_map.90
  30.8 0.9 %collective-permute-start.6 = (f32[2,128,128]{2,1,0:T(8,128)S(1)}, f32[2,128,128]{2,1,0:T(8,128)S(1)}, u32[]{:S(2)}, u32[]{:S(2)}) collective-permute-start(f32[2,128,128]{2,1,0:T(8,128)S(1)} %get-tuple-element.60), channel_id=1, source_target_pairs={{0,4},{2,6},{4,0},{6,2},{8,12},{10,14},{12,8},{14,10},{1,5},{3,7},... | collective-permute-start | bytes 393224 | tf_op jit(solution)/shard_map/ppermute | solution.py:174
  31.7 1.1 %collective-permute-start.7 = (f32[2,128,128]{2,1,0:T(8,128)S(1)}, f32[2,128,128]{2,1,0:T(8,128)S(1)}, u32[]{:S(2)}, u32[]{:S(2)}) collective-permute-start(f32[2,128,128]{2,1,0:T(8,128)S(1)} %get-tuple-element.61), channel_id=1, source_target_pairs={{0,2},{2,0},{4,6},{6,4},{8,10},{10,8},{12,14},{14,12},{1,3},{3,1},... | collective-permute-start | bytes 393224 | tf_op jit(solution)/shard_map/ppermute | solution.py:174
  32.8 0.3 collective-permute-done.12.refs_0_
  33.1 1.3 %collective-permute-start.8 = (f32[2,128,128]{2,1,0:T(8,128)S(1)}, f32[2,128,128]{2,1,0:T(8,128)S(1)}, u32[]{:S(2)}, u32[]{:S(2)}) collective-permute-start(f32[2,128,128]{2,1,0:T(8,128)S(1)} %get-tuple-element.62), channel_id=1, source_target_pairs={{0,6},{2,4},{4,2},{6,0},{8,14},{10,12},{12,10},{14,8},{1,7},{3,5},... | collective-permute-start | bytes 393224 | tf_op jit(solution)/shard_map/ppermute | solution.py:174
  34.3 3.4 %shard_map.89 = (bf16[128,2048]{1,0:T(8,128)(2,1)}, f32[128,1024]{1,0:T(8,128)S(1)}, f32[128,1024]{1,0:T(8,128)S(1)}, f32[128,1024]{1,0:T(8,128)S(1)}, f32[128,1024]{1,0:T(8,128)S(1)}) custom-call(bf16[128,2048]{1,0:T(8,128)(2,1)S(1)} %get-tuple-element.40.q_ref, bf16[128,2048]{1,0:T(8,128)(2,1)S(1)} %get-tuple-element.41.k_ref, ...), custom_call_target="tpu_custom_call" | custom-call | tf_op jit(solution)/shard_map/pallas_call | solution.py:252
  37.7 0.0 collective-permute-done.13.refs_1_
  37.7 0.0 collective-permute-done.14.refs_2_
  37.7 1.1 %shard_map.92 = (bf16[128,2048]{1,0:T(8,128)(2,1)}, bf16[128,2048]{1,0:T(8,128)(2,1)}) custom-call(bf16[128,2048]{1,0:T(8,128)(2,1)S(1)} %get-tuple-element.41.k_ref, bf16[128,2048]{1,0:T(8,128)(2,1)S(1)} %get-tuple-element.42.v_ref, f32[128,1024]{1,0:T(8,128)S(1)} %get-tuple-element.64.key_in, f32[128,1024]{1,0:T(8,128)S(1)} %get-tuple-element.65.value_in, ...), custom_call_target="tpu_custom_call" | custom-call | tf_op jit(solution)/shard_map/pallas_call | solution.py:262
  38.8 0.0 collective-permute-done.6.refs_0_
  38.8 0.7 %collective-permute-done.7.refs_1_ = f32[2,128,128]{2,1,0:T(8,128)S(1)} collective-permute-done((f32[2,128,128]{2,1,0:T(8,128)S(1)}, f32[2,128,128]{2,1,0:T(8,128)S(1)}, u32[]{:S(2)}, u32[]{:S(2)}) %collective-permute-start.7) | collective-permute-done | bytes 131104 | tf_op jit(solution)/shard_map/ppermute | solution.py:174
  39.5 1.0 %collective-permute-done.8.refs_2_ = f32[2,128,128]{2,1,0:T(8,128)S(1)} collective-permute-done((f32[2,128,128]{2,1,0:T(8,128)S(1)}, f32[2,128,128]{2,1,0:T(8,128)S(1)}, u32[]{:S(2)}, u32[]{:S(2)}) %collective-permute-start.8) | collective-permute-done | bytes 131104 | tf_op jit(solution)/shard_map/ppermute | solution.py:174
  40.5 1.1 %shard_map.93 = (bf16[128,2048]{1,0:T(8,128)(2,1)}, bf16[128,2048]{1,0:T(8,128)(2,1)}) custom-call(bf16[128,2048]{1,0:T(8,128)(2,1)S(1)} %get-tuple-element.41.k_ref, bf16[128,2048]{1,0:T(8,128)(2,1)S(1)} %get-tuple-element.42.v_ref, f32[128,1024]{1,0:T(8,128)S(1)} %get-tuple-element.54.key_in, ...), custom_call_target="tpu_custom_call", output_to_operand_aliasing={{0}: (8, {}), {1}: (9, {})} | custom-call | tf_op jit(solution)/shard_map/pallas_call | solution.py:262
  (2 shorter events, 0.1 us)
Async XLA Ops:
  3.0 1.4 %collective-permute-start = (f32[128,128]{1,0:T(8,128)S(1)}, f32[128,128]{1,0:T(8,128)S(1)}, u32[]{:S(2)}, u32[]{:S(2)}) collective-permute-start(f32[128,128]{1,0:T(8,128)S(1)} %get-tuple-element.45.own_ref), channel_id=1, source_target_pairs={{0,1},{1,0},{2,3},{3,2},{4,5},{5,4},{6,7},{7,6},{8,9},{9,8},{10,11... | collective-permute-start | bytes 196616 | tf_op jit(solution)/shard_map/ppermute | solution.py:174
  4.7 6.9 %collective-permute-start.1 = (f32[2,128,128]{2,1,0:T(8,128)S(1)}, f32[2,128,128]{2,1,0:T(8,128)S(1)}, u32[]{:S(2)}, u32[]{:S(2)}) collective-permute-start(f32[2,128,128]{2,1,0:T(8,128)S(1)} %get-tuple-element.51), channel_id=1, source_target_pairs={{0,4},{2,6},{4,0},{6,2},{8,12},{10,14},{12,8},{14,10},{1,5},{3,7},... | collective-permute-start | bytes 393224 | tf_op jit(solution)/shard_map/ppermute | solution.py:174
  8.1 8.6 %collective-permute-start.9 = (f32[2,128,128]{2,1,0:T(8,128)S(1)}, f32[2,128,128]{2,1,0:T(8,128)S(1)}, u32[]{:S(2)}, u32[]{:S(2)}) collective-permute-start(f32[2,128,128]{2,1,0:T(8,128)S(1)} %get-tuple-element.66), channel_id=1, source_target_pairs={{0,2},{2,0},{4,6},{6,4},{8,10},{10,8},{12,14},{14,12},{1,3},{3,1},... | collective-permute-start | bytes 393224 | tf_op jit(solution)/shard_map/ppermute | solution.py:174
  9.6 7.0 %collective-permute-start.10 = (f32[2,128,128]{2,1,0:T(8,128)S(1)}, f32[2,128,128]{2,1,0:T(8,128)S(1)}, u32[]{:S(2)}, u32[]{:S(2)}) collective-permute-start(f32[2,128,128]{2,1,0:T(8,128)S(1)} %get-tuple-element.67), channel_id=1, source_target_pairs={{0,6},{2,4},{4,2},{6,0},{8,14},{10,12},{12,10},{14,8},{1,7},{3,5},... | collective-permute-start | bytes 393224 | tf_op jit(solution)/shard_map/ppermute | solution.py:174
  12.0 7.9 %collective-permute-start.2 = (f32[2,128,128]{2,1,0:T(8,128)S(1)}, f32[2,128,128]{2,1,0:T(8,128)S(1)}, u32[]{:S(2)}, u32[]{:S(2)}) collective-permute-start(f32[2,128,128]{2,1,0:T(8,128)S(1)} %get-tuple-element.56), channel_id=1, source_target_pairs={{0,4},{2,6},{4,0},{6,2},{8,12},{10,14},{12,8},{14,10},{1,5},{3,7},... | collective-permute-start | bytes 393224 | tf_op jit(solution)/shard_map/ppermute | solution.py:174
  14.5 6.0 %collective-permute-start.3 = (f32[2,128,128]{2,1,0:T(8,128)S(1)}, f32[2,128,128]{2,1,0:T(8,128)S(1)}, u32[]{:S(2)}, u32[]{:S(2)}) collective-permute-start(f32[2,128,128]{2,1,0:T(8,128)S(1)} %get-tuple-element.57), channel_id=1, source_target_pairs={{0,2},{2,0},{4,6},{6,4},{8,10},{10,8},{12,14},{14,12},{1,3},{3,1},... | collective-permute-start | bytes 393224 | tf_op jit(solution)/shard_map/ppermute | solution.py:174
  16.0 6.6 %collective-permute-start.4 = (f32[2,128,128]{2,1,0:T(8,128)S(1)}, f32[2,128,128]{2,1,0:T(8,128)S(1)}, u32[]{:S(2)}, u32[]{:S(2)}) collective-permute-start(f32[2,128,128]{2,1,0:T(8,128)S(1)} %get-tuple-element.58), channel_id=1, source_target_pairs={{0,6},{2,4},{4,2},{6,0},{8,14},{10,12},{12,10},{14,8},{1,7},{3,5},... | collective-permute-start | bytes 393224 | tf_op jit(solution)/shard_map/ppermute | solution.py:174
  16.7 10.3 %collective-permute-start.11 = (f32[2,128,128]{2,1,0:T(8,128)S(1)}, f32[2,128,128]{2,1,0:T(8,128)S(1)}, u32[]{:S(2)}, u32[]{:S(2)}) collective-permute-start(f32[2,128,128]{2,1,0:T(8,128)S(1)} %add_add_fusion), channel_id=1, source_target_pairs={{0,8},{2,10},{4,12},{6,14},{8,0},{10,2},{12,4},{14,6},{1,9},{3,11}... | collective-permute-start | bytes 393224 | tf_op jit(solution)/shard_map/ppermute | solution.py:174
  22.7 7.9 %collective-permute-start.5 = (f32[2,128,128]{2,1,0:T(8,128)S(1)}, f32[2,128,128]{2,1,0:T(8,128)S(1)}, u32[]{:S(2)}, u32[]{:S(2)}) collective-permute-start(f32[2,128,128]{2,1,0:T(8,128)S(1)} %add_add_fusion.1), channel_id=1, source_target_pairs={{0,8},{2,10},{4,12},{6,14},{8,0},{10,2},{12,4},{14,6},{1,9},{3,11}... | collective-permute-start | bytes 393224 | tf_op jit(solution)/shard_map/ppermute | solution.py:174
  27.1 6.0 %collective-permute-start.12 = (f32[2,128,128]{2,1,0:T(8,128)S(1)}, f32[2,128,128]{2,1,0:T(8,128)S(1)}, u32[]{:S(2)}, u32[]{:S(2)}) collective-permute-start(f32[2,128,128]{2,1,0:T(8,128)S(1)} %get-tuple-element.69), channel_id=1, source_target_pairs={{0,4},{2,6},{4,0},{6,2},{8,12},{10,14},{12,8},{14,10},{1,5},{3,7},... | collective-permute-start | bytes 393224 | tf_op jit(solution)/shard_map/ppermute | solution.py:174
  27.7 10.0 %collective-permute-start.13 = (f32[2,128,128]{2,1,0:T(8,128)S(1)}, f32[2,128,128]{2,1,0:T(8,128)S(1)}, u32[]{:S(2)}, u32[]{:S(2)}) collective-permute-start(f32[2,128,128]{2,1,0:T(8,128)S(1)} %get-tuple-element.70), channel_id=1, source_target_pairs={{0,2},{2,0},{4,6},{6,4},{8,10},{10,8},{12,14},{14,12},{1,3},{3,1},... | collective-permute-start | bytes 393224 | tf_op jit(solution)/shard_map/ppermute | solution.py:174
  29.0 8.7 %collective-permute-start.14 = (f32[2,128,128]{2,1,0:T(8,128)S(1)}, f32[2,128,128]{2,1,0:T(8,128)S(1)}, u32[]{:S(2)}, u32[]{:S(2)}) collective-permute-start(f32[2,128,128]{2,1,0:T(8,128)S(1)} %get-tuple-element.71), channel_id=1, source_target_pairs={{0,6},{2,4},{4,2},{6,0},{8,14},{10,12},{12,10},{14,8},{1,7},{3,5},... | collective-permute-start | bytes 393224 | tf_op jit(solution)/shard_map/ppermute | solution.py:174
  30.8 8.1 %collective-permute-start.6 = (f32[2,128,128]{2,1,0:T(8,128)S(1)}, f32[2,128,128]{2,1,0:T(8,128)S(1)}, u32[]{:S(2)}, u32[]{:S(2)}) collective-permute-start(f32[2,128,128]{2,1,0:T(8,128)S(1)} %get-tuple-element.60), channel_id=1, source_target_pairs={{0,4},{2,6},{4,0},{6,2},{8,12},{10,14},{12,8},{14,10},{1,5},{3,7},... | collective-permute-start | bytes 393224 | tf_op jit(solution)/shard_map/ppermute | solution.py:174
  31.7 7.8 %collective-permute-start.7 = (f32[2,128,128]{2,1,0:T(8,128)S(1)}, f32[2,128,128]{2,1,0:T(8,128)S(1)}, u32[]{:S(2)}, u32[]{:S(2)}) collective-permute-start(f32[2,128,128]{2,1,0:T(8,128)S(1)} %get-tuple-element.61), channel_id=1, source_target_pairs={{0,2},{2,0},{4,6},{6,4},{8,10},{10,8},{12,14},{14,12},{1,3},{3,1},... | collective-permute-start | bytes 393224 | tf_op jit(solution)/shard_map/ppermute | solution.py:174
  33.1 7.5 %collective-permute-start.8 = (f32[2,128,128]{2,1,0:T(8,128)S(1)}, f32[2,128,128]{2,1,0:T(8,128)S(1)}, u32[]{:S(2)}, u32[]{:S(2)}) collective-permute-start(f32[2,128,128]{2,1,0:T(8,128)S(1)} %get-tuple-element.62), channel_id=1, source_target_pairs={{0,6},{2,4},{4,2},{6,0},{8,14},{10,12},{12,10},{14,8},{1,7},{3,5},... | collective-permute-start | bytes 393224 | tf_op jit(solution)/shard_map/ppermute | solution.py:174

commit v7 on v6

--- a/solution.py
+++ b/solution.py
@@ -32,6 +32,11 @@
     if isinstance(head, int):
         return pl.ds(head * HEAD, count * HEAD)
     return pl.ds(pl.multiple_of(head * HEAD, HEAD), count * HEAD)
+
+
+def turn(step):
+    core = lax.rem(lax.axis_index("tp"), 2)
+    return {0: 0, 1: 1 + core, 2: 2 - core, 3: 3}[step]
 
 
 def lower(rows):
@@ -114,8 +119,7 @@
     for target, step in enumerate(STEPS):
         value = behind
         for source, other in enumerate(STEPS):
-            if source != target:
-                value += jnp.where((me ^ other) > (me ^ step), blocks[source], 0.0)
+            value += jnp.where((me ^ other) > (me ^ turn(step)), blocks[source], 0.0)
         sum_refs[target][...] = value
 
 
@@ -149,14 +153,16 @@
     for index, step in enumerate(STEPS):
         slots = columns(index * count, count)
         for local in range(count):
-            at = columns((me ^ step) * each + start + local)
+            at = columns((me ^ turn(step)) * each + start + local)
             slot = columns(index * count + local)
+            held = index if index > 1 else lax.rem(lax.axis_index("tp") + index, 2)
+            source = columns(held * count + local)
             later = later_refs[index][local].astype(jnp.bfloat16)
-            key = key_in[:, slot] + dot(v_ref[:, at], later, NT)
+            key = key_in[:, source] + dot(v_ref[:, at], later, NT)
             key_ref[:, slot] = key.astype(jnp.bfloat16)
-            value = value_in[:, slot] + dot(k_ref[:, at], later, NN)
+            value = value_in[:, source] + dot(k_ref[:, at], later, NN)
             value_ref[:, slot] = value.astype(jnp.bfloat16)
-        at = columns((me ^ step) * each + start, count)
+        at = columns((me ^ turn(step)) * each + start, count)
         for pair, (source, target) in enumerate(((key_ref, key_hbm), (value_ref, value_hbm))):
             copy = pltpu.make_async_copy(source.at[:, slots], target.at[:, at], sems.at[index, pair])
             copy.start()
@@ -178,6 +184,20 @@
     return [
         partner(piece, "ctx", step) if step else piece for piece, step in zip(pieces, STEPS)
     ]
+
+
+def return_swap(pieces):
+    cores = lax.axis_size("tp")
+    places = range(lax.axis_size("ctx"))
+    came = []
+    for piece, step in zip(pieces, STEPS):
+        pairs = []
+        for place in places:
+            for core in range(cores):
+                other = {0: 0, 1: 1 + core % 2, 2: 2 - core % 2, 3: 3}[step]
+                pairs.append((place * cores + core, (place ^ other) * cores + core))
+        came.append(lax.ppermute(piece, ("ctx", "tp"), pairs) if step else piece)
+    return came
 
 
 def per_device(queries, keys, values, grad_y, state_low, gain):
@@ -246,7 +266,7 @@
             out_specs=(VMEM,) * QUAD,
             compiler_params=params(8),
         )(*blocks, *behind)
-        later.append(quad_swap(sums))
+        later.append(return_swap(sums))
 
     slots = [near((rows, QUAD * count * HEAD), jnp.float32) for _, count in parts]
     grad_query, *local = pl.pallas_call(

time: 41.8 us -> 41.7 us (level)
    ppermute x0 -> x6, starting transfers between devices: none -> 7.11 us  [return_swap(): came.append(lax.ppermute(piece, ('ctx', 'tp'), pairs) if step else piece)]
    ppermute x15 -> x9, starting transfers between devices: 21.9 us -> 15 us  [partner(): lax.ppermute(value, axis, [(source, source ^ mask) for source in range(co...]
    ppermute x15 -> x9, waiting for transfers between devices: 9.66 us -> 7.79 us  [partner(): lax.ppermute(value, axis, [(source, source ^ mask) for source in range(co...]
    ppermute x0 -> x6, waiting for transfers between devices: none -> 1.51 us  [return_swap(): came.append(lax.ppermute(piece, ('ctx', 'tp'), pairs) if step else piece)]
  transfers between devices with their start and end apart: 15 -> 15, of which waited for: 10 -> 8; matrix products, arithmetic and copies ran while one was open for 0% -> 0% of each run, Pallas kernels for 14% -> 14%
where the time goes in v7:
time: 41.7 us; the launch traced here: 41.6 us
  starting transfers between devices  22.1 us (53%)
  Pallas kernels  9.37 us (22%)
  waiting for transfers between devices  9.3 us (22%)
  between operations  0.71 us (2%)
    ppermute x9, starting transfers between devices, partner(): lax.ppermute(value, axis, [(source, source ^ mask) for source in range(co...  15 us
    ppermute x9, waiting for transfers between devices, partner(): lax.ppermute(value, axis, [(source, source ^ mask) for source in range(co...  7.79 us
    ppermute x6, starting transfers between devices, return_swap(): came.append(lax.ppermute(piece, ('ctx', 'tp'), pairs) if step else piece)  7.11 us
    pallas_call x1, Pallas kernels, per_device(): pl.pallas_call(functools.partial(local_kernel, each, parts), out_shape=(h...  3.39 us
    pallas_call x1, Pallas kernels, per_device(): pl.pallas_call(forward_kernel, out_shape=(near((rows, width), jnp.float32...  2.32 us
    pallas_call x2, Pallas kernels, per_device(): pl.pallas_call(functools.partial(final_kernel, each, start, count), out_s...  2.2 us
    ppermute x6, waiting for transfers between devices, return_swap(): came.append(lax.ppermute(piece, ('ctx', 'tp'), pairs) if step else piece)  1.51 us
    pallas_call x3, Pallas kernels, per_device(): pl.pallas_call(functools.partial(state_kernel, features, each, parts, pie...  1.14 us
  transfers between devices with their start and end apart: 15, of which 8 were waited for; matrix products, arithmetic and copies ran while one was open for 0% of the time, Pallas kernels for 14%

profile of v7, /device:TPU:0, one launch (start us, length us, event | category | flops | bytes accessed | tf_op | source)
XLA Modules:
  0.0 41.6 jit_solution(438311661906816475)
XLA Ops:
  0.6 2.3 %shard_map.85 = (f32[128,2048]{1,0:T(8,128)S(1)}, bf16[128,2048]{1,0:T(8,128)(2,1)S(1)}, f32[128,128]{1,0:T(8,128)S(1)}, bf16[128,2048]{1,0:T(8,128)(2,1)S(1)}, ...) custom-call(bf16[128,2048]{1,0:T(8,128)(2,1)} %q_hbm.1, ...), custom_call_target="tpu_custom_call" | custom-call | tf_op jit(solution)/shard_map/pallas_call | solution.py:215
  3.0 0.5 %collective-permute-start = (f32[128,128]{1,0:T(8,128)S(1)}, f32[128,128]{1,0:T(8,128)S(1)}, u32[]{:S(2)}, u32[]{:S(2)}) collective-permute-start(f32[128,128]{1,0:T(8,128)S(1)} %get-tuple-element.45.own_ref), channel_id=1, source_target_pairs={{0,1},{1,0},{2,3},{3,2},{4,5},{5,4},{6,7},{7,6},{8,9},{9,8},{10,11... | collective-permute-start | bytes 196616 | tf_op jit(solution)/shard_map/ppermute | solution.py:180
  3.5 0.9 %collective-permute-done.other_ref = f32[128,128]{1,0:T(8,128)S(1)} collective-permute-done((f32[128,128]{1,0:T(8,128)S(1)}, f32[128,128]{1,0:T(8,128)S(1)}, u32[]{:S(2)}, u32[]{:S(2)}) %collective-permute-start) | collective-permute-done | bytes 65568 | tf_op jit(solution)/shard_map/ppermute | solution.py:180
  4.4 0.3 shard_map.86
  4.7 3.0 %collective-permute-start.1 = (f32[2,128,128]{2,1,0:T(8,128)S(1)}, f32[2,128,128]{2,1,0:T(8,128)S(1)}, u32[]{:S(2)}, u32[]{:S(2)}) collective-permute-start(f32[2,128,128]{2,1,0:T(8,128)S(1)} %get-tuple-element.51), channel_id=1, source_target_pairs={{0,4},{2,6},{4,0},{6,2},{8,12},{10,14},{12,8},{14,10},{1,5},{3,7},... | collective-permute-start | bytes 393224 | tf_op jit(solution)/shard_map/ppermute | solution.py:180
  7.7 0.4 shard_map.87
  8.1 1.6 %collective-permute-start.9 = (f32[2,128,128]{2,1,0:T(8,128)S(1)}, f32[2,128,128]{2,1,0:T(8,128)S(1)}, u32[]{:S(2)}, u32[]{:S(2)}) collective-permute-start(f32[2,128,128]{2,1,0:T(8,128)S(1)} %get-tuple-element.66), channel_id=1, source_target_pairs={{0,2},{2,0},{4,6},{6,4},{8,10},{10,8},{12,14},{14,12},{1,3},{3,1},... | collective-permute-start | bytes 393224 | tf_op jit(solution)/shard_map/ppermute | solution.py:180
  9.6 0.0 collective-permute-start.10
  9.6 1.9 %collective-permute-done.1.refs_0_ = f32[2,128,128]{2,1,0:T(8,128)S(1)} collective-permute-done((f32[2,128,128]{2,1,0:T(8,128)S(1)}, f32[2,128,128]{2,1,0:T(8,128)S(1)}, u32[]{:S(2)}, u32[]{:S(2)}) %collective-permute-start.1) | collective-permute-done | bytes 131104 | tf_op jit(solution)/shard_map/ppermute | solution.py:180
  11.5 0.5 %shard_map.88 = (bf16[128,1024]{1,0:T(8,128)(2,1)S(1)}, f32[2,128,128]{2,1,0:T(8,128)S(1)}, f32[2,128,128]{2,1,0:T(8,128)S(1)}, f32[2,128,128]{2,1,0:T(8,128)S(1)}, f32[2,128,128]{2,1,0:T(8,128)S(1)}) custom-call(f32[128,128]{1,0:T(8,128)S(1)} %get-tuple-element.45.own_ref, f32[128,128]{1,0:T(8,128)S(1)} %collective-permute-done.other_ref, ...), custom_call_target="tpu_custom_call" | custom-call | tf_op jit(solution)/shard_map/pallas_call | solution.py:240
  12.0 2.5 %collective-permute-start.2 = (f32[2,128,128]{2,1,0:T(8,128)S(1)}, f32[2,128,128]{2,1,0:T(8,128)S(1)}, u32[]{:S(2)}, u32[]{:S(2)}) collective-permute-start(f32[2,128,128]{2,1,0:T(8,128)S(1)} %get-tuple-element.56), channel_id=1, source_target_pairs={{0,4},{2,6},{4,0},{6,2},{8,12},{10,14},{12,8},{14,10},{1,5},{3,7},... | collective-permute-start | bytes 393224 | tf_op jit(solution)/shard_map/ppermute | solution.py:180
  14.5 1.5 %collective-permute-start.3 = (f32[2,128,128]{2,1,0:T(8,128)S(1)}, f32[2,128,128]{2,1,0:T(8,128)S(1)}, u32[]{:S(2)}, u32[]{:S(2)}) collective-permute-start(f32[2,128,128]{2,1,0:T(8,128)S(1)} %get-tuple-element.57), channel_id=1, source_target_pairs={{0,2},{2,0},{4,6},{6,4},{8,10},{10,8},{12,14},{14,12},{1,3},{3,1},... | collective-permute-start | bytes 393224 | tf_op jit(solution)/shard_map/ppermute | solution.py:180
  16.0 0.1 collective-permute-start.4
  16.1 0.5 %collective-permute-done.9.refs_1_ = f32[2,128,128]{2,1,0:T(8,128)S(1)} collective-permute-done((f32[2,128,128]{2,1,0:T(8,128)S(1)}, f32[2,128,128]{2,1,0:T(8,128)S(1)}, u32[]{:S(2)}, u32[]{:S(2)}) %collective-permute-start.9) | collective-permute-done | bytes 131104 | tf_op jit(solution)/shard_map/ppermute | solution.py:180
  16.6 0.0 collective-permute-done.10.refs_2_
  16.7 2.7 %collective-permute-start.11 = (f32[2,128,128]{2,1,0:T(8,128)S(1)}, f32[2,128,128]{2,1,0:T(8,128)S(1)}, u32[]{:S(2)}, u32[]{:S(2)}) collective-permute-start(f32[2,128,128]{2,1,0:T(8,128)S(1)} %add_add_fusion), channel_id=1, source_target_pairs={{0,8},{2,10},{4,12},{6,14},{8,0},{10,2},{12,4},{14,6},{1,9},{3,11}... | collective-permute-start | bytes 393224 | tf_op jit(solution)/shard_map/ppermute | solution.py:180
  19.3 0.6 %collective-permute-done.2.refs_0_ = f32[2,128,128]{2,1,0:T(8,128)S(1)} collective-permute-done((f32[2,128,128]{2,1,0:T(8,128)S(1)}, f32[2,128,128]{2,1,0:T(8,128)S(1)}, u32[]{:S(2)}, u32[]{:S(2)}) %collective-permute-start.2) | collective-permute-done | bytes 131104 | tf_op jit(solution)/shard_map/ppermute | solution.py:180
  19.9 0.7 %collective-permute-done.3.refs_1_ = f32[2,128,128]{2,1,0:T(8,128)S(1)} collective-permute-done((f32[2,128,128]{2,1,0:T(8,128)S(1)}, f32[2,128,128]{2,1,0:T(8,128)S(1)}, u32[]{:S(2)}, u32[]{:S(2)}) %collective-permute-start.3) | collective-permute-done | bytes 131104 | tf_op jit(solution)/shard_map/ppermute | solution.py:180
  20.6 2.0 %collective-permute-done.4.refs_2_ = f32[2,128,128]{2,1,0:T(8,128)S(1)} collective-permute-done((f32[2,128,128]{2,1,0:T(8,128)S(1)}, f32[2,128,128]{2,1,0:T(8,128)S(1)}, u32[]{:S(2)}, u32[]{:S(2)}) %collective-permute-start.4) | collective-permute-done | bytes 131104 | tf_op jit(solution)/shard_map/ppermute | solution.py:180
  22.7 3.2 %collective-permute-start.5 = (f32[2,128,128]{2,1,0:T(8,128)S(1)}, f32[2,128,128]{2,1,0:T(8,128)S(1)}, u32[]{:S(2)}, u32[]{:S(2)}) collective-permute-start(f32[2,128,128]{2,1,0:T(8,128)S(1)} %add_add_fusion.1), channel_id=1, source_target_pairs={{0,8},{2,10},{4,12},{6,14},{8,0},{10,2},{12,4},{14,6},{1,9},{3,11}... | collective-permute-start | bytes 393224 | tf_op jit(solution)/shard_map/ppermute | solution.py:180
  25.9 1.1 %collective-permute-done.11.refs_4_ = f32[2,128,128]{2,1,0:T(8,128)S(1)} collective-permute-done((f32[2,128,128]{2,1,0:T(8,128)S(1)}, f32[2,128,128]{2,1,0:T(8,128)S(1)}, u32[]{:S(2)}, u32[]{:S(2)}) %collective-permute-start.11) | collective-permute-done | bytes 131104 | tf_op jit(solution)/shard_map/ppermute | solution.py:180
  27.0 0.1 shard_map.91
  27.2 0.6 %collective-permute-start.12 = (f32[2,128,128]{2,1,0:T(8,128)S(1)}, f32[2,128,128]{2,1,0:T(8,128)S(1)}, u32[]{:S(2)}, u32[]{:S(2)}) collective-permute-start(f32[2,128,128]{2,1,0:T(8,128)S(1)} %get-tuple-element.69), channel_id=1, source_target_pairs={{0,4},{1,3},{2,6},{3,1},{4,0},{5,7},{6,2},{7,5},{8,12},{9,11},{10,... | collective-permute-start | bytes 393224 | tf_op jit(solution)/shard_map/ppermute | solution.py:199
  27.7 1.2 %collective-permute-start.13 = (f32[2,128,128]{2,1,0:T(8,128)S(1)}, f32[2,128,128]{2,1,0:T(8,128)S(1)}, u32[]{:S(2)}, u32[]{:S(2)}) collective-permute-start(f32[2,128,128]{2,1,0:T(8,128)S(1)} %get-tuple-element.70), channel_id=1, source_target_pairs={{0,2},{1,5},{2,0},{3,7},{4,6},{5,1},{6,4},{7,3},{8,10},{9,13},{10,... | collective-permute-start | bytes 393224 | tf_op jit(solution)/shard_map/ppermute | solution.py:199
  29.0 1.8 %collective-permute-start.14 = (f32[2,128,128]{2,1,0:T(8,128)S(1)}, f32[2,128,128]{2,1,0:T(8,128)S(1)}, u32[]{:S(2)}, u32[]{:S(2)}) collective-permute-start(f32[2,128,128]{2,1,0:T(8,128)S(1)} %get-tuple-element.71), channel_id=1, source_target_pairs={{0,6},{1,7},{2,4},{3,5},{4,2},{5,3},{6,0},{7,1},{8,14},{9,15},{10,... | collective-permute-start | bytes 393224 | tf_op jit(solution)/shard_map/ppermute | solution.py:199
  30.7 0.0 collective-permute-done.5.refs_4_
  30.7 0.2 shard_map.90
  30.9 1.2 %collective-permute-start.6 = (f32[2,128,128]{2,1,0:T(8,128)S(1)}, f32[2,128,128]{2,1,0:T(8,128)S(1)}, u32[]{:S(2)}, u32[]{:S(2)}) collective-permute-start(f32[2,128,128]{2,1,0:T(8,128)S(1)} %get-tuple-element.60), channel_id=1, source_target_pairs={{0,4},{1,3},{2,6},{3,1},{4,0},{5,7},{6,2},{7,5},{8,12},{9,11},{10,... | collective-permute-start | bytes 393224 | tf_op jit(solution)/shard_map/ppermute | solution.py:199
  32.1 0.7 %collective-permute-start.7 = (f32[2,128,128]{2,1,0:T(8,128)S(1)}, f32[2,128,128]{2,1,0:T(8,128)S(1)}, u32[]{:S(2)}, u32[]{:S(2)}) collective-permute-start(f32[2,128,128]{2,1,0:T(8,128)S(1)} %get-tuple-element.61), channel_id=1, source_target_pairs={{0,2},{1,5},{2,0},{3,7},{4,6},{5,1},{6,4},{7,3},{8,10},{9,13},{10,... | collective-permute-start | bytes 393224 | tf_op jit(solution)/shard_map/ppermute | solution.py:199
  32.8 0.0 collective-permute-done.12.refs_0_
  32.8 1.7 %collective-permute-start.8 = (f32[2,128,128]{2,1,0:T(8,128)S(1)}, f32[2,128,128]{2,1,0:T(8,128)S(1)}, u32[]{:S(2)}, u32[]{:S(2)}) collective-permute-start(f32[2,128,128]{2,1,0:T(8,128)S(1)} %get-tuple-element.62), channel_id=1, source_target_pairs={{0,6},{1,7},{2,4},{3,5},{4,2},{5,3},{6,0},{7,1},{8,14},{9,15},{10,... | collective-permute-start | bytes 393224 | tf_op jit(solution)/shard_map/ppermute | solution.py:199
  34.5 3.4 %shard_map.89 = (bf16[128,2048]{1,0:T(8,128)(2,1)}, f32[128,1024]{1,0:T(8,128)S(1)}, f32[128,1024]{1,0:T(8,128)S(1)}, f32[128,1024]{1,0:T(8,128)S(1)}, f32[128,1024]{1,0:T(8,128)S(1)}) custom-call(bf16[128,2048]{1,0:T(8,128)(2,1)S(1)} %get-tuple-element.40.q_ref, bf16[128,2048]{1,0:T(8,128)(2,1)S(1)} %get-tuple-element.41.k_ref, ...), custom_call_target="tpu_custom_call" | custom-call | tf_op jit(solution)/shard_map/pallas_call | solution.py:272
  37.9 0.0 collective-permute-done.13.refs_1_
  37.9 0.0 collective-permute-done.14.refs_2_
  37.9 1.1 %shard_map.92 = (bf16[128,2048]{1,0:T(8,128)(2,1)}, bf16[128,2048]{1,0:T(8,128)(2,1)}) custom-call(bf16[128,2048]{1,0:T(8,128)(2,1)S(1)} %get-tuple-element.41.k_ref, bf16[128,2048]{1,0:T(8,128)(2,1)S(1)} %get-tuple-element.42.v_ref, f32[128,1024]{1,0:T(8,128)S(1)} %get-tuple-element.64.key_in, f32[128,1024]{1,0:T(8,128)S(1)} %get-tuple-element.65.value_in, ...), custom_call_target="tpu_custom_call" | custom-call | tf_op jit(solution)/shard_map/pallas_call | solution.py:282
  39.0 0.0 collective-permute-done.6.refs_0_
  39.0 0.0 collective-permute-done.7.refs_1_
  39.0 1.5 %collective-permute-done.8.refs_2_ = f32[2,128,128]{2,1,0:T(8,128)S(1)} collective-permute-done((f32[2,128,128]{2,1,0:T(8,128)S(1)}, f32[2,128,128]{2,1,0:T(8,128)S(1)}, u32[]{:S(2)}, u32[]{:S(2)}) %collective-permute-start.8) | collective-permute-done | bytes 131104 | tf_op jit(solution)/shard_map/ppermute | solution.py:199
  40.5 1.1 %shard_map.93 = (bf16[128,2048]{1,0:T(8,128)(2,1)}, bf16[128,2048]{1,0:T(8,128)(2,1)}) custom-call(bf16[128,2048]{1,0:T(8,128)(2,1)S(1)} %get-tuple-element.41.k_ref, bf16[128,2048]{1,0:T(8,128)(2,1)S(1)} %get-tuple-element.42.v_ref, f32[128,1024]{1,0:T(8,128)S(1)} %get-tuple-element.54.key_in, ...), custom_call_target="tpu_custom_call", output_to_operand_aliasing={{0}: (8, {}), {1}: (9, {})} | custom-call | tf_op jit(solution)/shard_map/pallas_call | solution.py:282
  (2 shorter events, 0.1 us)
Async XLA Ops:
  3.0 1.4 %collective-permute-start = (f32[128,128]{1,0:T(8,128)S(1)}, f32[128,128]{1,0:T(8,128)S(1)}, u32[]{:S(2)}, u32[]{:S(2)}) collective-permute-start(f32[128,128]{1,0:T(8,128)S(1)} %get-tuple-element.45.own_ref), channel_id=1, source_target_pairs={{0,1},{1,0},{2,3},{3,2},{4,5},{5,4},{6,7},{7,6},{8,9},{9,8},{10,11... | collective-permute-start | bytes 196616 | tf_op jit(solution)/shard_map/ppermute | solution.py:180
  4.7 6.9 %collective-permute-start.1 = (f32[2,128,128]{2,1,0:T(8,128)S(1)}, f32[2,128,128]{2,1,0:T(8,128)S(1)}, u32[]{:S(2)}, u32[]{:S(2)}) collective-permute-start(f32[2,128,128]{2,1,0:T(8,128)S(1)} %get-tuple-element.51), channel_id=1, source_target_pairs={{0,4},{2,6},{4,0},{6,2},{8,12},{10,14},{12,8},{14,10},{1,5},{3,7},... | collective-permute-start | bytes 393224 | tf_op jit(solution)/shard_map/ppermute | solution.py:180
  8.1 8.6 %collective-permute-start.9 = (f32[2,128,128]{2,1,0:T(8,128)S(1)}, f32[2,128,128]{2,1,0:T(8,128)S(1)}, u32[]{:S(2)}, u32[]{:S(2)}) collective-permute-start(f32[2,128,128]{2,1,0:T(8,128)S(1)} %get-tuple-element.66), channel_id=1, source_target_pairs={{0,2},{2,0},{4,6},{6,4},{8,10},{10,8},{12,14},{14,12},{1,3},{3,1},... | collective-permute-start | bytes 393224 | tf_op jit(solution)/shard_map/ppermute | solution.py:180
  9.6 7.0 %collective-permute-start.10 = (f32[2,128,128]{2,1,0:T(8,128)S(1)}, f32[2,128,128]{2,1,0:T(8,128)S(1)}, u32[]{:S(2)}, u32[]{:S(2)}) collective-permute-start(f32[2,128,128]{2,1,0:T(8,128)S(1)} %get-tuple-element.67), channel_id=1, source_target_pairs={{0,6},{2,4},{4,2},{6,0},{8,14},{10,12},{12,10},{14,8},{1,7},{3,5},... | collective-permute-start | bytes 393224 | tf_op jit(solution)/shard_map/ppermute | solution.py:180
  12.0 7.9 %collective-permute-start.2 = (f32[2,128,128]{2,1,0:T(8,128)S(1)}, f32[2,128,128]{2,1,0:T(8,128)S(1)}, u32[]{:S(2)}, u32[]{:S(2)}) collective-permute-start(f32[2,128,128]{2,1,0:T(8,128)S(1)} %get-tuple-element.56), channel_id=1, source_target_pairs={{0,4},{2,6},{4,0},{6,2},{8,12},{10,14},{12,8},{14,10},{1,5},{3,7},... | collective-permute-start | bytes 393224 | tf_op jit(solution)/shard_map/ppermute | solution.py:180
  14.5 6.0 %collective-permute-start.3 = (f32[2,128,128]{2,1,0:T(8,128)S(1)}, f32[2,128,128]{2,1,0:T(8,128)S(1)}, u32[]{:S(2)}, u32[]{:S(2)}) collective-permute-start(f32[2,128,128]{2,1,0:T(8,128)S(1)} %get-tuple-element.57), channel_id=1, source_target_pairs={{0,2},{2,0},{4,6},{6,4},{8,10},{10,8},{12,14},{14,12},{1,3},{3,1},... | collective-permute-start | bytes 393224 | tf_op jit(solution)/shard_map/ppermute | solution.py:180
  16.0 6.6 %collective-permute-start.4 = (f32[2,128,128]{2,1,0:T(8,128)S(1)}, f32[2,128,128]{2,1,0:T(8,128)S(1)}, u32[]{:S(2)}, u32[]{:S(2)}) collective-permute-start(f32[2,128,128]{2,1,0:T(8,128)S(1)} %get-tuple-element.58), channel_id=1, source_target_pairs={{0,6},{2,4},{4,2},{6,0},{8,14},{10,12},{12,10},{14,8},{1,7},{3,5},... | collective-permute-start | bytes 393224 | tf_op jit(solution)/shard_map/ppermute | solution.py:180
  16.7 10.4 %collective-permute-start.11 = (f32[2,128,128]{2,1,0:T(8,128)S(1)}, f32[2,128,128]{2,1,0:T(8,128)S(1)}, u32[]{:S(2)}, u32[]{:S(2)}) collective-permute-start(f32[2,128,128]{2,1,0:T(8,128)S(1)} %add_add_fusion), channel_id=1, source_target_pairs={{0,8},{2,10},{4,12},{6,14},{8,0},{10,2},{12,4},{14,6},{1,9},{3,11}... | collective-permute-start | bytes 393224 | tf_op jit(solution)/shard_map/ppermute | solution.py:180
  22.7 8.1 %collective-permute-start.5 = (f32[2,128,128]{2,1,0:T(8,128)S(1)}, f32[2,128,128]{2,1,0:T(8,128)S(1)}, u32[]{:S(2)}, u32[]{:S(2)}) collective-permute-start(f32[2,128,128]{2,1,0:T(8,128)S(1)} %add_add_fusion.1), channel_id=1, source_target_pairs={{0,8},{2,10},{4,12},{6,14},{8,0},{10,2},{12,4},{14,6},{1,9},{3,11}... | collective-permute-start | bytes 393224 | tf_op jit(solution)/shard_map/ppermute | solution.py:180
  27.2 5.6 %collective-permute-start.12 = (f32[2,128,128]{2,1,0:T(8,128)S(1)}, f32[2,128,128]{2,1,0:T(8,128)S(1)}, u32[]{:S(2)}, u32[]{:S(2)}) collective-permute-start(f32[2,128,128]{2,1,0:T(8,128)S(1)} %get-tuple-element.69), channel_id=1, source_target_pairs={{0,4},{1,3},{2,6},{3,1},{4,0},{5,7},{6,2},{7,5},{8,12},{9,11},{10,... | collective-permute-start | bytes 393224 | tf_op jit(solution)/shard_map/ppermute | solution.py:199
  27.7 10.1 %collective-permute-start.13 = (f32[2,128,128]{2,1,0:T(8,128)S(1)}, f32[2,128,128]{2,1,0:T(8,128)S(1)}, u32[]{:S(2)}, u32[]{:S(2)}) collective-permute-start(f32[2,128,128]{2,1,0:T(8,128)S(1)} %get-tuple-element.70), channel_id=1, source_target_pairs={{0,2},{1,5},{2,0},{3,7},{4,6},{5,1},{6,4},{7,3},{8,10},{9,13},{10,... | collective-permute-start | bytes 393224 | tf_op jit(solution)/shard_map/ppermute | solution.py:199
  29.0 8.9 %collective-permute-start.14 = (f32[2,128,128]{2,1,0:T(8,128)S(1)}, f32[2,128,128]{2,1,0:T(8,128)S(1)}, u32[]{:S(2)}, u32[]{:S(2)}) collective-permute-start(f32[2,128,128]{2,1,0:T(8,128)S(1)} %get-tuple-element.71), channel_id=1, source_target_pairs={{0,6},{1,7},{2,4},{3,5},{4,2},{5,3},{6,0},{7,1},{8,14},{9,15},{10,... | collective-permute-start | bytes 393224 | tf_op jit(solution)/shard_map/ppermute | solution.py:199
  30.9 8.1 %collective-permute-start.6 = (f32[2,128,128]{2,1,0:T(8,128)S(1)}, f32[2,128,128]{2,1,0:T(8,128)S(1)}, u32[]{:S(2)}, u32[]{:S(2)}) collective-permute-start(f32[2,128,128]{2,1,0:T(8,128)S(1)} %get-tuple-element.60), channel_id=1, source_target_pairs={{0,4},{1,3},{2,6},{3,1},{4,0},{5,7},{6,2},{7,5},{8,12},{9,11},{10,... | collective-permute-start | bytes 393224 | tf_op jit(solution)/shard_map/ppermute | solution.py:199
  32.1 6.9 %collective-permute-start.7 = (f32[2,128,128]{2,1,0:T(8,128)S(1)}, f32[2,128,128]{2,1,0:T(8,128)S(1)}, u32[]{:S(2)}, u32[]{:S(2)}) collective-permute-start(f32[2,128,128]{2,1,0:T(8,128)S(1)} %get-tuple-element.61), channel_id=1, source_target_pairs={{0,2},{1,5},{2,0},{3,7},{4,6},{5,1},{6,4},{7,3},{8,10},{9,13},{10,... | collective-permute-start | bytes 393224 | tf_op jit(solution)/shard_map/ppermute | solution.py:199
  32.8 7.7 %collective-permute-start.8 = (f32[2,128,128]{2,1,0:T(8,128)S(1)}, f32[2,128,128]{2,1,0:T(8,128)S(1)}, u32[]{:S(2)}, u32[]{:S(2)}) collective-permute-start(f32[2,128,128]{2,1,0:T(8,128)S(1)} %get-tuple-element.62), channel_id=1, source_target_pairs={{0,6},{1,7},{2,4},{3,5},{4,2},{5,3},{6,0},{7,1},{8,14},{9,15},{10,... | collective-permute-start | bytes 393224 | tf_op jit(solution)/shard_map/ppermute | solution.py:199

commit v8 on v7

--- a/solution.py
+++ b/solution.py
@@ -14,7 +14,8 @@
 CALLS = (
     (((0, 2),), None),
     (((0, 1), (0, 3), (0, 0)), None),
-    (((1, 2), (1, 1), (1, 3), (1, 0)), (0, 2)),
+    (((1, 2),), (0, 2)),
+    (((1, 1), (1, 3), (1, 0)), (0, 2)),
 )
 VMEM = pl.BlockSpec(memory_space=pltpu.VMEM)
 ANY = pl.BlockSpec(memory_space=pl.ANY)

time: 41.7 us -> 42.1 us (level)
    pallas_call x3 -> x4, Pallas kernels: 1.14 us -> 1.37 us  [per_device(): pl.pallas_call(functools.partial(state_kernel, features, each, parts, pie...]
  transfers between devices with their start and end apart: 15 -> 15, of which waited for: 8 -> 7; matrix products, arithmetic and copies ran while one was open for 0% -> 0% of each run, Pallas kernels for 14% -> 14%
where the time goes in v8:
time: 42.1 us; the launch traced here: 41.9 us
  starting transfers between devices  22.3 us (53%)
  Pallas kernels  9.58 us (23%)
  waiting for transfers between devices  9.25 us (22%)
  between operations  0.72 us (2%)
    ppermute x9, starting transfers between devices, partner(): lax.ppermute(value, axis, [(source, source ^ mask) for source in range(co...  15.2 us
    ppermute x9, waiting for transfers between devices, partner(): lax.ppermute(value, axis, [(source, source ^ mask) for source in range(co...  7.4 us
    ppermute x6, starting transfers between devices, return_swap(): came.append(lax.ppermute(piece, ('ctx', 'tp'), pairs) if step else piece)  7.11 us
    pallas_call x1, Pallas kernels, per_device(): pl.pallas_call(functools.partial(local_kernel, each, parts), out_shape=(h...  3.39 us
    pallas_call x1, Pallas kernels, per_device(): pl.pallas_call(forward_kernel, out_shape=(near((rows, width), jnp.float32...  2.32 us
    pallas_call x2, Pallas kernels, per_device(): pl.pallas_call(functools.partial(final_kernel, each, start, count), out_s...  2.2 us
    ppermute x6, waiting for transfers between devices, return_swap(): came.append(lax.ppermute(piece, ('ctx', 'tp'), pairs) if step else piece)  1.85 us
    pallas_call x4, Pallas kernels, per_device(): pl.pallas_call(functools.partial(state_kernel, features, each, parts, pie...  1.37 us
  transfers between devices with their start and end apart: 15, of which 7 were waited for; matrix products, arithmetic and copies ran while one was open for 0% of the time, Pallas kernels for 14%

profile of v8, /device:TPU:0, one launch (start us, length us, event | category | flops | bytes accessed | tf_op | source)
XLA Modules:
  0.0 41.9 jit_solution(15884675358231423591)
XLA Ops:
  0.6 2.3 %shard_map.85 = (f32[128,2048]{1,0:T(8,128)S(1)}, bf16[128,2048]{1,0:T(8,128)(2,1)S(1)}, f32[128,128]{1,0:T(8,128)S(1)}, bf16[128,2048]{1,0:T(8,128)(2,1)S(1)}, ...) custom-call(bf16[128,2048]{1,0:T(8,128)(2,1)} %q_hbm.1, ...), custom_call_target="tpu_custom_call" | custom-call | tf_op jit(solution)/shard_map/pallas_call | solution.py:216
  3.0 0.5 %collective-permute-start = (f32[128,128]{1,0:T(8,128)S(1)}, f32[128,128]{1,0:T(8,128)S(1)}, u32[]{:S(2)}, u32[]{:S(2)}) collective-permute-start(f32[128,128]{1,0:T(8,128)S(1)} %get-tuple-element.46.own_ref), channel_id=1, source_target_pairs={{0,1},{1,0},{2,3},{3,2},{4,5},{5,4},{6,7},{7,6},{8,9},{9,8},{10,11... | collective-permute-start | bytes 196616 | tf_op jit(solution)/shard_map/ppermute | solution.py:181
  3.5 0.9 %collective-permute-done.other_ref = f32[128,128]{1,0:T(8,128)S(1)} collective-permute-done((f32[128,128]{1,0:T(8,128)S(1)}, f32[128,128]{1,0:T(8,128)S(1)}, u32[]{:S(2)}, u32[]{:S(2)}) %collective-permute-start) | collective-permute-done | bytes 65568 | tf_op jit(solution)/shard_map/ppermute | solution.py:181
  4.4 0.3 shard_map.86
  4.7 3.0 %collective-permute-start.1 = (f32[2,128,128]{2,1,0:T(8,128)S(1)}, f32[2,128,128]{2,1,0:T(8,128)S(1)}, u32[]{:S(2)}, u32[]{:S(2)}) collective-permute-start(f32[2,128,128]{2,1,0:T(8,128)S(1)} %get-tuple-element.52), channel_id=1, source_target_pairs={{0,4},{2,6},{4,0},{6,2},{8,12},{10,14},{12,8},{14,10},{1,5},{3,7},... | collective-permute-start | bytes 393224 | tf_op jit(solution)/shard_map/ppermute | solution.py:181
  7.7 0.4 shard_map.87
  8.1 1.6 %collective-permute-start.9 = (f32[2,128,128]{2,1,0:T(8,128)S(1)}, f32[2,128,128]{2,1,0:T(8,128)S(1)}, u32[]{:S(2)}, u32[]{:S(2)}) collective-permute-start(f32[2,128,128]{2,1,0:T(8,128)S(1)} %get-tuple-element.68), channel_id=1, source_target_pairs={{0,2},{2,0},{4,6},{6,4},{8,10},{10,8},{12,14},{14,12},{1,3},{3,1},... | collective-permute-start | bytes 393224 | tf_op jit(solution)/shard_map/ppermute | solution.py:181
  9.6 0.0 collective-permute-start.10
  9.6 1.9 %collective-permute-done.1.refs_0_ = f32[2,128,128]{2,1,0:T(8,128)S(1)} collective-permute-done((f32[2,128,128]{2,1,0:T(8,128)S(1)}, f32[2,128,128]{2,1,0:T(8,128)S(1)}, u32[]{:S(2)}, u32[]{:S(2)}) %collective-permute-start.1) | collective-permute-done | bytes 131104 | tf_op jit(solution)/shard_map/ppermute | solution.py:181
  11.5 0.3 shard_map.88
  11.8 2.5 %collective-permute-start.2 = (f32[2,128,128]{2,1,0:T(8,128)S(1)}, f32[2,128,128]{2,1,0:T(8,128)S(1)}, u32[]{:S(2)}, u32[]{:S(2)}) collective-permute-start(f32[2,128,128]{2,1,0:T(8,128)S(1)} %get-tuple-element.58), channel_id=1, source_target_pairs={{0,4},{2,6},{4,0},{6,2},{8,12},{10,14},{12,8},{14,10},{1,5},{3,7},... | collective-permute-start | bytes 393224 | tf_op jit(solution)/shard_map/ppermute | solution.py:181
  14.4 0.4 shard_map.89
  14.8 1.6 %collective-permute-start.3 = (f32[2,128,128]{2,1,0:T(8,128)S(1)}, f32[2,128,128]{2,1,0:T(8,128)S(1)}, u32[]{:S(2)}, u32[]{:S(2)}) collective-permute-start(f32[2,128,128]{2,1,0:T(8,128)S(1)} %get-tuple-element.59), channel_id=1, source_target_pairs={{0,2},{2,0},{4,6},{6,4},{8,10},{10,8},{12,14},{14,12},{1,3},{3,1},... | collective-permute-start | bytes 393224 | tf_op jit(solution)/shard_map/ppermute | solution.py:181
  16.3 0.0 collective-permute-start.4
  16.3 0.0 collective-permute-done.9.refs_1_
  16.4 0.0 collective-permute-done.10.refs_2_
  16.4 2.7 %collective-permute-start.11 = (f32[2,128,128]{2,1,0:T(8,128)S(1)}, f32[2,128,128]{2,1,0:T(8,128)S(1)}, u32[]{:S(2)}, u32[]{:S(2)}) collective-permute-start(f32[2,128,128]{2,1,0:T(8,128)S(1)} %add_add_fusion), channel_id=1, source_target_pairs={{0,8},{2,10},{4,12},{6,14},{8,0},{10,2},{12,4},{14,6},{1,9},{3,11}... | collective-permute-start | bytes 393224 | tf_op jit(solution)/shard_map/ppermute | solution.py:181
  19.1 0.0 collective-permute-done.2.refs_0_
  19.1 1.8 %collective-permute-done.3.refs_1_ = f32[2,128,128]{2,1,0:T(8,128)S(1)} collective-permute-done((f32[2,128,128]{2,1,0:T(8,128)S(1)}, f32[2,128,128]{2,1,0:T(8,128)S(1)}, u32[]{:S(2)}, u32[]{:S(2)}) %collective-permute-start.3) | collective-permute-done | bytes 131104 | tf_op jit(solution)/shard_map/ppermute | solution.py:181
  20.9 1.7 %collective-permute-done.4.refs_2_ = f32[2,128,128]{2,1,0:T(8,128)S(1)} collective-permute-done((f32[2,128,128]{2,1,0:T(8,128)S(1)}, f32[2,128,128]{2,1,0:T(8,128)S(1)}, u32[]{:S(2)}, u32[]{:S(2)}) %collective-permute-start.4) | collective-permute-done | bytes 131104 | tf_op jit(solution)/shard_map/ppermute | solution.py:181
  22.7 3.4 %collective-permute-start.5 = (f32[2,128,128]{2,1,0:T(8,128)S(1)}, f32[2,128,128]{2,1,0:T(8,128)S(1)}, u32[]{:S(2)}, u32[]{:S(2)}) collective-permute-start(f32[2,128,128]{2,1,0:T(8,128)S(1)} %add_add_fusion.1), channel_id=1, source_target_pairs={{0,8},{2,10},{4,12},{6,14},{8,0},{10,2},{12,4},{14,6},{1,9},{3,11}... | collective-permute-start | bytes 393224 | tf_op jit(solution)/shard_map/ppermute | solution.py:181
  26.1 0.9 %collective-permute-done.11.refs_4_ = f32[2,128,128]{2,1,0:T(8,128)S(1)} collective-permute-done((f32[2,128,128]{2,1,0:T(8,128)S(1)}, f32[2,128,128]{2,1,0:T(8,128)S(1)}, u32[]{:S(2)}, u32[]{:S(2)}) %collective-permute-start.11) | collective-permute-done | bytes 131104 | tf_op jit(solution)/shard_map/ppermute | solution.py:181
  26.9 0.1 shard_map.92
  27.1 0.8 %collective-permute-start.12 = (f32[2,128,128]{2,1,0:T(8,128)S(1)}, f32[2,128,128]{2,1,0:T(8,128)S(1)}, u32[]{:S(2)}, u32[]{:S(2)}) collective-permute-start(f32[2,128,128]{2,1,0:T(8,128)S(1)} %get-tuple-element.71), channel_id=1, source_target_pairs={{0,4},{1,3},{2,6},{3,1},{4,0},{5,7},{6,2},{7,5},{8,12},{9,11},{10,... | collective-permute-start | bytes 393224 | tf_op jit(solution)/shard_map/ppermute | solution.py:200
  27.9 1.5 %collective-permute-start.13 = (f32[2,128,128]{2,1,0:T(8,128)S(1)}, f32[2,128,128]{2,1,0:T(8,128)S(1)}, u32[]{:S(2)}, u32[]{:S(2)}) collective-permute-start(f32[2,128,128]{2,1,0:T(8,128)S(1)} %get-tuple-element.72), channel_id=1, source_target_pairs={{0,2},{1,5},{2,0},{3,7},{4,6},{5,1},{6,4},{7,3},{8,10},{9,13},{10,... | collective-permute-start | bytes 393224 | tf_op jit(solution)/shard_map/ppermute | solution.py:200
  29.4 1.3 %collective-permute-start.14 = (f32[2,128,128]{2,1,0:T(8,128)S(1)}, f32[2,128,128]{2,1,0:T(8,128)S(1)}, u32[]{:S(2)}, u32[]{:S(2)}) collective-permute-start(f32[2,128,128]{2,1,0:T(8,128)S(1)} %get-tuple-element.73), channel_id=1, source_target_pairs={{0,6},{1,7},{2,4},{3,5},{4,2},{5,3},{6,0},{7,1},{8,14},{9,15},{10,... | collective-permute-start | bytes 393224 | tf_op jit(solution)/shard_map/ppermute | solution.py:200
  30.6 0.1 collective-permute-done.5.refs_4_
  30.8 0.1 shard_map.91
  30.9 0.7 %collective-permute-start.6 = (f32[2,128,128]{2,1,0:T(8,128)S(1)}, f32[2,128,128]{2,1,0:T(8,128)S(1)}, u32[]{:S(2)}, u32[]{:S(2)}) collective-permute-start(f32[2,128,128]{2,1,0:T(8,128)S(1)} %get-tuple-element.62), channel_id=1, source_target_pairs={{0,4},{1,3},{2,6},{3,1},{4,0},{5,7},{6,2},{7,5},{8,12},{9,11},{10,... | collective-permute-start | bytes 393224 | tf_op jit(solution)/shard_map/ppermute | solution.py:200
  31.6 1.5 %collective-permute-start.7 = (f32[2,128,128]{2,1,0:T(8,128)S(1)}, f32[2,128,128]{2,1,0:T(8,128)S(1)}, u32[]{:S(2)}, u32[]{:S(2)}) collective-permute-start(f32[2,128,128]{2,1,0:T(8,128)S(1)} %get-tuple-element.63), channel_id=1, source_target_pairs={{0,2},{1,5},{2,0},{3,7},{4,6},{5,1},{6,4},{7,3},{8,10},{9,13},{10,... | collective-permute-start | bytes 393224 | tf_op jit(solution)/shard_map/ppermute | solution.py:200
  33.1 0.0 collective-permute-done.12.refs_0_
  33.1 1.4 %collective-permute-start.8 = (f32[2,128,128]{2,1,0:T(8,128)S(1)}, f32[2,128,128]{2,1,0:T(8,128)S(1)}, u32[]{:S(2)}, u32[]{:S(2)}) collective-permute-start(f32[2,128,128]{2,1,0:T(8,128)S(1)} %get-tuple-element.64), channel_id=1, source_target_pairs={{0,6},{1,7},{2,4},{3,5},{4,2},{5,3},{6,0},{7,1},{8,14},{9,15},{10,... | collective-permute-start | bytes 393224 | tf_op jit(solution)/shard_map/ppermute | solution.py:200
  34.5 3.4 %shard_map.90 = (bf16[128,2048]{1,0:T(8,128)(2,1)}, f32[128,1024]{1,0:T(8,128)S(1)}, f32[128,1024]{1,0:T(8,128)S(1)}, f32[128,1024]{1,0:T(8,128)S(1)}, f32[128,1024]{1,0:T(8,128)S(1)}) custom-call(bf16[128,2048]{1,0:T(8,128)(2,1)S(1)} %get-tuple-element.41.q_ref, bf16[128,2048]{1,0:T(8,128)(2,1)S(1)} %get-tuple-element.42.k_ref, ...), custom_call_target="tpu_custom_call" | custom-call | tf_op jit(solution)/shard_map/pallas_call | solution.py:273
  37.9 0.0 collective-permute-done.13.refs_1_
  37.9 0.0 collective-permute-done.14.refs_2_
  37.9 1.1 %shard_map.93 = (bf16[128,2048]{1,0:T(8,128)(2,1)}, bf16[128,2048]{1,0:T(8,128)(2,1)}) custom-call(bf16[128,2048]{1,0:T(8,128)(2,1)S(1)} %get-tuple-element.42.k_ref, bf16[128,2048]{1,0:T(8,128)(2,1)S(1)} %get-tuple-element.43.v_ref, f32[128,1024]{1,0:T(8,128)S(1)} %get-tuple-element.66.key_in, f32[128,1024]{1,0:T(8,128)S(1)} %get-tuple-element.67.value_in, ...), custom_call_target="tpu_custom_call" | custom-call | tf_op jit(solution)/shard_map/pallas_call | solution.py:283
  39.0 0.0 collective-permute-done.6.refs_0_
  39.0 0.0 collective-permute-done.7.refs_1_
  39.0 1.8 %collective-permute-done.8.refs_2_ = f32[2,128,128]{2,1,0:T(8,128)S(1)} collective-permute-done((f32[2,128,128]{2,1,0:T(8,128)S(1)}, f32[2,128,128]{2,1,0:T(8,128)S(1)}, u32[]{:S(2)}, u32[]{:S(2)}) %collective-permute-start.8) | collective-permute-done | bytes 131104 | tf_op jit(solution)/shard_map/ppermute | solution.py:200
  40.8 1.1 %shard_map.94 = (bf16[128,2048]{1,0:T(8,128)(2,1)}, bf16[128,2048]{1,0:T(8,128)(2,1)}) custom-call(bf16[128,2048]{1,0:T(8,128)(2,1)S(1)} %get-tuple-element.42.k_ref, bf16[128,2048]{1,0:T(8,128)(2,1)S(1)} %get-tuple-element.43.v_ref, f32[128,1024]{1,0:T(8,128)S(1)} %get-tuple-element.56.key_in, ...), custom_call_target="tpu_custom_call", output_to_operand_aliasing={{0}: (8, {}), {1}: (9, {})} | custom-call | tf_op jit(solution)/shard_map/pallas_call | solution.py:283
  (2 shorter events, 0.1 us)
Async XLA Ops:
  3.0 1.4 %collective-permute-start = (f32[128,128]{1,0:T(8,128)S(1)}, f32[128,128]{1,0:T(8,128)S(1)}, u32[]{:S(2)}, u32[]{:S(2)}) collective-permute-start(f32[128,128]{1,0:T(8,128)S(1)} %get-tuple-element.46.own_ref), channel_id=1, source_target_pairs={{0,1},{1,0},{2,3},{3,2},{4,5},{5,4},{6,7},{7,6},{8,9},{9,8},{10,11... | collective-permute-start | bytes 196616 | tf_op jit(solution)/shard_map/ppermute | solution.py:181
  4.7 6.9 %collective-permute-start.1 = (f32[2,128,128]{2,1,0:T(8,128)S(1)}, f32[2,128,128]{2,1,0:T(8,128)S(1)}, u32[]{:S(2)}, u32[]{:S(2)}) collective-permute-start(f32[2,128,128]{2,1,0:T(8,128)S(1)} %get-tuple-element.52), channel_id=1, source_target_pairs={{0,4},{2,6},{4,0},{6,2},{8,12},{10,14},{12,8},{14,10},{1,5},{3,7},... | collective-permute-start | bytes 393224 | tf_op jit(solution)/shard_map/ppermute | solution.py:181
  8.1 8.3 %collective-permute-start.9 = (f32[2,128,128]{2,1,0:T(8,128)S(1)}, f32[2,128,128]{2,1,0:T(8,128)S(1)}, u32[]{:S(2)}, u32[]{:S(2)}) collective-permute-start(f32[2,128,128]{2,1,0:T(8,128)S(1)} %get-tuple-element.68), channel_id=1, source_target_pairs={{0,2},{2,0},{4,6},{6,4},{8,10},{10,8},{12,14},{14,12},{1,3},{3,1},... | collective-permute-start | bytes 393224 | tf_op jit(solution)/shard_map/ppermute | solution.py:181
  9.6 6.8 %collective-permute-start.10 = (f32[2,128,128]{2,1,0:T(8,128)S(1)}, f32[2,128,128]{2,1,0:T(8,128)S(1)}, u32[]{:S(2)}, u32[]{:S(2)}) collective-permute-start(f32[2,128,128]{2,1,0:T(8,128)S(1)} %get-tuple-element.69), channel_id=1, source_target_pairs={{0,6},{2,4},{4,2},{6,0},{8,14},{10,12},{12,10},{14,8},{1,7},{3,5},... | collective-permute-start | bytes 393224 | tf_op jit(solution)/shard_map/ppermute | solution.py:181
  11.8 7.2 %collective-permute-start.2 = (f32[2,128,128]{2,1,0:T(8,128)S(1)}, f32[2,128,128]{2,1,0:T(8,128)S(1)}, u32[]{:S(2)}, u32[]{:S(2)}) collective-permute-start(f32[2,128,128]{2,1,0:T(8,128)S(1)} %get-tuple-element.58), channel_id=1, source_target_pairs={{0,4},{2,6},{4,0},{6,2},{8,12},{10,14},{12,8},{14,10},{1,5},{3,7},... | collective-permute-start | bytes 393224 | tf_op jit(solution)/shard_map/ppermute | solution.py:181
  14.8 6.1 %collective-permute-start.3 = (f32[2,128,128]{2,1,0:T(8,128)S(1)}, f32[2,128,128]{2,1,0:T(8,128)S(1)}, u32[]{:S(2)}, u32[]{:S(2)}) collective-permute-start(f32[2,128,128]{2,1,0:T(8,128)S(1)} %get-tuple-element.59), channel_id=1, source_target_pairs={{0,2},{2,0},{4,6},{6,4},{8,10},{10,8},{12,14},{14,12},{1,3},{3,1},... | collective-permute-start | bytes 393224 | tf_op jit(solution)/shard_map/ppermute | solution.py:181
  16.3 6.3 %collective-permute-start.4 = (f32[2,128,128]{2,1,0:T(8,128)S(1)}, f32[2,128,128]{2,1,0:T(8,128)S(1)}, u32[]{:S(2)}, u32[]{:S(2)}) collective-permute-start(f32[2,128,128]{2,1,0:T(8,128)S(1)} %get-tuple-element.60), channel_id=1, source_target_pairs={{0,6},{2,4},{4,2},{6,0},{8,14},{10,12},{12,10},{14,8},{1,7},{3,5},... | collective-permute-start | bytes 393224 | tf_op jit(solution)/shard_map/ppermute | solution.py:181
  16.4 10.5 %collective-permute-start.11 = (f32[2,128,128]{2,1,0:T(8,128)S(1)}, f32[2,128,128]{2,1,0:T(8,128)S(1)}, u32[]{:S(2)}, u32[]{:S(2)}) collective-permute-start(f32[2,128,128]{2,1,0:T(8,128)S(1)} %add_add_fusion), channel_id=1, source_target_pairs={{0,8},{2,10},{4,12},{6,14},{8,0},{10,2},{12,4},{14,6},{1,9},{3,11}... | collective-permute-start | bytes 393224 | tf_op jit(solution)/shard_map/ppermute | solution.py:181
  22.7 8.1 %collective-permute-start.5 = (f32[2,128,128]{2,1,0:T(8,128)S(1)}, f32[2,128,128]{2,1,0:T(8,128)S(1)}, u32[]{:S(2)}, u32[]{:S(2)}) collective-permute-start(f32[2,128,128]{2,1,0:T(8,128)S(1)} %add_add_fusion.1), channel_id=1, source_target_pairs={{0,8},{2,10},{4,12},{6,14},{8,0},{10,2},{12,4},{14,6},{1,9},{3,11}... | collective-permute-start | bytes 393224 | tf_op jit(solution)/shard_map/ppermute | solution.py:181
  27.1 6.0 %collective-permute-start.12 = (f32[2,128,128]{2,1,0:T(8,128)S(1)}, f32[2,128,128]{2,1,0:T(8,128)S(1)}, u32[]{:S(2)}, u32[]{:S(2)}) collective-permute-start(f32[2,128,128]{2,1,0:T(8,128)S(1)} %get-tuple-element.71), channel_id=1, source_target_pairs={{0,4},{1,3},{2,6},{3,1},{4,0},{5,7},{6,2},{7,5},{8,12},{9,11},{10,... | collective-permute-start | bytes 393224 | tf_op jit(solution)/shard_map/ppermute | solution.py:200
  27.9 10.0 %collective-permute-start.13 = (f32[2,128,128]{2,1,0:T(8,128)S(1)}, f32[2,128,128]{2,1,0:T(8,128)S(1)}, u32[]{:S(2)}, u32[]{:S(2)}) collective-permute-start(f32[2,128,128]{2,1,0:T(8,128)S(1)} %get-tuple-element.72), channel_id=1, source_target_pairs={{0,2},{1,5},{2,0},{3,7},{4,6},{5,1},{6,4},{7,3},{8,10},{9,13},{10,... | collective-permute-start | bytes 393224 | tf_op jit(solution)/shard_map/ppermute | solution.py:200
  29.4 8.5 %collective-permute-start.14 = (f32[2,128,128]{2,1,0:T(8,128)S(1)}, f32[2,128,128]{2,1,0:T(8,128)S(1)}, u32[]{:S(2)}, u32[]{:S(2)}) collective-permute-start(f32[2,128,128]{2,1,0:T(8,128)S(1)} %get-tuple-element.73), channel_id=1, source_target_pairs={{0,6},{1,7},{2,4},{3,5},{4,2},{5,3},{6,0},{7,1},{8,14},{9,15},{10,... | collective-permute-start | bytes 393224 | tf_op jit(solution)/shard_map/ppermute | solution.py:200
  30.9 8.1 %collective-permute-start.6 = (f32[2,128,128]{2,1,0:T(8,128)S(1)}, f32[2,128,128]{2,1,0:T(8,128)S(1)}, u32[]{:S(2)}, u32[]{:S(2)}) collective-permute-start(f32[2,128,128]{2,1,0:T(8,128)S(1)} %get-tuple-element.62), channel_id=1, source_target_pairs={{0,4},{1,3},{2,6},{3,1},{4,0},{5,7},{6,2},{7,5},{8,12},{9,11},{10,... | collective-permute-start | bytes 393224 | tf_op jit(solution)/shard_map/ppermute | solution.py:200
  31.6 7.4 %collective-permute-start.7 = (f32[2,128,128]{2,1,0:T(8,128)S(1)}, f32[2,128,128]{2,1,0:T(8,128)S(1)}, u32[]{:S(2)}, u32[]{:S(2)}) collective-permute-start(f32[2,128,128]{2,1,0:T(8,128)S(1)} %get-tuple-element.63), channel_id=1, source_target_pairs={{0,2},{1,5},{2,0},{3,7},{4,6},{5,1},{6,4},{7,3},{8,10},{9,13},{10,... | collective-permute-start | bytes 393224 | tf_op jit(solution)/shard_map/ppermute | solution.py:200
  33.1 7.8 %collective-permute-start.8 = (f32[2,128,128]{2,1,0:T(8,128)S(1)}, f32[2,128,128]{2,1,0:T(8,128)S(1)}, u32[]{:S(2)}, u32[]{:S(2)}) collective-permute-start(f32[2,128,128]{2,1,0:T(8,128)S(1)} %get-tuple-element.64), channel_id=1, source_target_pairs={{0,6},{1,7},{2,4},{3,5},{4,2},{5,3},{6,0},{7,1},{8,14},{9,15},{10,... | collective-permute-start | bytes 393224 | tf_op jit(solution)/shard_map/ppermute | solution.py:200

commit v9 on v7

--- a/solution.py
+++ b/solution.py
@@ -234,16 +234,17 @@
 
     grads, found = [], {}
     for pieces, token in CALLS:
-        tokens = [found[token]] if token else []
         shapes = [near((parts[part][1], HEAD, HEAD), jnp.float32) for part, _ in pieces]
         wide = sum(shape.shape[0] for shape in shapes) * HEAD
         grad, *own = pl.pallas_call(
             functools.partial(state_kernel, features, each, parts, pieces),
             out_shape=(near((rows, wide), jnp.bfloat16), *shapes),
-            in_specs=[VMEM] * 6 + [ANY] * len(tokens),
+            in_specs=[VMEM] * 6,
             out_specs=(VMEM,) * (1 + len(pieces)),
             compiler_params=params(8),
-        )(stat, other, out, y, gain_v, q, *tokens)
+        )(stat, other, out, y, gain_v, q)
+        if token:
+            own, found[token] = lax.optimization_barrier((own, found[token]))
         grads.append(grad)
         for (part, step), piece in zip(pieces, own):
             found[part, step] = partner(piece, "ctx", step) if step else piece

time: 41.7 us -> 42.7 us (1.024)
  starting transfers between devices: 22.1 us -> 23.8 us
  waiting for transfers between devices: 9.3 us -> 8.66 us
    ppermute x6, starting transfers between devices: 7.11 us -> 9.15 us  [return_swap(): came.append(lax.ppermute(piece, ('ctx', 'tp'), pairs) if step else piece)]
    ppermute x9, waiting for transfers between devices: 7.79 us -> 6.74 us  [partner(): lax.ppermute(value, axis, [(source, source ^ mask) for source in range(co...]
  transfers between devices with their start and end apart: 15 -> 15, of which waited for: 8 -> 8; matrix products, arithmetic and copies ran while one was open for 0% -> 0% of each run, Pallas kernels for 14% -> 13%
where the time goes in v9:
time: 42.7 us; the launch traced here: 42.6 us
  starting transfers between devices  23.8 us (56%)
  Pallas kernels  9.36 us (22%)
  waiting for transfers between devices  8.66 us (20%)
  between operations  0.7 us (2%)
    ppermute x9, starting transfers between devices, partner(): lax.ppermute(value, axis, [(source, source ^ mask) for source in range(co...  14.6 us
    ppermute x6, starting transfers between devices, return_swap(): came.append(lax.ppermute(piece, ('ctx', 'tp'), pairs) if step else piece)  9.15 us
    ppermute x9, waiting for transfers between devices, partner(): lax.ppermute(value, axis, [(source, source ^ mask) for source in range(co...  6.74 us
    pallas_call x1, Pallas kernels, per_device(): pl.pallas_call(functools.partial(local_kernel, each, parts), out_shape=(h...  3.39 us
    pallas_call x1, Pallas kernels, per_device(): pl.pallas_call(forward_kernel, out_shape=(near((rows, width), jnp.float32...  2.32 us
    pallas_call x2, Pallas kernels, per_device(): pl.pallas_call(functools.partial(final_kernel, each, start, count), out_s...  2.2 us
    ppermute x6, waiting for transfers between devices, return_swap(): came.append(lax.ppermute(piece, ('ctx', 'tp'), pairs) if step else piece)  1.92 us
    pallas_call x3, Pallas kernels, per_device(): pl.pallas_call(functools.partial(state_kernel, features, each, parts, pie...  1.13 us
  transfers between devices with their start and end apart: 15, of which 8 were waited for; matrix products, arithmetic and copies ran while one was open for 0% of the time, Pallas kernels for 13%

profile of v9, /device:TPU:0, one launch (start us, length us, event | category | flops | bytes accessed | tf_op | source)
XLA Modules:
  0.0 42.6 jit_solution(5184388403406220859)
XLA Ops:
  0.6 2.3 %shard_map.85 = (f32[128,2048]{1,0:T(8,128)S(1)}, bf16[128,2048]{1,0:T(8,128)(2,1)S(1)}, f32[128,128]{1,0:T(8,128)S(1)}, bf16[128,2048]{1,0:T(8,128)(2,1)S(1)}, ...) custom-call(bf16[128,2048]{1,0:T(8,128)(2,1)} %q_hbm.1, ...), custom_call_target="tpu_custom_call" | custom-call | tf_op jit(solution)/shard_map/pallas_call | solution.py:215
  3.0 0.5 %collective-permute-start = (f32[128,128]{1,0:T(8,128)S(1)}, f32[128,128]{1,0:T(8,128)S(1)}, u32[]{:S(2)}, u32[]{:S(2)}) collective-permute-start(f32[128,128]{1,0:T(8,128)S(1)} %get-tuple-element.50.own_ref), channel_id=1, source_target_pairs={{0,1},{1,0},{2,3},{3,2},{4,5},{5,4},{6,7},{7,6},{8,9},{9,8},{10,11... | collective-permute-start | bytes 196616 | tf_op jit(solution)/shard_map/ppermute | solution.py:180
  3.5 0.9 %collective-permute-done.other_ref = f32[128,128]{1,0:T(8,128)S(1)} collective-permute-done((f32[128,128]{1,0:T(8,128)S(1)}, f32[128,128]{1,0:T(8,128)S(1)}, u32[]{:S(2)}, u32[]{:S(2)}) %collective-permute-start) | collective-permute-done | bytes 65568 | tf_op jit(solution)/shard_map/ppermute | solution.py:180
  4.4 0.3 shard_map.86
  4.7 3.0 %collective-permute-start.1 = (f32[2,128,128]{2,1,0:T(8,128)S(1)}, f32[2,128,128]{2,1,0:T(8,128)S(1)}, u32[]{:S(2)}, u32[]{:S(2)}) collective-permute-start(f32[2,128,128]{2,1,0:T(8,128)S(1)} %get-tuple-element.64), channel_id=1, source_target_pairs={{0,4},{2,6},{4,0},{6,2},{8,12},{10,14},{12,8},{14,10},{1,5},{3,7},... | collective-permute-start | bytes 393224 | tf_op jit(solution)/shard_map/ppermute | solution.py:180
  7.7 0.4 shard_map.87
  8.1 1.6 %collective-permute-start.9 = (f32[2,128,128]{2,1,0:T(8,128)S(1)}, f32[2,128,128]{2,1,0:T(8,128)S(1)}, u32[]{:S(2)}, u32[]{:S(2)}) collective-permute-start(f32[2,128,128]{2,1,0:T(8,128)S(1)} %get-tuple-element.76), channel_id=1, source_target_pairs={{0,2},{2,0},{4,6},{6,4},{8,10},{10,8},{12,14},{14,12},{1,3},{3,1},... | collective-permute-start | bytes 393224 | tf_op jit(solution)/shard_map/ppermute | solution.py:180
  9.6 0.0 collective-permute-start.10
  9.6 0.4 %shard_map.88 = (bf16[128,1024]{1,0:T(8,128)(2,1)S(1)}, f32[2,128,128]{2,1,0:T(8,128)S(1)}, f32[2,128,128]{2,1,0:T(8,128)S(1)}, f32[2,128,128]{2,1,0:T(8,128)S(1)}, f32[2,128,128]{2,1,0:T(8,128)S(1)}) custom-call(f32[128,128]{1,0:T(8,128)S(1)} %get-tuple-element.50.own_ref, f32[128,128]{1,0:T(8,128)S(1)} %collective-permute-done.other_ref, ...), custom_call_target="tpu_custom_call" | custom-call | tf_op jit(solution)/shard_map/pallas_call | solution.py:239
  10.1 1.4 %collective-permute-done.1.refs_0_ = f32[2,128,128]{2,1,0:T(8,128)S(1)} collective-permute-done((f32[2,128,128]{2,1,0:T(8,128)S(1)}, f32[2,128,128]{2,1,0:T(8,128)S(1)}, u32[]{:S(2)}, u32[]{:S(2)}) %collective-permute-start.1) | collective-permute-done | bytes 131104 | tf_op jit(solution)/shard_map/ppermute | solution.py:180
  11.5 2.5 %collective-permute-start.2 = (f32[2,128,128]{2,1,0:T(8,128)S(1)}, f32[2,128,128]{2,1,0:T(8,128)S(1)}, u32[]{:S(2)}, u32[]{:S(2)}) collective-permute-start(f32[2,128,128]{2,1,0:T(8,128)S(1)} %get-tuple-element.65), channel_id=1, source_target_pairs={{0,4},{2,6},{4,0},{6,2},{8,12},{10,14},{12,8},{14,10},{1,5},{3,7},... | collective-permute-start | bytes 393224 | tf_op jit(solution)/shard_map/ppermute | solution.py:180
  14.0 1.5 %collective-permute-start.3 = (f32[2,128,128]{2,1,0:T(8,128)S(1)}, f32[2,128,128]{2,1,0:T(8,128)S(1)}, u32[]{:S(2)}, u32[]{:S(2)}) collective-permute-start(f32[2,128,128]{2,1,0:T(8,128)S(1)} %get-tuple-element.66), channel_id=1, source_target_pairs={{0,2},{2,0},{4,6},{6,4},{8,10},{10,8},{12,14},{14,12},{1,3},{3,1},... | collective-permute-start | bytes 393224 | tf_op jit(solution)/shard_map/ppermute | solution.py:180
  15.5 0.0 collective-permute-start.4
  15.5 1.1 %collective-permute-done.9.refs_1_ = f32[2,128,128]{2,1,0:T(8,128)S(1)} collective-permute-done((f32[2,128,128]{2,1,0:T(8,128)S(1)}, f32[2,128,128]{2,1,0:T(8,128)S(1)}, u32[]{:S(2)}, u32[]{:S(2)}) %collective-permute-start.9) | collective-permute-done | bytes 131104 | tf_op jit(solution)/shard_map/ppermute | solution.py:180
  16.6 0.0 collective-permute-done.10.refs_2_
  16.7 2.7 %collective-permute-start.11 = (f32[2,128,128]{2,1,0:T(8,128)S(1)}, f32[2,128,128]{2,1,0:T(8,128)S(1)}, u32[]{:S(2)}, u32[]{:S(2)}) collective-permute-start(f32[2,128,128]{2,1,0:T(8,128)S(1)} %add_add_fusion), channel_id=1, source_target_pairs={{0,8},{2,10},{4,12},{6,14},{8,0},{10,2},{12,4},{14,6},{1,9},{3,11}... | collective-permute-start | bytes 393224 | tf_op jit(solution)/shard_map/ppermute | solution.py:180
  19.3 0.5 %collective-permute-done.2.refs_0_ = f32[2,128,128]{2,1,0:T(8,128)S(1)} collective-permute-done((f32[2,128,128]{2,1,0:T(8,128)S(1)}, f32[2,128,128]{2,1,0:T(8,128)S(1)}, u32[]{:S(2)}, u32[]{:S(2)}) %collective-permute-start.2) | collective-permute-done | bytes 131104 | tf_op jit(solution)/shard_map/ppermute | solution.py:180
  19.9 0.2 collective-permute-done.3.refs_1_
  20.1 2.5 %collective-permute-done.4.refs_2_ = f32[2,128,128]{2,1,0:T(8,128)S(1)} collective-permute-done((f32[2,128,128]{2,1,0:T(8,128)S(1)}, f32[2,128,128]{2,1,0:T(8,128)S(1)}, u32[]{:S(2)}, u32[]{:S(2)}) %collective-permute-start.4) | collective-permute-done | bytes 131104 | tf_op jit(solution)/shard_map/ppermute | solution.py:180
  22.6 2.9 %collective-permute-start.5 = (f32[2,128,128]{2,1,0:T(8,128)S(1)}, f32[2,128,128]{2,1,0:T(8,128)S(1)}, u32[]{:S(2)}, u32[]{:S(2)}) collective-permute-start(f32[2,128,128]{2,1,0:T(8,128)S(1)} %add_add_fusion.1), channel_id=1, source_target_pairs={{0,8},{2,10},{4,12},{6,14},{8,0},{10,2},{12,4},{14,6},{1,9},{3,11}... | collective-permute-start | bytes 393224 | tf_op jit(solution)/shard_map/ppermute | solution.py:180
  25.5 0.0 collective-permute-done.11.refs_4_
  25.5 0.1 shard_map.91
  25.7 2.8 %collective-permute-start.12 = (f32[2,128,128]{2,1,0:T(8,128)S(1)}, f32[2,128,128]{2,1,0:T(8,128)S(1)}, u32[]{:S(2)}, u32[]{:S(2)}) collective-permute-start(f32[2,128,128]{2,1,0:T(8,128)S(1)} %get-tuple-element.79), channel_id=1, source_target_pairs={{0,4},{1,3},{2,6},{3,1},{4,0},{5,7},{6,2},{7,5},{8,12},{9,11},{10,... | collective-permute-start | bytes 393224 | tf_op jit(solution)/shard_map/ppermute | solution.py:199
  28.5 1.4 %collective-permute-start.13 = (f32[2,128,128]{2,1,0:T(8,128)S(1)}, f32[2,128,128]{2,1,0:T(8,128)S(1)}, u32[]{:S(2)}, u32[]{:S(2)}) collective-permute-start(f32[2,128,128]{2,1,0:T(8,128)S(1)} %get-tuple-element.80), channel_id=1, source_target_pairs={{0,2},{1,5},{2,0},{3,7},{4,6},{5,1},{6,4},{7,3},{8,10},{9,13},{10,... | collective-permute-start | bytes 393224 | tf_op jit(solution)/shard_map/ppermute | solution.py:199
  29.9 1.4 %collective-permute-start.14 = (f32[2,128,128]{2,1,0:T(8,128)S(1)}, f32[2,128,128]{2,1,0:T(8,128)S(1)}, u32[]{:S(2)}, u32[]{:S(2)}) collective-permute-start(f32[2,128,128]{2,1,0:T(8,128)S(1)} %get-tuple-element.81), channel_id=1, source_target_pairs={{0,6},{1,7},{2,4},{3,5},{4,2},{5,3},{6,0},{7,1},{8,14},{9,15},{10,... | collective-permute-start | bytes 393224 | tf_op jit(solution)/shard_map/ppermute | solution.py:199
  31.3 0.0 collective-permute-done.5.refs_4_
  31.3 0.2 shard_map.90
  31.5 0.9 %collective-permute-start.6 = (f32[2,128,128]{2,1,0:T(8,128)S(1)}, f32[2,128,128]{2,1,0:T(8,128)S(1)}, u32[]{:S(2)}, u32[]{:S(2)}) collective-permute-start(f32[2,128,128]{2,1,0:T(8,128)S(1)} %get-tuple-element.69), channel_id=1, source_target_pairs={{0,4},{1,3},{2,6},{3,1},{4,0},{5,7},{6,2},{7,5},{8,12},{9,11},{10,... | collective-permute-start | bytes 393224 | tf_op jit(solution)/shard_map/ppermute | solution.py:199
  32.3 1.3 %collective-permute-start.7 = (f32[2,128,128]{2,1,0:T(8,128)S(1)}, f32[2,128,128]{2,1,0:T(8,128)S(1)}, u32[]{:S(2)}, u32[]{:S(2)}) collective-permute-start(f32[2,128,128]{2,1,0:T(8,128)S(1)} %get-tuple-element.70), channel_id=1, source_target_pairs={{0,2},{1,5},{2,0},{3,7},{4,6},{5,1},{6,4},{7,3},{8,10},{9,13},{10,... | collective-permute-start | bytes 393224 | tf_op jit(solution)/shard_map/ppermute | solution.py:199
  33.6 0.0 collective-permute-done.12.refs_0_
  33.6 1.4 %collective-permute-start.8 = (f32[2,128,128]{2,1,0:T(8,128)S(1)}, f32[2,128,128]{2,1,0:T(8,128)S(1)}, u32[]{:S(2)}, u32[]{:S(2)}) collective-permute-start(f32[2,128,128]{2,1,0:T(8,128)S(1)} %get-tuple-element.71), channel_id=1, source_target_pairs={{0,6},{1,7},{2,4},{3,5},{4,2},{5,3},{6,0},{7,1},{8,14},{9,15},{10,... | collective-permute-start | bytes 393224 | tf_op jit(solution)/shard_map/ppermute | solution.py:199
  35.0 3.4 %shard_map.89 = (bf16[128,2048]{1,0:T(8,128)(2,1)}, f32[128,1024]{1,0:T(8,128)S(1)}, f32[128,1024]{1,0:T(8,128)S(1)}, f32[128,1024]{1,0:T(8,128)S(1)}, f32[128,1024]{1,0:T(8,128)S(1)}) custom-call(bf16[128,2048]{1,0:T(8,128)(2,1)S(1)} %get-tuple-element.45.q_ref, bf16[128,2048]{1,0:T(8,128)(2,1)S(1)} %get-tuple-element.46.k_ref, ...), custom_call_target="tpu_custom_call" | custom-call | tf_op jit(solution)/shard_map/pallas_call | solution.py:273
  38.4 0.0 collective-permute-done.13.refs_1_
  38.4 0.0 collective-permute-done.14.refs_2_
  38.4 1.1 %shard_map.92 = (bf16[128,2048]{1,0:T(8,128)(2,1)}, bf16[128,2048]{1,0:T(8,128)(2,1)}) custom-call(bf16[128,2048]{1,0:T(8,128)(2,1)S(1)} %get-tuple-element.46.k_ref, bf16[128,2048]{1,0:T(8,128)(2,1)S(1)} %get-tuple-element.47.v_ref, f32[128,1024]{1,0:T(8,128)S(1)} %get-tuple-element.73.key_in, f32[128,1024]{1,0:T(8,128)S(1)} %get-tuple-element.74.value_in, ...), custom_call_target="tpu_custom_call" | custom-call | tf_op jit(solution)/shard_map/pallas_call | solution.py:283
  39.5 0.0 collective-permute-done.6.refs_0_
  39.5 1.0 %collective-permute-done.7.refs_1_ = f32[2,128,128]{2,1,0:T(8,128)S(1)} collective-permute-done((f32[2,128,128]{2,1,0:T(8,128)S(1)}, f32[2,128,128]{2,1,0:T(8,128)S(1)}, u32[]{:S(2)}, u32[]{:S(2)}) %collective-permute-start.7) | collective-permute-done | bytes 131104 | tf_op jit(solution)/shard_map/ppermute | solution.py:199
  40.5 0.9 %collective-permute-done.8.refs_2_ = f32[2,128,128]{2,1,0:T(8,128)S(1)} collective-permute-done((f32[2,128,128]{2,1,0:T(8,128)S(1)}, f32[2,128,128]{2,1,0:T(8,128)S(1)}, u32[]{:S(2)}, u32[]{:S(2)}) %collective-permute-start.8) | collective-permute-done | bytes 131104 | tf_op jit(solution)/shard_map/ppermute | solution.py:199
  41.5 1.1 %shard_map.93 = (bf16[128,2048]{1,0:T(8,128)(2,1)}, bf16[128,2048]{1,0:T(8,128)(2,1)}) custom-call(bf16[128,2048]{1,0:T(8,128)(2,1)S(1)} %get-tuple-element.46.k_ref, bf16[128,2048]{1,0:T(8,128)(2,1)S(1)} %get-tuple-element.47.v_ref, f32[128,1024]{1,0:T(8,128)S(1)} %get-tuple-element.58.key_in, ...), custom_call_target="tpu_custom_call", output_to_operand_aliasing={{0}: (8, {}), {1}: (9, {})} | custom-call | tf_op jit(solution)/shard_map/pallas_call | solution.py:283
  (2 shorter events, 0.1 us)
Async XLA Ops:
  3.0 1.4 %collective-permute-start = (f32[128,128]{1,0:T(8,128)S(1)}, f32[128,128]{1,0:T(8,128)S(1)}, u32[]{:S(2)}, u32[]{:S(2)}) collective-permute-start(f32[128,128]{1,0:T(8,128)S(1)} %get-tuple-element.50.own_ref), channel_id=1, source_target_pairs={{0,1},{1,0},{2,3},{3,2},{4,5},{5,4},{6,7},{7,6},{8,9},{9,8},{10,11... | collective-permute-start | bytes 196616 | tf_op jit(solution)/shard_map/ppermute | solution.py:180
  4.7 6.9 %collective-permute-start.1 = (f32[2,128,128]{2,1,0:T(8,128)S(1)}, f32[2,128,128]{2,1,0:T(8,128)S(1)}, u32[]{:S(2)}, u32[]{:S(2)}) collective-permute-start(f32[2,128,128]{2,1,0:T(8,128)S(1)} %get-tuple-element.64), channel_id=1, source_target_pairs={{0,4},{2,6},{4,0},{6,2},{8,12},{10,14},{12,8},{14,10},{1,5},{3,7},... | collective-permute-start | bytes 393224 | tf_op jit(solution)/shard_map/ppermute | solution.py:180
  8.1 8.6 %collective-permute-start.9 = (f32[2,128,128]{2,1,0:T(8,128)S(1)}, f32[2,128,128]{2,1,0:T(8,128)S(1)}, u32[]{:S(2)}, u32[]{:S(2)}) collective-permute-start(f32[2,128,128]{2,1,0:T(8,128)S(1)} %get-tuple-element.76), channel_id=1, source_target_pairs={{0,2},{2,0},{4,6},{6,4},{8,10},{10,8},{12,14},{14,12},{1,3},{3,1},... | collective-permute-start | bytes 393224 | tf_op jit(solution)/shard_map/ppermute | solution.py:180
  9.6 7.0 %collective-permute-start.10 = (f32[2,128,128]{2,1,0:T(8,128)S(1)}, f32[2,128,128]{2,1,0:T(8,128)S(1)}, u32[]{:S(2)}, u32[]{:S(2)}) collective-permute-start(f32[2,128,128]{2,1,0:T(8,128)S(1)} %get-tuple-element.77), channel_id=1, source_target_pairs={{0,6},{2,4},{4,2},{6,0},{8,14},{10,12},{12,10},{14,8},{1,7},{3,5},... | collective-permute-start | bytes 393224 | tf_op jit(solution)/shard_map/ppermute | solution.py:180
  11.5 8.3 %collective-permute-start.2 = (f32[2,128,128]{2,1,0:T(8,128)S(1)}, f32[2,128,128]{2,1,0:T(8,128)S(1)}, u32[]{:S(2)}, u32[]{:S(2)}) collective-permute-start(f32[2,128,128]{2,1,0:T(8,128)S(1)} %get-tuple-element.65), channel_id=1, source_target_pairs={{0,4},{2,6},{4,0},{6,2},{8,12},{10,14},{12,8},{14,10},{1,5},{3,7},... | collective-permute-start | bytes 393224 | tf_op jit(solution)/shard_map/ppermute | solution.py:180
  14.0 6.0 %collective-permute-start.3 = (f32[2,128,128]{2,1,0:T(8,128)S(1)}, f32[2,128,128]{2,1,0:T(8,128)S(1)}, u32[]{:S(2)}, u32[]{:S(2)}) collective-permute-start(f32[2,128,128]{2,1,0:T(8,128)S(1)} %get-tuple-element.66), channel_id=1, source_target_pairs={{0,2},{2,0},{4,6},{6,4},{8,10},{10,8},{12,14},{14,12},{1,3},{3,1},... | collective-permute-start | bytes 393224 | tf_op jit(solution)/shard_map/ppermute | solution.py:180
  15.5 7.1 %collective-permute-start.4 = (f32[2,128,128]{2,1,0:T(8,128)S(1)}, f32[2,128,128]{2,1,0:T(8,128)S(1)}, u32[]{:S(2)}, u32[]{:S(2)}) collective-permute-start(f32[2,128,128]{2,1,0:T(8,128)S(1)} %get-tuple-element.67), channel_id=1, source_target_pairs={{0,6},{2,4},{4,2},{6,0},{8,14},{10,12},{12,10},{14,8},{1,7},{3,5},... | collective-permute-start | bytes 393224 | tf_op jit(solution)/shard_map/ppermute | solution.py:180
  16.7 8.9 %collective-permute-start.11 = (f32[2,128,128]{2,1,0:T(8,128)S(1)}, f32[2,128,128]{2,1,0:T(8,128)S(1)}, u32[]{:S(2)}, u32[]{:S(2)}) collective-permute-start(f32[2,128,128]{2,1,0:T(8,128)S(1)} %add_add_fusion), channel_id=1, source_target_pairs={{0,8},{2,10},{4,12},{6,14},{8,0},{10,2},{12,4},{14,6},{1,9},{3,11}... | collective-permute-start | bytes 393224 | tf_op jit(solution)/shard_map/ppermute | solution.py:180
  22.6 8.7 %collective-permute-start.5 = (f32[2,128,128]{2,1,0:T(8,128)S(1)}, f32[2,128,128]{2,1,0:T(8,128)S(1)}, u32[]{:S(2)}, u32[]{:S(2)}) collective-permute-start(f32[2,128,128]{2,1,0:T(8,128)S(1)} %add_add_fusion.1), channel_id=1, source_target_pairs={{0,8},{2,10},{4,12},{6,14},{8,0},{10,2},{12,4},{14,6},{1,9},{3,11}... | collective-permute-start | bytes 393224 | tf_op jit(solution)/shard_map/ppermute | solution.py:180
  25.7 7.9 %collective-permute-start.12 = (f32[2,128,128]{2,1,0:T(8,128)S(1)}, f32[2,128,128]{2,1,0:T(8,128)S(1)}, u32[]{:S(2)}, u32[]{:S(2)}) collective-permute-start(f32[2,128,128]{2,1,0:T(8,128)S(1)} %get-tuple-element.79), channel_id=1, source_target_pairs={{0,4},{1,3},{2,6},{3,1},{4,0},{5,7},{6,2},{7,5},{8,12},{9,11},{10,... | collective-permute-start | bytes 393224 | tf_op jit(solution)/shard_map/ppermute | solution.py:199
  28.5 9.9 %collective-permute-start.13 = (f32[2,128,128]{2,1,0:T(8,128)S(1)}, f32[2,128,128]{2,1,0:T(8,128)S(1)}, u32[]{:S(2)}, u32[]{:S(2)}) collective-permute-start(f32[2,128,128]{2,1,0:T(8,128)S(1)} %get-tuple-element.80), channel_id=1, source_target_pairs={{0,2},{1,5},{2,0},{3,7},{4,6},{5,1},{6,4},{7,3},{8,10},{9,13},{10,... | collective-permute-start | bytes 393224 | tf_op jit(solution)/shard_map/ppermute | solution.py:199
  29.9 8.5 %collective-permute-start.14 = (f32[2,128,128]{2,1,0:T(8,128)S(1)}, f32[2,128,128]{2,1,0:T(8,128)S(1)}, u32[]{:S(2)}, u32[]{:S(2)}) collective-permute-start(f32[2,128,128]{2,1,0:T(8,128)S(1)} %get-tuple-element.81), channel_id=1, source_target_pairs={{0,6},{1,7},{2,4},{3,5},{4,2},{5,3},{6,0},{7,1},{8,14},{9,15},{10,... | collective-permute-start | bytes 393224 | tf_op jit(solution)/shard_map/ppermute | solution.py:199
  31.5 8.1 %collective-permute-start.6 = (f32[2,128,128]{2,1,0:T(8,128)S(1)}, f32[2,128,128]{2,1,0:T(8,128)S(1)}, u32[]{:S(2)}, u32[]{:S(2)}) collective-permute-start(f32[2,128,128]{2,1,0:T(8,128)S(1)} %get-tuple-element.69), channel_id=1, source_target_pairs={{0,4},{1,3},{2,6},{3,1},{4,0},{5,7},{6,2},{7,5},{8,12},{9,11},{10,... | collective-permute-start | bytes 393224 | tf_op jit(solution)/shard_map/ppermute | solution.py:199
  32.3 8.2 %collective-permute-start.7 = (f32[2,128,128]{2,1,0:T(8,128)S(1)}, f32[2,128,128]{2,1,0:T(8,128)S(1)}, u32[]{:S(2)}, u32[]{:S(2)}) collective-permute-start(f32[2,128,128]{2,1,0:T(8,128)S(1)} %get-tuple-element.70), channel_id=1, source_target_pairs={{0,2},{1,5},{2,0},{3,7},{4,6},{5,1},{6,4},{7,3},{8,10},{9,13},{10,... | collective-permute-start | bytes 393224 | tf_op jit(solution)/shard_map/ppermute | solution.py:199
  33.6 7.8 %collective-permute-start.8 = (f32[2,128,128]{2,1,0:T(8,128)S(1)}, f32[2,128,128]{2,1,0:T(8,128)S(1)}, u32[]{:S(2)}, u32[]{:S(2)}) collective-permute-start(f32[2,128,128]{2,1,0:T(8,128)S(1)} %get-tuple-element.71), channel_id=1, source_target_pairs={{0,6},{1,7},{2,4},{3,5},{4,2},{5,3},{6,0},{7,1},{8,14},{9,15},{10,... | collective-permute-start | bytes 393224 | tf_op jit(solution)/shard_map/ppermute | solution.py:199
